TPU v7x, 256 devices: a whole 4x4x8 slice. The times are simulated.
256 devices in a mesh: inst: 16 (over y, x_lo, core), tp: 16 (over x_hi, z).
Axes of the slice: x: 4 (x_hi: 2, x_lo: 2; x = x_hi * 2 + x_lo), y: 4, z: 8, core: 2. Of those that a mesh axis runs over, the one named last changes fastest.
Arguments:
- source_cache: bfloat16 [16, 16, 2, 512, 1024], P('inst', 'tp'), may hold values from -6 to 6
- resident_cache: bfloat16 [16, 16, 8, 2, 512, 128], P('inst', 'tp'), may hold values from -6 to 6
- new_kv: bfloat16 [16, 24, 2, 1024], P('inst'), may hold values from -6 to 6
- queries: bfloat16 [16, 24, 4096], P('inst', None, 'tp'), may hold values from -103 to 103
- residual: bfloat16 [16, 24, 8192], P('inst'), may hold values from -1.5 to 1.5
- lengths: int32 [16, 24], P('inst'), may hold values from 1 to 512, 6144 in all within a row
- out_weight: bfloat16 [4096, 8192], P('tp'), may hold values from -0.09375 to 0.09375
Outputs:
- mixed: bfloat16 [16, 24, 8192], P('inst')
- adopted_cache: bfloat16 [16, 16, 16, 2, 512, 128], P('inst', 'tp')
All inputs are finite; a program needn't handle non-finite values.
Results may differ from a plain program's by a relative error of at most 0.0052.
Values may be sent and summed in bfloat16 or wider, within the bound.
No kernel may reach another device: no remote copies, remote signals or barrier semaphores. Data moves between devices by JAX's collectives and lax.ppermute only.
A program may use at most 64 MiB of HBM per device.

v0:
```python
import math

import jax
import jax.numpy as jnp
from jax import lax
from jax.sharding import PartitionSpec as P

HD = 128
KVH = 8
QH = 32


def from_behind(value, axis, steps):
    count = lax.axis_size(axis)
    pairs = [(source, (source + steps) % count) for source in range(count)]
    return lax.ppermute(value, axis, pairs)


def attend(query_vector, key_cache, value_cache, incoming_key, value_fresh, seq_lengths):
    softmax_scale = 1.0 / math.sqrt(query_vector.shape[-1])
    scores = (
        jnp.einsum("bkgd,blkd->bkgl", query_vector, key_cache, preferred_element_type=jnp.float32)
        * softmax_scale
    )
    local_score = (
        jnp.einsum("heox,hex->heo", query_vector, incoming_key, preferred_element_type=jnp.float32)
        * softmax_scale
    )
    places = jnp.arange(key_cache.shape[1], dtype=jnp.int32)
    live_mask = (places[None, :] < seq_lengths[:, None])[:, None, None, :]
    scores = jnp.where(live_mask, scores, -1e30)
    top_score = jnp.maximum(jnp.max(scores, axis=-1), local_score)
    weights = jnp.where(live_mask, jnp.exp(scores - top_score[..., None]), 0.0)
    local_weight = jnp.exp(local_score - top_score)
    total = jnp.sum(weights, axis=-1) + local_weight
    probs = (weights / total[..., None]).astype(jnp.bfloat16)
    own_prob = (local_weight / total).astype(jnp.bfloat16)
    blended = jnp.einsum("bkgl,blkd->bkgd", probs, value_cache, preferred_element_type=jnp.float32)
    blended = (
        blended
        + own_prob.astype(jnp.float32)[..., None] * value_fresh.astype(jnp.float32)[:, :, None, :]
    )
    return blended.reshape(blended.shape[0], -1).astype(jnp.bfloat16)


def on_device(source_cache, resident_cache, new_kv, queries, residual, lengths, out_weight):
    tp_count = lax.axis_size("tp")
    inst_count = lax.axis_size("inst")
    tp_rank = lax.axis_index("tp")
    per_dev = queries.shape[-1] // HD
    group = QH // KVH
    kv_dev = max(1, per_dev // group)
    per_kv = per_dev // kv_dev
    req_dev = source_cache.shape[1]
    span = source_cache.shape[3]
    adopt_rows = req_dev * tp_count
    own_lengths = lengths[0]
    parted = source_cache[0].reshape(req_dev, 2, span, KVH, HD)
    parted = jnp.repeat(parted, tp_count // KVH, axis=3)
    spread_now = lax.all_to_all(parted, "tp", split_axis=3, concat_axis=0, tiled=True)
    adopted, handed_len = from_behind(
        (spread_now, own_lengths[:adopt_rows]), "inst", inst_count // 2
    )
    adopted_flat = adopted.reshape(adopt_rows, 2, span, kv_dev * HD)
    adopted = adopted_flat.reshape(adopt_rows, 2, span, kv_dev, HD)
    resident = resident_cache[0, 0].reshape(resident_cache.shape[2], 2, span, kv_dev, HD)
    first_head = tp_rank * per_dev // group
    fresh = lax.dynamic_slice_in_dim(new_kv[0], first_head * HD, kv_dev * HD, axis=2)
    fresh = fresh.reshape(fresh.shape[0], 2, kv_dev, HD)
    query_rows = queries[0].reshape(queries.shape[1], kv_dev, per_kv, HD)
    out_adopt = attend(
        query_rows[:adopt_rows],
        adopted[:, 0],
        adopted[:, 1],
        fresh[:adopt_rows, 0],
        fresh[:adopt_rows, 1],
        handed_len,
    )
    out_res = attend(
        query_rows[adopt_rows:],
        resident[:, 0],
        resident[:, 1],
        fresh[adopt_rows:, 0],
        fresh[adopt_rows:, 1],
        own_lengths[adopt_rows:],
    )
    attn = jnp.concatenate([out_adopt, out_res], axis=0)
    value_portion = jnp.dot(attn, out_weight, preferred_element_type=jnp.float32)
    summed = lax.psum(value_portion, "tp")
    mixed = (residual[0].astype(jnp.float32) + summed).astype(jnp.bfloat16)
    return (mixed[None], adopted_flat[None, None])


def solution(mesh):
    in_specs = (
        P("inst", "tp", None, None, None),
        P("inst", "tp", None, None, None, None),
        P("inst", None, None, None),
        P("inst", None, "tp"),
        P("inst", None, None),
        P("inst", None),
        P("tp", None),
    )
    out_specs = (P("inst", None, None), P("inst", "tp", None, None, None, None))
    return jax.shard_map(
        on_device, mesh=mesh, in_specs=in_specs, out_specs=out_specs, check_vma=False
    )
```

profile of v0, /device:TPU:8, one launch (start us, length us, event | category | flops | bytes accessed | tf_op | source)
XLA Modules:
  0.0 383.0 jit_solution(8133648202668662293)
XLA Ops:
  7.2 0.0 copy-start
  7.2 0.0 all-reduce.2.cloned.1.call-start
  7.2 2.2 copy.26
  9.4 0.4 copy.16
  9.9 1.2 broadcast_in_dim.59
  11.1 106.7 %all_to_all.18 = bf16[1,2,512,16,128]{4,2,1,0,3:T(8,128)(2,1)S(1)} all-to-all(bf16[1,2,512,16,128]{4,2,1,0,3:T(8,128)(2,1)S(1)} %bitcast.89), channel_id=1, replica_groups=mesh['inst'=16,'tp'=16] {'tp'}, dimensions={3} | all-to-all | bytes 8388608 | tf_op jit(solution)/shard_map/all_to_all | solution.py:60
  117.7 0.0 copy-start.4
  117.7 0.0 slice-start
  117.7 0.0 slice-start.1
  117.7 0.0 copy-start.2
  117.8 2.3 copy.38
  120.1 2.3 collective-permute-start.1
  122.4 0.0 copy-done.4
  122.4 1.2 collective-permute-start
  123.6 0.0 slice-done
  123.6 0.0 slice-done.1
  123.6 0.0 copy-done
  123.7 0.0 copy-done.2
  123.7 0.1 copy.39
  123.8 0.1 slice_bitcast_fusion.20
  123.9 0.1 iota_compare_fusion.1
  124.0 0.1 fusion.23
  124.1 0.0 copy-start.1
  124.1 0.5 fusion.32
  124.6 0.2 fusion.20
  124.8 0.3 fusion.8
  125.1 0.1 fusion.18
  125.2 86.7 %collective-permute-done = s32[16]{0:T(128)S(1)} collective-permute-done((s32[16]{0:T(128)S(1)}, s32[16]{0:T(128)S(1)}, u32[]{:S(2)}, u32[]{:S(2)}) %collective-permute-start) | collective-permute-done | bytes 96 | tf_op jit(solution)/shard_map/ppermute | solution.py:16
  211.9 0.1 iota_compare_fusion
  212.0 0.0 collective-permute-done.1
  212.0 2.3 fusion.33
  214.4 0.2 fusion.17
  214.6 2.0 fusion.6
  216.6 0.0 copy-done.1
  216.7 1.6 fusion.13
  218.2 0.0 all-reduce.2.cloned.1.call-update
  218.3 0.0 copy-start.3
  218.3 4.7 %copy.20 = bf16[1,1,16,2,512,128]{5,4,3,2,1,0:T(8,128)(2,1)} copy(bf16[1,1,16,2,512,128]{5,4,2,3,1,0:T(8,128)(2,1)} %bitcast.24) | data formatting | bytes 8388608
  223.0 151.3 %all-reduce.2.cloned.1.call-done = f32[24,8192]{1,0:T(8,128)} async-done(((f32[24,8192]{1,0:T(8,128)}), f32[24,8192]{1,0:T(8,128)}) %all-reduce.2.cloned.1.call-update) | async-done | bytes 786448 | tf_op jit(solution)/shard_map/psum | solution.py:89
  374.2 0.0 copy-done.3
  374.2 1.9 fusion.10
  (13 shorter events, 0.1 us)
Async XLA Ops:
  7.2 116.5 %copy-start = (bf16[1,24,2,1024]{3,2,1,0:T(2,128)(2,1)S(1)}, bf16[1,24,2,1024]{3,2,1,0:T(2,128)(2,1)}, u32[]{:S(2)}) copy-start(bf16[1,24,2,1024]{3,2,1,0:T(2,128)(2,1)} %param.9) | copy-start | bytes 294916
  7.2 367.1 %all-reduce.2.cloned.1.call-start = ((), (), s32[]{:S(2)}) async-start(), calls=%async_computation.1 | async-start | bytes 1572864 | tf_op jit(solution)/shard_map/psum | solution.py:89
  117.7 4.6 %copy-start.4 = (s32[1,24]{1,0:T(1,128)S(1)}, s32[1,24]{1,0:T(1,128)}, u32[]{:S(2)}) copy-start(s32[1,24]{1,0:T(1,128)} %param.12) | copy-start | bytes 292
  117.7 5.9 %slice-start = ((bf16[1,24,256]{2,1,0:T(8,128)(2,1)}), bf16[1,8,256]{2,1,0:T(8,128)(2,1)S(1)}, s32[]{:S(2)}) async-start(bf16[1,24,256]{2,1,0:T(8,128)(2,1)} %param.10), calls=%async_computation.2 | async-start | bytes 8192 | tf_op jit(solution)/shard_map/slice | solution.py:80
  117.7 5.9 %slice-start.1 = ((bf16[1,24,256]{2,1,0:T(8,128)(2,1)}), bf16[1,16,256]{2,1,0:T(8,128)(2,1)S(1)}, s32[]{:S(2)}) async-start(bf16[1,24,256]{2,1,0:T(8,128)(2,1)} %param.10), calls=%async_computation.3 | async-start | bytes 16384 | tf_op jit(solution)/shard_map/slice | solution.py:72
  117.7 5.9 %copy-start.2 = (bf16[1,1,8,2,512,128]{5,4,3,2,1,0:T(8,128)(2,1)S(1)}, bf16[1,1,8,2,512,128]{5,4,3,2,1,0:T(8,128)(2,1)}, u32[]{:S(2)}) copy-start(bf16[1,1,8,2,512,128]{5,4,3,2,1,0:T(8,128)(2,1)} %param.8) | copy-start | bytes 6291460
  120.1 92.0 %collective-permute-start.1 = (bf16[16,2,512,1,128]{4,2,0,3,1:T(8,128)(2,1)}, bf16[16,2,512,1,128]{4,2,0,3,1:T(8,128)(2,1)}, u32[]{:S(2)}, u32[]{:S(2)}) collective-permute-start(bf16[16,2,512,1,128]{4,2,0,3,1:T(8,128)(2,1)} %bitcast.84), channel_id=1, source_target_pairs={{0,128},{16,144},{32,160},{48,176},{64,192},{80,208},{96,224},{112... | collective-permute-start | bytes 12582920 | tf_op jit(solution)/shard_map/ppermute | solution.py:16
  122.4 89.6 %collective-permute-start = (s32[16]{0:T(128)S(1)}, s32[16]{0:T(128)S(1)}, u32[]{:S(2)}, u32[]{:S(2)}) collective-permute-start(s32[16]{0:T(128)S(1)} %slice_bitcast_fusion.21), channel_id=1, source_target_pairs={{0,128},{16,144},{32,160},{48,176},{64,192},{80,208},{96,224},{112... | collective-permute-start | bytes 200 | tf_op jit(solution)/shard_map/ppermute | solution.py:16
  124.1 92.5 %copy-start.1 = (bf16[256,8192]{1,0:T(8,128)(2,1)S(1)}, bf16[256,8192]{1,0:T(8,128)(2,1)}, u32[]{:S(2)}) copy-start(bf16[256,8192]{1,0:T(8,128)(2,1)} %param.13) | copy-start | bytes 12582916
  218.3 156.0 %copy-start.3 = (bf16[1,24,8192]{2,1,0:T(8,128)(2,1)S(1)}, bf16[1,24,8192]{2,1,0:T(8,128)(2,1)}, u32[]{:S(2)}) copy-start(bf16[1,24,8192]{2,1,0:T(8,128)(2,1)} %param.11) | copy-start | bytes 1179652
Sparse Core Ops, SparseCore 0:
  218.4 155.8 all-reduce.1
where the time goes:
time: 383 us
  waiting for transfers between devices  238 us (62%)
  blocking collectives  107 us (28%)
  between operations  14.2 us (4%)
  local copies, waits for them, and re-layouts  11.1 us (3%)
  matrix products  6.95 us (2%)
    psum x1, waiting for transfers between devices, on_device(): summed = lax.psum(value_portion, 'tp')  151 us
    all_to_all x1, blocking collectives, on_device(): lax.all_to_all(parted, 'tp', split_axis=3, concat_axis=0, tiled=True)  107 us
    ppermute x2, waiting for transfers between devices, from_behind(): return lax.ppermute(value, axis, pairs)  86.7 us
  transfers between devices with their start and end apart: 3, of which 2 were waited for; matrix products, arithmetic and copies ran while one was open for 2% of the time, Pallas kernels for 0%

commit v1 on v0

v1 whole, which is shorter than its diff:
```python
import functools
import math

import jax
import jax.numpy as jnp
import numpy as np
from jax import lax
from jax.experimental import pallas as pl
from jax.experimental.pallas import tpu as pltpu
from jax.sharding import PartitionSpec as P

HD = 128
KVH = 8
QH = 32
GROUP = QH // KVH
NZ = 8
PAD = 8
MIB = 1 << 20
ROUNDS = ((-3, 0), (0, 1), (2, 0), (-1, 1), (-3, 1), (0, 0), (2, 1), (-1, 0))
N_ROUNDS = len(ROUNDS)

ANY = pl.BlockSpec(memory_space=pl.ANY)
VMEM = pl.BlockSpec(memory_space=pltpu.VMEM)
SMEM = pl.BlockSpec(memory_space=pltpu.SMEM)


def round_target(rank, step):
    shift, flip = ROUNDS[step]
    high, low = divmod(rank, NZ)
    sign = 1 if low % 2 == 0 else -1
    return (high + flip) % 2 * NZ + (low + sign * shift) % NZ


def partner(rank):
    return rank ^ 1


def tables(count, rows):
    heads = np.zeros((count, N_ROUNDS), np.int32)
    mine = np.zeros((count, N_ROUNDS), np.int32)
    for rank in range(count):
        for step in range(N_ROUNDS):
            target = round_target(rank, step)
            heads[rank, step] = target // 2
            mine[target, step] = rank
    theirs = mine[[partner(rank) for rank in range(count)]]
    late = np.broadcast_to(np.arange(count, rows, dtype=np.int32), (count, rows - count))
    order = np.concatenate([mine, theirs, late], axis=1)
    place = np.arange(rows)[None, :, None] == order[:, None, :]
    select = np.concatenate([mine, late], axis=1)[:, :, None] == np.arange(rows)[None, None, :]
    return np.concatenate([heads, mine, theirs], axis=1), place, select


def run_copies(copies):
    for copy in copies:
        copy.start()
    for copy in copies:
        copy.wait()


def extract_kernel(index_ref, cache_ref, *rest):
    outs, sem = rest[:N_ROUNDS], rest[N_ROUNDS]
    copies = []
    for step in range(N_ROUNDS):
        columns = pl.ds(pl.multiple_of(index_ref[step] * HD, HD), HD)
        copies.append(pltpu.make_async_copy(cache_ref.at[:, :, columns], outs[step], sem.at[step]))
    run_copies(copies)


def extract(index, cache):
    shape = jax.ShapeDtypeStruct((2, cache.shape[1], HD), cache.dtype)
    return pl.pallas_call(
        extract_kernel,
        out_shape=[shape] * N_ROUNDS,
        in_specs=[SMEM, ANY],
        out_specs=[VMEM] * N_ROUNDS,
        scratch_shapes=[pltpu.SemaphoreType.DMA((N_ROUNDS,))],
        compiler_params=pltpu.CompilerParams(vmem_limit_bytes=16 * MIB),
        name="extract",
    )(index, cache)


def place_kernel(offset, count, has_base, index_ref, *rest):
    blocks = rest[:count]
    out_ref, sem = rest[count + has_base], rest[count + has_base + 1]
    run_copies([
        pltpu.make_async_copy(blocks[i], out_ref.at[index_ref[offset + i]], sem.at[i])
        for i in range(count)
    ])


def place(index, offset, blocks, rows, base=None):
    count = len(blocks)
    has_base = 0 if base is None else 1
    extra = [] if base is None else [base]
    return pl.pallas_call(
        functools.partial(place_kernel, offset, count, has_base),
        out_shape=jax.ShapeDtypeStruct((rows,) + blocks[0].shape, blocks[0].dtype),
        in_specs=[SMEM] + [VMEM] * count + [ANY] * has_base,
        out_specs=ANY,
        scratch_shapes=[pltpu.SemaphoreType.DMA((count,))],
        input_output_aliases={1 + count: 0} if has_base else {},
        compiler_params=pltpu.CompilerParams(vmem_limit_bytes=16 * MIB),
        name="place",
    )(index, *blocks, *extra)


def attend_kernel(first, heads, scale, len_ref, rows_ref, *rest):
    n_out = heads // 2
    blocks, outs = rest[: -5 - n_out], rest[-5 - n_out : -5]
    q_ref, k_ref, v_ref, prob_ref, blend_ref = rest[-5:]
    count = q_ref.shape[0] // PAD

    def block(b, kind):
        return blocks[0][b, kind] if len(blocks) == 1 else blocks[b][kind]

    new = GROUP * HD
    picked = slice(first, first + count)
    for g in range(PAD):
        spread = pl.ds(g, count, stride=PAD)
        lane = min(g, heads - 1) * HD
        q_ref[spread, :] = rows_ref[picked, lane : lane + HD]
        k_ref[spread, :] = rows_ref[picked, new : new + HD]
        v_ref[spread, :] = rows_ref[picked, new + HD : new + 2 * HD]
    for b in range(count):
        rows = slice(b * PAD, (b + 1) * PAD)
        scores = lax.dot_general(
            q_ref[rows, :].astype(jnp.bfloat16),
            block(b, 0),
            (((1,), (1,)), ((), ())),
            preferred_element_type=jnp.float32,
        )
        live = lax.broadcasted_iota(jnp.int32, scores.shape, 1) < len_ref[b]
        prob_ref[rows, :] = jnp.where(live, scores * scale, -1e30)
    scores = prob_ref[...]
    own = jnp.sum(q_ref[...] * k_ref[...], axis=-1, keepdims=True) * scale
    top = jnp.maximum(jnp.max(scores, axis=-1, keepdims=True), own)
    weights = jnp.exp(scores - top)
    own_weight = jnp.exp(own - top)
    total = jnp.sum(weights, axis=-1, keepdims=True) + own_weight
    prob_ref[...] = weights / total
    own_prob = (own_weight / total).astype(jnp.bfloat16).astype(jnp.float32)
    fresh = own_prob * v_ref[...]
    for b in range(count):
        rows = slice(b * PAD, (b + 1) * PAD)
        blended = jnp.dot(
            prob_ref[rows, :].astype(jnp.bfloat16),
            block(b, 1),
            preferred_element_type=jnp.float32,
        )
        blend_ref[rows, :] = blended + fresh[rows, :]
    for g in range(heads):
        outs[g // 2][:, g % 2 * HD : (g % 2 + 1) * HD] = blend_ref[pl.ds(g, count, stride=PAD), :]


def attend(first, heads, lengths, table, blocks):
    span = blocks[0].shape[-2]
    count = lengths.shape[0]
    wide = pltpu.VMEM((count * PAD, HD), jnp.float32)
    return pl.pallas_call(
        functools.partial(attend_kernel, first, heads, 1.0 / math.sqrt(HD)),
        out_shape=[jax.ShapeDtypeStruct((count, 2 * HD), jnp.float32)] * (heads // 2),
        in_specs=[SMEM] + [VMEM] * (1 + len(blocks)),
        out_specs=[VMEM] * (heads // 2),
        scratch_shapes=[wide, wide, wide, pltpu.VMEM((count * PAD, span), jnp.float32), wide],
        compiler_params=pltpu.CompilerParams(vmem_limit_bytes=16 * MIB),
        name="attend",
    )(lengths, table, *blocks)


def project_kernel(place_ref, kept_ref, traded_ref, res_ref, weight_ref, out_ref):
    gathered = jnp.concatenate([kept_ref[...], traded_ref[...], res_ref[...]], axis=0)
    attn = jnp.dot(
        place_ref[...], gathered.astype(jnp.bfloat16), preferred_element_type=jnp.float32
    ).astype(jnp.bfloat16)
    chunk = out_ref.shape[2]
    for c in range(out_ref.shape[0]):
        out_ref[c] = jnp.dot(
            attn, weight_ref[:, c * chunk : (c + 1) * chunk], preferred_element_type=jnp.float32
        ).astype(out_ref.dtype)


def project(order, kept, traded, res, weight, count):
    rows = order.shape[0]
    return pl.pallas_call(
        project_kernel,
        out_shape=jax.ShapeDtypeStruct((count, rows, weight.shape[1] // count), jnp.bfloat16),
        in_specs=[VMEM] * 5,
        out_specs=VMEM,
        compiler_params=pltpu.CompilerParams(vmem_limit_bytes=24 * MIB),
        name="project",
    )(order, kept, traded, res, weight)


def total_kernel(parts_ref, residual_ref, out_ref):
    summed = parts_ref[0].astype(jnp.float32)
    for c in range(1, parts_ref.shape[0]):
        summed = summed + parts_ref[c].astype(jnp.float32)
    mixed = (residual_ref[...].astype(jnp.float32) + summed).astype(out_ref.dtype)
    for c in range(out_ref.shape[0]):
        out_ref[c] = mixed


def total(parts, residual):
    return pl.pallas_call(
        total_kernel,
        out_shape=jax.ShapeDtypeStruct(parts.shape, jnp.bfloat16),
        in_specs=[VMEM] * 2,
        out_specs=VMEM,
        compiler_params=pltpu.CompilerParams(vmem_limit_bytes=16 * MIB),
        name="total",
    )(parts, residual)


def join_kernel(parts_ref, out_ref):
    chunk = parts_ref.shape[2]
    for c in range(parts_ref.shape[0]):
        out_ref[0, :, c * chunk : (c + 1) * chunk] = parts_ref[c]


def join(parts):
    count, rows, chunk = parts.shape
    return pl.pallas_call(
        join_kernel,
        out_shape=jax.ShapeDtypeStruct((1, rows, count * chunk), parts.dtype),
        in_specs=[VMEM],
        out_specs=VMEM,
        compiler_params=pltpu.CompilerParams(vmem_limit_bytes=16 * MIB),
        name="join",
    )(parts)


def hop(value, inst_count, tp_count, target):
    half = inst_count // 2
    pairs = [
        (i * tp_count + t, (i + half) % inst_count * tp_count + target(t))
        for i in range(inst_count)
        for t in range(tp_count)
    ]
    return lax.ppermute(value, ("inst", "tp"), pairs)


def swap(value, tp_count):
    return lax.ppermute(value, "tp", [(t, partner(t)) for t in range(tp_count)])


def on_device(source_cache, resident_cache, new_kv, queries, residual, lengths, out_weight):
    tp_count = lax.axis_size("tp")
    inst_count = lax.axis_size("inst")
    rank = lax.axis_index("tp")
    rows = queries.shape[1]
    adopt = tp_count
    chunk = out_weight.shape[1] // tp_count

    index, order, select = tables(tp_count, rows)
    index = lax.dynamic_index_in_dim(jnp.asarray(index), rank, keepdims=False)
    order = lax.dynamic_index_in_dim(jnp.asarray(order, jnp.bfloat16), rank, keepdims=False)
    select = lax.dynamic_index_in_dim(jnp.asarray(select, jnp.bfloat16), rank, keepdims=False)
    mine = index[N_ROUNDS : 2 * N_ROUNDS]

    handed = hop(lengths[0], inst_count, tp_count, lambda t: t)
    other_q = swap(queries[0], tp_count)
    sent = extract(index, source_cache[0, 0])
    arrived = [
        hop(sent[step], inst_count, tp_count, lambda t, step=step: round_target(t, step))
        for step in range(N_ROUNDS)
    ]
    passed = [swap(block, tp_count) for block in arrived]

    fresh = lax.dynamic_slice_in_dim(new_kv[0], rank // 2 * HD, HD, axis=2)
    table = jnp.concatenate([queries[0], other_q, fresh.reshape(rows, 2 * HD)], axis=1)
    table = jnp.dot(select, table, preferred_element_type=jnp.float32)
    hit = mine[:, None] == jnp.arange(rows, dtype=jnp.int32)[None, :]
    adopt_len = jnp.sum(jnp.where(hit, handed[None, :], 0), axis=1)
    (res,) = attend(N_ROUNDS, 2, lengths[0, adopt:], table, [resident_cache[0, 0]])
    kept, traded = attend(0, GROUP, adopt_len, table, arrived)
    traded = swap(traded, tp_count)

    parts = project(order, kept, traded, res, out_weight, tp_count)
    parts = lax.all_to_all(parts, "tp", 0, 0)
    own_residual = lax.dynamic_slice_in_dim(residual[0], rank * chunk, chunk, axis=1)
    mixed = join(lax.all_to_all(total(parts, own_residual), "tp", 0, 0))

    adopted = place(index, N_ROUNDS, arrived, adopt)
    adopted = place(index, 2 * N_ROUNDS, passed, adopt, adopted)
    return (mixed, adopted[None, None])


def solution(mesh):
    in_specs = (
        P("inst", "tp", None, None, None),
        P("inst", "tp", None, None, None, None),
        P("inst", None, None, None),
        P("inst", None, "tp"),
        P("inst", None, None),
        P("inst", None),
        P("tp", None),
    )
    out_specs = (P("inst", None, None), P("inst", "tp", None, None, None, None))
    return jax.shard_map(
        on_device, mesh=mesh, in_specs=in_specs, out_specs=out_specs, check_vma=False
    )
```

time: 383 us -> 159 us (0.42)
  waiting for transfers between devices: 238 us -> 70.1 us
  blocking collectives: 107 us -> 0 us
  starting transfers between devices: 3.57 us -> 67.3 us
  between operations: 14.2 us -> 0.85 us
  Pallas kernels: 0 us -> 11.6 us
  matrix products: 6.95 us -> 0.87 us
    psum x1 -> x0, waiting for transfers between devices: 151 us -> none  [on_device(): summed = lax.psum(value_portion, 'tp')]
    all_to_all x1 -> x0, blocking collectives: 107 us -> none  [on_device(): lax.all_to_all(parted, 'tp', split_axis=3, concat_axis=0, tiled=True)]
    ppermute x2 -> x19, starting transfers between devices: 3.53 us -> 53.8 us  [the longest x9 40.9 us: hop(): return lax.ppermute(value, ('inst', 'tp'), pairs)]
    ppermute x2 -> x19, waiting for transfers between devices: 86.7 us -> 56.4 us  [the longest x10 43.8 us: swap(): return lax.ppermute(value, 'tp', [(t, partner(t)) for t in range(tp_count)])]
    all_to_all x0 -> x2, waiting for transfers between devices: none -> 13.7 us  [the longest x1 13.7 us: on_device(): parts = lax.all_to_all(parts, 'tp', 0, 0)]
    all_to_all x0 -> x2, starting transfers between devices: none -> 13.5 us  [the longest x1 8.62 us: on_device(): parts = lax.all_to_all(parts, 'tp', 0, 0)]
    pallas_call x0 -> x8, Pallas kernels: none -> 11.6 us  [the longest x2 3.83 us: place(): pl.pallas_call(functools.partial(place_kernel, offset, count, has_base),...]
    dot_general x7 -> x1, matrix products: 6.95 us -> 0.87 us  [on_device(): table = jnp.dot(select, table, preferred_element_type=jnp.float32)]
  transfers between devices with their start and end apart: 3 -> 21, of which waited for: 2 -> 13; matrix products, arithmetic and copies ran while one was open for 2% -> 2% of each run, Pallas kernels for 0% -> 4%
where the time goes in v1:
time: 159 us
  waiting for transfers between devices  70.1 us (44%)
  starting transfers between devices  67.3 us (42%)
  Pallas kernels  11.6 us (7%)
  local copies, waits for them, and re-layouts  8.07 us (5%)
    ppermute x10, waiting for transfers between devices, swap(): return lax.ppermute(value, 'tp', [(t, partner(t)) for t in range(tp_count)])  43.8 us
    ppermute x9, starting transfers between devices, hop(): return lax.ppermute(value, ('inst', 'tp'), pairs)  40.9 us
    all_to_all x1, waiting for transfers between devices, on_device(): parts = lax.all_to_all(parts, 'tp', 0, 0)  13.7 us
    ppermute x10, starting transfers between devices, swap(): return lax.ppermute(value, 'tp', [(t, partner(t)) for t in range(tp_count)])  12.9 us
    ppermute x9, waiting for transfers between devices, hop(): return lax.ppermute(value, ('inst', 'tp'), pairs)  12.6 us
    all_to_all x1, starting transfers between devices, on_device(): parts = lax.all_to_all(parts, 'tp', 0, 0)  8.62 us
    unnamed x35, local copies, waits for them, and re-layouts  5.16 us
    all_to_all x1, starting transfers between devices, on_device(): mixed = join(lax.all_to_all(total(parts, own_residual), 'tp', 0, 0))  4.85 us
  transfers between devices with their start and end apart: 21, of which 13 were waited for; matrix products, arithmetic and copies ran while one was open for 2% of the time, Pallas kernels for 4%

profile of v1, /device:TPU:8, one launch (start us, length us, event | category | flops | bytes accessed | tf_op | source)
XLA Modules:
  0.0 158.9 jit_solution(14519521058367514321)
XLA Ops:
  0.6 2.4 %collective-permute-start = (s32[24]{0:T(128)}, s32[24]{0:T(128)S(1)}, u32[]{:S(2)}, u32[]{:S(2)}) collective-permute-start(s32[24]{0:T(128)} %bitcast.30), channel_id=1, source_target_pairs={{0,128},{1,129},{2,130},{3,131},{4,132},{5,133},{6,134},{7,135},{8... | collective-permute-start | bytes 296 | tf_op jit(solution)/shard_map/ppermute | solution.py:240
  3.0 1.9 %collective-permute-start.1 = (bf16[24,256]{1,0:T(8,128)(2,1)}, bf16[24,256]{1,0:T(8,128)(2,1)}, u32[]{:S(2)}, u32[]{:S(2)}) collective-permute-start(bf16[24,256]{1,0:T(8,128)(2,1)} %bitcast.28), channel_id=1, source_target_pairs={{0,1},{1,0},{2,3},{3,2},{4,5},{5,4},{6,7},{7,6},{8,9},{9,8},{10,11... | collective-permute-start | bytes 36872 | tf_op jit(solution)/shard_map/ppermute | solution.py:244
  4.9 0.7 fusion.10
  5.6 1.6 copy-done.2
  7.2 2.1 %extract.1 = (bf16[2,512,128]{2,1,0:T(8,128)(2,1)}, bf16[2,512,128]{2,1,0:T(8,128)(2,1)}, bf16[2,512,128]{2,1,0:T(8,128)(2,1)}, bf16[2,512,128]{2,1,0:T(8,128)(2...) custom-call(s32[24]{0:T(128)S(1)} %get-tuple-element.22.index_ref, ...), custom_call_target="tpu_custom_call" | custom-call | tf_op jit(solution)/shard_map/extract/pallas_call | solution.py:72
  9.3 0.7 copy-done.12
  10.0 0.7 copy-done.13
  10.7 0.7 copy-done.14
  11.4 0.7 copy-done.15
  12.1 0.7 copy-done.16
  12.8 6.5 %collective-permute-start.2 = (bf16[2,512,128]{2,1,0:T(8,128)(2,1)}, bf16[2,512,128]{2,1,0:T(8,128)(2,1)S(1)}, u32[]{:S(2)}, u32[]{:S(2)}) collective-permute-start(bf16[2,512,128]{2,1,0:T(8,128)(2,1)} %get-tuple-element.12), channel_id=1, source_target_pairs={{0,133},{1,132},{2,135},{3,134},{4,129},{5,128},{6,131},{7,130},{8... | collective-permute-start | bytes 786440 | tf_op jit(solution)/shard_map/ppermute | solution.py:240
  19.3 4.8 %collective-permute-start.3 = (bf16[2,512,128]{2,1,0:T(8,128)(2,1)}, bf16[2,512,128]{2,1,0:T(8,128)(2,1)S(1)}, u32[]{:S(2)}, u32[]{:S(2)}) collective-permute-start(bf16[2,512,128]{2,1,0:T(8,128)(2,1)} %get-tuple-element.13), channel_id=1, source_target_pairs={{0,136},{1,137},{2,138},{3,139},{4,140},{5,141},{6,142},{7,143},{8... | collective-permute-start | bytes 786440 | tf_op jit(solution)/shard_map/ppermute | solution.py:240
  24.1 2.1 %collective-permute-start.4 = (bf16[2,512,128]{2,1,0:T(8,128)(2,1)}, bf16[2,512,128]{2,1,0:T(8,128)(2,1)S(1)}, u32[]{:S(2)}, u32[]{:S(2)}) collective-permute-start(bf16[2,512,128]{2,1,0:T(8,128)(2,1)} %get-tuple-element.14), channel_id=1, source_target_pairs={{0,130},{1,135},{2,132},{3,129},{4,134},{5,131},{6,128},{7,133},{8... | collective-permute-start | bytes 786440 | tf_op jit(solution)/shard_map/ppermute | solution.py:240
  26.2 0.7 slice_bitcast_fusion.len_ref
  27.1 8.9 %collective-permute-start.6 = (bf16[2,512,128]{2,1,0:T(8,128)(2,1)}, bf16[2,512,128]{2,1,0:T(8,128)(2,1)S(1)}, u32[]{:S(2)}, u32[]{:S(2)}) collective-permute-start(bf16[2,512,128]{2,1,0:T(8,128)(2,1)} %copy-done.15), channel_id=1, source_target_pairs={{0,141},{1,140},{2,143},{3,142},{4,137},{5,136},{6,139},{7,138},{8... | collective-permute-start | bytes 786440 | tf_op jit(solution)/shard_map/ppermute | solution.py:240
  36.0 2.3 %collective-permute-start.7 = (bf16[2,512,128]{2,1,0:T(8,128)(2,1)}, bf16[2,512,128]{2,1,0:T(8,128)(2,1)S(1)}, u32[]{:S(2)}, u32[]{:S(2)}) collective-permute-start(bf16[2,512,128]{2,1,0:T(8,128)(2,1)} %copy-done.14), channel_id=1, source_target_pairs={{0,128},{1,129},{2,130},{3,131},{4,132},{5,133},{6,134},{7,135},{8... | collective-permute-start | bytes 786440 | tf_op jit(solution)/shard_map/ppermute | solution.py:240
  38.3 13.9 %collective-permute-start.8 = (bf16[2,512,128]{2,1,0:T(8,128)(2,1)}, bf16[2,512,128]{2,1,0:T(8,128)(2,1)S(1)}, u32[]{:S(2)}, u32[]{:S(2)}) collective-permute-start(bf16[2,512,128]{2,1,0:T(8,128)(2,1)} %copy-done.13), channel_id=1, source_target_pairs={{0,138},{1,143},{2,140},{3,137},{4,142},{5,139},{6,136},{7,141},{8... | collective-permute-start | bytes 786440 | tf_op jit(solution)/shard_map/ppermute | solution.py:240
  52.2 0.7 constant_dynamic-slice_fusion
  53.1 0.9 fusion.rows_ref
  54.1 8.5 %collective-permute-done.6.rest_4_ = bf16[2,512,128]{2,1,0:T(8,128)(2,1)S(1)} collective-permute-done((bf16[2,512,128]{2,1,0:T(8,128)(2,1)}, bf16[2,512,128]{2,1,0:T(8,128)(2,1)S(1)}, u32[]{:S(2)}, u32[]{:S(2)}) %collective-permute-start.6) | collective-permute-done | bytes 262176 | tf_op jit(solution)/shard_map/ppermute | solution.py:240
  62.6 3.7 %collective-permute-done.7.rest_5_ = bf16[2,512,128]{2,1,0:T(8,128)(2,1)S(1)} collective-permute-done((bf16[2,512,128]{2,1,0:T(8,128)(2,1)}, bf16[2,512,128]{2,1,0:T(8,128)(2,1)S(1)}, u32[]{:S(2)}, u32[]{:S(2)}) %collective-permute-start.7) | collective-permute-done | bytes 262176 | tf_op jit(solution)/shard_map/ppermute | solution.py:240
  66.3 0.3 collective-permute-done.9.rest_7_
  66.6 1.2 attend.2
  67.8 1.8 %collective-permute-start.10 = (f32[8,256]{1,0:T(8,128)S(1)}, f32[8,256]{1,0:T(8,128)S(1)}, u32[]{:S(2)}, u32[]{:S(2)}) collective-permute-start(f32[8,256]{1,0:T(8,128)S(1)} %get-tuple-element.21), channel_id=1, source_target_pairs={{0,1},{1,0},{2,3},{3,2},{4,5},{5,4},{6,7},{7,6},{8,9},{9,8},{10,11... | collective-permute-start | bytes 24584 | tf_op jit(solution)/shard_map/ppermute | solution.py:244
  69.6 0.7 dynamic-slice_bitcast_fusion.1.place_ref
  70.3 1.2 attend.3.res_ref
  71.6 1.7 %project.1 = bf16[16,24,512]{2,1,0:T(8,128)(2,1)} custom-call(bf16[24,24]{1,0:T(8,128)(2,1)S(1)} %dynamic-slice_bitcast_fusion.1.place_ref, f32[8,256]{1,0:T(8,128)S(1)} %get-tuple-element.20.kept_ref, f32[8,256]{1,0:T(8,128)S(1)} %collective-permute-done.10.traded_ref, f32[8,256]{1,0:T(8,128)S(1)} %attend.3.res_ref, bf16[256,8192]{1,0:T(8,128)(2,1)S(1)} %copy-done.1), custom_call_target="tpu_custom_call" | custom-call | tf_op jit(solution)/shard_map/project/pallas_call | solution.py:185
  73.3 8.6 %all-to-all-start = ((bf16[16,24,512]{2,1,0:T(8,128)(2,1)}), bf16[16,24,512]{2,1,0:T(8,128)(2,1)S(1)}, u32[]{:S(2)}, u32[]{:S(2)}) async-start(bf16[16,24,512]{2,1,0:T(8,128)(2,1)} %project.1), calls=%async_computation | async-start | bytes 786432 | tf_op jit(solution)/shard_map/all_to_all | solution.py:280
  82.0 13.7 %all-to-all-done.parts_ref = bf16[16,24,512]{2,1,0:T(8,128)(2,1)S(1)} async-done(((bf16[16,24,512]{2,1,0:T(8,128)(2,1)}), bf16[16,24,512]{2,1,0:T(8,128)(2,1)S(1)}, u32[]{:S(2)}, u32[]{:S(2)}) %all-to-all-start) | async-done | bytes 393248 | tf_op jit(solution)/shard_map/all_to_all | solution.py:280
  95.7 0.8 total.1
  96.5 4.8 %all-to-all-start.1 = ((bf16[16,24,512]{2,1,0:T(8,128)(2,1)}), bf16[16,24,512]{2,1,0:T(8,128)(2,1)S(1)}, u32[]{:S(2)}, u32[]{:S(2)}) async-start(bf16[16,24,512]{2,1,0:T(8,128)(2,1)} %total.1), calls=%async_computation.1 | async-start | bytes 786432 | tf_op jit(solution)/shard_map/all_to_all | solution.py:282
  101.3 1.9 %collective-permute-start.11 = (bf16[2,512,128]{2,1,0:T(8,128)(2,1)S(1)}, bf16[2,512,128]{2,1,0:T(8,128)(2,1)S(1)}, u32[]{:S(2)}, u32[]{:S(2)}) collective-permute-start(bf16[2,512,128]{2,1,0:T(8,128)(2,1)S(1)} %collective-permute-done.2.rest_0_), channel_id=1, source_target_pairs={{0,1},{1,0},{2,3},{3,2},{4,5},{5,4},{6,7},{7,6},{8,9},{9,8},{10,11... | collective-permute-start | bytes 786440 | tf_op jit(solution)/shard_map/ppermute | solution.py:244
  103.5 1.8 %collective-permute-start.13 = (bf16[2,512,128]{2,1,0:T(8,128)(2,1)S(1)}, bf16[2,512,128]{2,1,0:T(8,128)(2,1)S(1)}, u32[]{:S(2)}, u32[]{:S(2)}) collective-permute-start(bf16[2,512,128]{2,1,0:T(8,128)(2,1)S(1)} %collective-permute-done.4.rest_2_), channel_id=1, source_target_pairs={{0,1},{1,0},{2,3},{3,2},{4,5},{5,4},{6,7},{7,6},{8,9},{9,8},{10,11... | collective-permute-start | bytes 786440 | tf_op jit(solution)/shard_map/ppermute | solution.py:244
  105.5 1.8 %collective-permute-start.15 = (bf16[2,512,128]{2,1,0:T(8,128)(2,1)S(1)}, bf16[2,512,128]{2,1,0:T(8,128)(2,1)S(1)}, u32[]{:S(2)}, u32[]{:S(2)}) collective-permute-start(bf16[2,512,128]{2,1,0:T(8,128)(2,1)S(1)} %copy-done.5), channel_id=1, source_target_pairs={{0,1},{1,0},{2,3},{3,2},{4,5},{5,4},{6,7},{7,6},{8,9},{9,8},{10,11... | collective-permute-start | bytes 786440 | tf_op jit(solution)/shard_map/ppermute | solution.py:244
  107.3 10.7 %collective-permute-done.11.rest_0_ = bf16[2,512,128]{2,1,0:T(8,128)(2,1)S(1)} collective-permute-done((bf16[2,512,128]{2,1,0:T(8,128)(2,1)S(1)}, bf16[2,512,128]{2,1,0:T(8,128)(2,1)S(1)}, u32[]{:S(2)}, u32[]{:S(2)}) %collective-permute-start.11) | collective-permute-done | bytes 262176 | tf_op jit(solution)/shard_map/ppermute | solution.py:244
  118.1 1.1 collective-permute-start.16
  119.1 4.6 %collective-permute-done.12.rest_1_ = bf16[2,512,128]{2,1,0:T(8,128)(2,1)S(1)} collective-permute-done((bf16[2,512,128]{2,1,0:T(8,128)(2,1)S(1)}, bf16[2,512,128]{2,1,0:T(8,128)(2,1)S(1)}, u32[]{:S(2)}, u32[]{:S(2)}) %collective-permute-start.12) | collective-permute-done | bytes 262176 | tf_op jit(solution)/shard_map/ppermute | solution.py:244
  123.7 1.1 collective-permute-start.17
  124.7 4.6 %collective-permute-done.13.rest_2_ = bf16[2,512,128]{2,1,0:T(8,128)(2,1)S(1)} collective-permute-done((bf16[2,512,128]{2,1,0:T(8,128)(2,1)S(1)}, bf16[2,512,128]{2,1,0:T(8,128)(2,1)S(1)}, u32[]{:S(2)}, u32[]{:S(2)}) %collective-permute-start.13) | collective-permute-done | bytes 262176 | tf_op jit(solution)/shard_map/ppermute | solution.py:244
  129.3 1.1 collective-permute-start.18
  130.4 1.9 %place.2.rest_8_ = bf16[16,2,512,128]{3,2,1,0:T(8,128)(2,1)} custom-call(s32[24]{0:T(128)S(1)} %get-tuple-element.22.index_ref, bf16[2,512,128]{2,1,0:T(8,128)(2,1)S(1)} %collective-permute-done.2.rest_0_, bf16[2,512,128]{2,1,0:T(8,128)(2,1)S(1)} %collective-permute-done.3.rest_1_, bf16[2,512,128]{2,1,0:T(8,128)(2,1)S(1)} %collective-permute-done.4.rest_2_, ...), custom_call_target="tpu_custom_call" | custom-call | tf_op jit(solution)/shard_map/place/pallas_call | solution.py:96
  132.3 2.6 %collective-permute-done.14.rest_3_ = bf16[2,512,128]{2,1,0:T(8,128)(2,1)S(1)} collective-permute-done((bf16[2,512,128]{2,1,0:T(8,128)(2,1)S(1)}, bf16[2,512,128]{2,1,0:T(8,128)(2,1)S(1)}, u32[]{:S(2)}, u32[]{:S(2)}) %collective-permute-start.14) | collective-permute-done | bytes 262176 | tf_op jit(solution)/shard_map/ppermute | solution.py:244
  134.9 5.6 %collective-permute-done.15.rest_4_ = bf16[2,512,128]{2,1,0:T(8,128)(2,1)S(1)} collective-permute-done((bf16[2,512,128]{2,1,0:T(8,128)(2,1)S(1)}, bf16[2,512,128]{2,1,0:T(8,128)(2,1)S(1)}, u32[]{:S(2)}, u32[]{:S(2)}) %collective-permute-start.15) | collective-permute-done | bytes 262176 | tf_op jit(solution)/shard_map/ppermute | solution.py:244
  140.5 5.6 %collective-permute-done.16.rest_5_ = bf16[2,512,128]{2,1,0:T(8,128)(2,1)S(1)} collective-permute-done((bf16[2,512,128]{2,1,0:T(8,128)(2,1)S(1)}, bf16[2,512,128]{2,1,0:T(8,128)(2,1)S(1)}, u32[]{:S(2)}, u32[]{:S(2)}) %collective-permute-start.16) | collective-permute-done | bytes 262176 | tf_op jit(solution)/shard_map/ppermute | solution.py:244
  146.2 5.6 %collective-permute-done.17.rest_6_ = bf16[2,512,128]{2,1,0:T(8,128)(2,1)S(1)} collective-permute-done((bf16[2,512,128]{2,1,0:T(8,128)(2,1)S(1)}, bf16[2,512,128]{2,1,0:T(8,128)(2,1)S(1)}, u32[]{:S(2)}, u32[]{:S(2)}) %collective-permute-start.17) | collective-permute-done | bytes 262176 | tf_op jit(solution)/shard_map/ppermute | solution.py:244
  151.8 4.4 %collective-permute-done.18.rest_7_ = bf16[2,512,128]{2,1,0:T(8,128)(2,1)S(1)} collective-permute-done((bf16[2,512,128]{2,1,0:T(8,128)(2,1)S(1)}, bf16[2,512,128]{2,1,0:T(8,128)(2,1)S(1)}, u32[]{:S(2)}, u32[]{:S(2)}) %collective-permute-start.18) | collective-permute-done | bytes 262176 | tf_op jit(solution)/shard_map/ppermute | solution.py:244
  156.2 1.9 %place.3 = bf16[16,2,512,128]{3,2,1,0:T(8,128)(2,1)} custom-call(s32[24]{0:T(128)S(1)} %get-tuple-element.22.index_ref, bf16[2,512,128]{2,1,0:T(8,128)(2,1)S(1)} %collective-permute-done.11.rest_0_, bf16[2,512,128]{2,1,0:T(8,128)(2,1)S(1)} %collective-permute-done.12.rest_1_, ...), custom_call_target="tpu_custom_call", output_to_operand_aliasing={{}: (9, {})} | custom-call | tf_op jit(solution)/shard_map/place/pallas_call | solution.py:96
  158.1 0.8 join.1
  (45 shorter events, 0.9 us)
Async XLA Ops:
  0.6 81.3 %copy-start = (bf16[1,24,8192]{2,1,0:T(8,128)(2,1)S(1)}, bf16[1,24,8192]{2,1,0:T(8,128)(2,1)}, u32[]{:S(2)}) copy-start(bf16[1,24,8192]{2,1,0:T(8,128)(2,1)} %param.14) | copy-start | bytes 1179652
  0.6 26.4 %collective-permute-start = (s32[24]{0:T(128)}, s32[24]{0:T(128)S(1)}, u32[]{:S(2)}, u32[]{:S(2)}) collective-permute-start(s32[24]{0:T(128)} %bitcast.30), channel_id=1, source_target_pairs={{0,128},{1,129},{2,130},{3,131},{4,132},{5,133},{6,134},{7,135},{8... | collective-permute-start | bytes 296 | tf_op jit(solution)/shard_map/ppermute | solution.py:240
  3.0 24.1 %collective-permute-start.1 = (bf16[24,256]{1,0:T(8,128)(2,1)}, bf16[24,256]{1,0:T(8,128)(2,1)}, u32[]{:S(2)}, u32[]{:S(2)}) collective-permute-start(bf16[24,256]{1,0:T(8,128)(2,1)} %bitcast.28), channel_id=1, source_target_pairs={{0,1},{1,0},{2,3},{3,2},{4,5},{5,4},{6,7},{7,6},{8,9},{9,8},{10,11... | collective-permute-start | bytes 36872 | tf_op jit(solution)/shard_map/ppermute | solution.py:244
  5.6 1.6 %copy-start.2 = (bf16[1,1,2,512,1024]{4,3,2,1,0:T(8,128)(2,1)S(1)}, bf16[1,1,2,512,1024]{4,3,2,1,0:T(8,128)(2,1)}, u32[]{:S(2)}) copy-start(bf16[1,1,2,512,1024]{4,3,2,1,0:T(8,128)(2,1)} %param.10) | copy-start | bytes 6291460
  7.2 63.1 %copy-start.3 = (bf16[1,1,8,2,512,128]{5,4,3,2,1,0:T(8,128)(2,1)S(1)}, bf16[1,1,8,2,512,128]{5,4,3,2,1,0:T(8,128)(2,1)}, u32[]{:S(2)}) copy-start(bf16[1,1,8,2,512,128]{5,4,3,2,1,0:T(8,128)(2,1)} %param.11) | copy-start | bytes 6291460
  9.3 0.7 copy-start.12
  10.0 0.7 copy-start.13
  10.7 0.7 copy-start.14
  11.4 0.7 copy-start.15
  12.1 0.7 copy-start.16
  12.8 23.2 %collective-permute-start.2 = (bf16[2,512,128]{2,1,0:T(8,128)(2,1)}, bf16[2,512,128]{2,1,0:T(8,128)(2,1)S(1)}, u32[]{:S(2)}, u32[]{:S(2)}) collective-permute-start(bf16[2,512,128]{2,1,0:T(8,128)(2,1)} %get-tuple-element.12), channel_id=1, source_target_pairs={{0,133},{1,132},{2,135},{3,134},{4,129},{5,128},{6,131},{7,130},{8... | collective-permute-start | bytes 786440 | tf_op jit(solution)/shard_map/ppermute | solution.py:240
  19.3 19.0 %collective-permute-start.3 = (bf16[2,512,128]{2,1,0:T(8,128)(2,1)}, bf16[2,512,128]{2,1,0:T(8,128)(2,1)S(1)}, u32[]{:S(2)}, u32[]{:S(2)}) collective-permute-start(bf16[2,512,128]{2,1,0:T(8,128)(2,1)} %get-tuple-element.13), channel_id=1, source_target_pairs={{0,136},{1,137},{2,138},{3,139},{4,140},{5,141},{6,142},{7,143},{8... | collective-permute-start | bytes 786440 | tf_op jit(solution)/shard_map/ppermute | solution.py:240
  24.1 28.1 %collective-permute-start.4 = (bf16[2,512,128]{2,1,0:T(8,128)(2,1)}, bf16[2,512,128]{2,1,0:T(8,128)(2,1)S(1)}, u32[]{:S(2)}, u32[]{:S(2)}) collective-permute-start(bf16[2,512,128]{2,1,0:T(8,128)(2,1)} %get-tuple-element.14), channel_id=1, source_target_pairs={{0,130},{1,135},{2,132},{3,129},{4,134},{5,131},{6,128},{7,133},{8... | collective-permute-start | bytes 786440 | tf_op jit(solution)/shard_map/ppermute | solution.py:240
  27.0 44.5 %copy-start.1 = (bf16[256,8192]{1,0:T(8,128)(2,1)S(1)}, bf16[256,8192]{1,0:T(8,128)(2,1)}, u32[]{:S(2)}) copy-start(bf16[256,8192]{1,0:T(8,128)(2,1)} %weight_ref.1) | copy-start | bytes 12582916
  27.0 27.1 %collective-permute-start.5 = (bf16[2,512,128]{2,1,0:T(8,128)(2,1)}, bf16[2,512,128]{2,1,0:T(8,128)(2,1)S(1)}, u32[]{:S(2)}, u32[]{:S(2)}) collective-permute-start(bf16[2,512,128]{2,1,0:T(8,128)(2,1)} %copy-done.16), channel_id=1, source_target_pairs={{0,143},{1,138},{2,137},{3,140},{4,139},{5,142},{6,141},{7,136},{8... | collective-permute-start | bytes 786440 | tf_op jit(solution)/shard_map/ppermute | solution.py:240
  27.1 35.5 %collective-permute-start.6 = (bf16[2,512,128]{2,1,0:T(8,128)(2,1)}, bf16[2,512,128]{2,1,0:T(8,128)(2,1)S(1)}, u32[]{:S(2)}, u32[]{:S(2)}) collective-permute-start(bf16[2,512,128]{2,1,0:T(8,128)(2,1)} %copy-done.15), channel_id=1, source_target_pairs={{0,141},{1,140},{2,143},{3,142},{4,137},{5,136},{6,139},{7,138},{8... | collective-permute-start | bytes 786440 | tf_op jit(solution)/shard_map/ppermute | solution.py:240
  36.0 30.3 %collective-permute-start.7 = (bf16[2,512,128]{2,1,0:T(8,128)(2,1)}, bf16[2,512,128]{2,1,0:T(8,128)(2,1)S(1)}, u32[]{:S(2)}, u32[]{:S(2)}) collective-permute-start(bf16[2,512,128]{2,1,0:T(8,128)(2,1)} %copy-done.14), channel_id=1, source_target_pairs={{0,128},{1,129},{2,130},{3,131},{4,132},{5,133},{6,134},{7,135},{8... | collective-permute-start | bytes 786440 | tf_op jit(solution)/shard_map/ppermute | solution.py:240
  38.3 28.0 %collective-permute-start.8 = (bf16[2,512,128]{2,1,0:T(8,128)(2,1)}, bf16[2,512,128]{2,1,0:T(8,128)(2,1)S(1)}, u32[]{:S(2)}, u32[]{:S(2)}) collective-permute-start(bf16[2,512,128]{2,1,0:T(8,128)(2,1)} %copy-done.13), channel_id=1, source_target_pairs={{0,138},{1,143},{2,140},{3,137},{4,142},{5,139},{6,136},{7,141},{8... | collective-permute-start | bytes 786440 | tf_op jit(solution)/shard_map/ppermute | solution.py:240
  52.2 14.4 %collective-permute-start.9 = (bf16[2,512,128]{2,1,0:T(8,128)(2,1)}, bf16[2,512,128]{2,1,0:T(8,128)(2,1)S(1)}, u32[]{:S(2)}, u32[]{:S(2)}) collective-permute-start(bf16[2,512,128]{2,1,0:T(8,128)(2,1)} %copy-done.12), channel_id=1, source_target_pairs={{0,135},{1,130},{2,129},{3,132},{4,131},{5,134},{6,133},{7,128},{8... | collective-permute-start | bytes 786440 | tf_op jit(solution)/shard_map/ppermute | solution.py:240
  62.6 8.9 %copy-start.4 = (bf16[2,512,128]{2,1,0:T(8,128)(2,1)}, bf16[2,512,128]{2,1,0:T(8,128)(2,1)S(1)}, u32[]{:S(2)}) copy-start(bf16[2,512,128]{2,1,0:T(8,128)(2,1)S(1)} %collective-permute-done.6.rest_4_) | copy-start | bytes 786436
  66.3 5.3 %copy-start.6 = (bf16[2,512,128]{2,1,0:T(8,128)(2,1)}, bf16[2,512,128]{2,1,0:T(8,128)(2,1)S(1)}, u32[]{:S(2)}) copy-start(bf16[2,512,128]{2,1,0:T(8,128)(2,1)S(1)} %collective-permute-done.7.rest_5_) | copy-start | bytes 786436
  66.3 5.3 %copy-start.8 = (bf16[2,512,128]{2,1,0:T(8,128)(2,1)}, bf16[2,512,128]{2,1,0:T(8,128)(2,1)S(1)}, u32[]{:S(2)}) copy-start(bf16[2,512,128]{2,1,0:T(8,128)(2,1)S(1)} %collective-permute-done.8.rest_6_) | copy-start | bytes 786436
  66.6 5.0 %copy-start.10 = (bf16[2,512,128]{2,1,0:T(8,128)(2,1)}, bf16[2,512,128]{2,1,0:T(8,128)(2,1)S(1)}, u32[]{:S(2)}) copy-start(bf16[2,512,128]{2,1,0:T(8,128)(2,1)S(1)} %collective-permute-done.9.rest_7_) | copy-start | bytes 786436
  67.8 3.7 %collective-permute-start.10 = (f32[8,256]{1,0:T(8,128)S(1)}, f32[8,256]{1,0:T(8,128)S(1)}, u32[]{:S(2)}, u32[]{:S(2)}) collective-permute-start(f32[8,256]{1,0:T(8,128)S(1)} %get-tuple-element.21), channel_id=1, source_target_pairs={{0,1},{1,0},{2,3},{3,2},{4,5},{5,4},{6,7},{7,6},{8,9},{9,8},{10,11... | collective-permute-start | bytes 24584 | tf_op jit(solution)/shard_map/ppermute | solution.py:244
  71.6 33.9 %copy-start.5 = (bf16[2,512,128]{2,1,0:T(8,128)(2,1)S(1)}, bf16[2,512,128]{2,1,0:T(8,128)(2,1)}, u32[]{:S(2)}) copy-start(bf16[2,512,128]{2,1,0:T(8,128)(2,1)} %copy-done.4) | copy-start | bytes 786436
  71.6 46.5 %copy-start.7 = (bf16[2,512,128]{2,1,0:T(8,128)(2,1)S(1)}, bf16[2,512,128]{2,1,0:T(8,128)(2,1)}, u32[]{:S(2)}) copy-start(bf16[2,512,128]{2,1,0:T(8,128)(2,1)} %copy-done.6) | copy-start | bytes 786436
  71.6 52.1 %copy-start.9 = (bf16[2,512,128]{2,1,0:T(8,128)(2,1)S(1)}, bf16[2,512,128]{2,1,0:T(8,128)(2,1)}, u32[]{:S(2)}) copy-start(bf16[2,512,128]{2,1,0:T(8,128)(2,1)} %copy-done.8) | copy-start | bytes 786436
  71.6 57.7 %copy-start.11 = (bf16[2,512,128]{2,1,0:T(8,128)(2,1)S(1)}, bf16[2,512,128]{2,1,0:T(8,128)(2,1)}, u32[]{:S(2)}) copy-start(bf16[2,512,128]{2,1,0:T(8,128)(2,1)} %copy-done.10) | copy-start | bytes 786436
  73.3 22.4 %all-to-all-start = ((bf16[16,24,512]{2,1,0:T(8,128)(2,1)}), bf16[16,24,512]{2,1,0:T(8,128)(2,1)S(1)}, u32[]{:S(2)}, u32[]{:S(2)}) async-start(bf16[16,24,512]{2,1,0:T(8,128)(2,1)} %project.1), calls=%async_computation | async-start | bytes 786432 | tf_op jit(solution)/shard_map/all_to_all | solution.py:280
  96.5 61.6 %all-to-all-start.1 = ((bf16[16,24,512]{2,1,0:T(8,128)(2,1)}), bf16[16,24,512]{2,1,0:T(8,128)(2,1)S(1)}, u32[]{:S(2)}, u32[]{:S(2)}) async-start(bf16[16,24,512]{2,1,0:T(8,128)(2,1)} %total.1), calls=%async_computation.1 | async-start | bytes 786432 | tf_op jit(solution)/shard_map/all_to_all | solution.py:282
  101.3 16.7 %collective-permute-start.11 = (bf16[2,512,128]{2,1,0:T(8,128)(2,1)S(1)}, bf16[2,512,128]{2,1,0:T(8,128)(2,1)S(1)}, u32[]{:S(2)}, u32[]{:S(2)}) collective-permute-start(bf16[2,512,128]{2,1,0:T(8,128)(2,1)S(1)} %collective-permute-done.2.rest_0_), channel_id=1, source_target_pairs={{0,1},{1,0},{2,3},{3,2},{4,5},{5,4},{6,7},{7,6},{8,9},{9,8},{10,11... | collective-permute-start | bytes 786440 | tf_op jit(solution)/shard_map/ppermute | solution.py:244
  103.3 20.4 %collective-permute-start.12 = (bf16[2,512,128]{2,1,0:T(8,128)(2,1)S(1)}, bf16[2,512,128]{2,1,0:T(8,128)(2,1)S(1)}, u32[]{:S(2)}, u32[]{:S(2)}) collective-permute-start(bf16[2,512,128]{2,1,0:T(8,128)(2,1)S(1)} %collective-permute-done.3.rest_1_), channel_id=1, source_target_pairs={{0,1},{1,0},{2,3},{3,2},{4,5},{5,4},{6,7},{7,6},{8,9},{9,8},{10,11... | collective-permute-start | bytes 786440 | tf_op jit(solution)/shard_map/ppermute | solution.py:244
  103.5 25.8 %collective-permute-start.13 = (bf16[2,512,128]{2,1,0:T(8,128)(2,1)S(1)}, bf16[2,512,128]{2,1,0:T(8,128)(2,1)S(1)}, u32[]{:S(2)}, u32[]{:S(2)}) collective-permute-start(bf16[2,512,128]{2,1,0:T(8,128)(2,1)S(1)} %collective-permute-done.4.rest_2_), channel_id=1, source_target_pairs={{0,1},{1,0},{2,3},{3,2},{4,5},{5,4},{6,7},{7,6},{8,9},{9,8},{10,11... | collective-permute-start | bytes 786440 | tf_op jit(solution)/shard_map/ppermute | solution.py:244
  105.3 29.6 %collective-permute-start.14 = (bf16[2,512,128]{2,1,0:T(8,128)(2,1)S(1)}, bf16[2,512,128]{2,1,0:T(8,128)(2,1)S(1)}, u32[]{:S(2)}, u32[]{:S(2)}) collective-permute-start(bf16[2,512,128]{2,1,0:T(8,128)(2,1)S(1)} %collective-permute-done.5.rest_3_), channel_id=1, source_target_pairs={{0,1},{1,0},{2,3},{3,2},{4,5},{5,4},{6,7},{7,6},{8,9},{9,8},{10,11... | collective-permute-start | bytes 786440 | tf_op jit(solution)/shard_map/ppermute | solution.py:244
  105.5 35.0 %collective-permute-start.15 = (bf16[2,512,128]{2,1,0:T(8,128)(2,1)S(1)}, bf16[2,512,128]{2,1,0:T(8,128)(2,1)S(1)}, u32[]{:S(2)}, u32[]{:S(2)}) collective-permute-start(bf16[2,512,128]{2,1,0:T(8,128)(2,1)S(1)} %copy-done.5), channel_id=1, source_target_pairs={{0,1},{1,0},{2,3},{3,2},{4,5},{5,4},{6,7},{7,6},{8,9},{9,8},{10,11... | collective-permute-start | bytes 786440 | tf_op jit(solution)/shard_map/ppermute | solution.py:244
  118.1 28.1 %collective-permute-start.16 = (bf16[2,512,128]{2,1,0:T(8,128)(2,1)S(1)}, bf16[2,512,128]{2,1,0:T(8,128)(2,1)S(1)}, u32[]{:S(2)}, u32[]{:S(2)}) collective-permute-start(bf16[2,512,128]{2,1,0:T(8,128)(2,1)S(1)} %copy-done.7), channel_id=1, source_target_pairs={{0,1},{1,0},{2,3},{3,2},{4,5},{5,4},{6,7},{7,6},{8,9},{9,8},{10,11... | collective-permute-start | bytes 786440 | tf_op jit(solution)/shard_map/ppermute | solution.py:244
  123.7 28.1 %collective-permute-start.17 = (bf16[2,512,128]{2,1,0:T(8,128)(2,1)S(1)}, bf16[2,512,128]{2,1,0:T(8,128)(2,1)S(1)}, u32[]{:S(2)}, u32[]{:S(2)}) collective-permute-start(bf16[2,512,128]{2,1,0:T(8,128)(2,1)S(1)} %copy-done.9), channel_id=1, source_target_pairs={{0,1},{1,0},{2,3},{3,2},{4,5},{5,4},{6,7},{7,6},{8,9},{9,8},{10,11... | collective-permute-start | bytes 786440 | tf_op jit(solution)/shard_map/ppermute | solution.py:244
  129.3 26.9 %collective-permute-start.18 = (bf16[2,512,128]{2,1,0:T(8,128)(2,1)S(1)}, bf16[2,512,128]{2,1,0:T(8,128)(2,1)S(1)}, u32[]{:S(2)}, u32[]{:S(2)}) collective-permute-start(bf16[2,512,128]{2,1,0:T(8,128)(2,1)S(1)} %copy-done.11), channel_id=1, source_target_pairs={{0,1},{1,0},{2,3},{3,2},{4,5},{5,4},{6,7},{7,6},{8,9},{9,8},{10,11... | collective-permute-start | bytes 786440 | tf_op jit(solution)/shard_map/ppermute | solution.py:244

commit v2 on v1

v2 whole, which is shorter than its diff:
```python
import functools
import math

import jax
import jax.numpy as jnp
import numpy as np
from jax import lax
from jax.experimental import pallas as pl
from jax.experimental.pallas import tpu as pltpu
from jax.sharding import PartitionSpec as P

HD = 128
KVH = 8
QH = 32
GROUP = QH // KVH
NZ = 8
PAD = 8
MIB = 1 << 20
NEAR = (1, 8, 9)
FAR = (2, 4, 6)
ROUNDS = ((0, 0), (-3, 0), (0, 1), (-3, 1), (2, 0), (-1, 1), (2, 1), (-1, 0))
N_ROUNDS = len(ROUNDS)
EARLY = 3
FIRST = 5
SMALL = 4

ANY = pl.BlockSpec(memory_space=pl.ANY)
VMEM = pl.BlockSpec(memory_space=pltpu.VMEM)
SMEM = pl.BlockSpec(memory_space=pltpu.SMEM)


def round_target(rank, step):
    shift, flip = ROUNDS[step]
    high, low = divmod(rank, NZ)
    sign = 1 if low % 2 == 0 else -1
    return (high + flip) % 2 * NZ + (low + sign * shift) % NZ


def partner(rank):
    return rank ^ 1


def tables(count, rows):
    mine = np.zeros((count, N_ROUNDS), np.int32)
    for rank in range(count):
        for step in range(N_ROUNDS):
            mine[round_target(rank, step), step] = rank
    theirs = mine[[partner(rank) for rank in range(count)]]
    late = np.broadcast_to(np.arange(count, rows, dtype=np.int32), (count, rows - count))
    order = np.concatenate([mine, theirs, late], axis=1)
    place = np.arange(rows)[None, :, None] == order[:, None, :]
    select = np.concatenate([mine, late], axis=1)[:, :, None] == np.arange(rows)[None, None, :]
    return np.concatenate([mine, theirs], axis=1), place, select


def run_copies(copies):
    for copy in copies:
        copy.start()
    for copy in copies:
        copy.wait()


def extract_kernel(meta_ref, cache_ref, *rest):
    outs, (held, in_sem, out_sem) = rest[:N_ROUNDS], rest[N_ROUNDS:]
    rank = meta_ref[0]
    high, low = rank // NZ, rank % NZ
    sign = 1 - 2 * (low % 2)
    loads, stores = [], []
    for step, (shift, flip) in enumerate(ROUNDS):
        target = (high + flip) % 2 * NZ + (low + NZ + sign * shift) % NZ
        columns = pl.ds(pl.multiple_of(target // 2 * HD, HD), HD)
        loads.append(
            pltpu.make_async_copy(cache_ref.at[:, :, columns], held.at[step], in_sem.at[step])
        )
        stores.append(pltpu.make_async_copy(held.at[step], outs[step], out_sem.at[step]))
    for load in loads:
        load.start()
    for load, store in zip(loads, stores):
        load.wait()
        store.start()
    for store in stores:
        store.wait()


def extract(meta, cache):
    block = (2, cache.shape[1], HD)
    return pl.pallas_call(
        extract_kernel,
        out_shape=[jax.ShapeDtypeStruct(block, cache.dtype)] * N_ROUNDS,
        in_specs=[SMEM, ANY],
        out_specs=[ANY] * N_ROUNDS,
        scratch_shapes=[
            pltpu.VMEM((N_ROUNDS,) + block, cache.dtype),
            pltpu.SemaphoreType.DMA((N_ROUNDS,)),
            pltpu.SemaphoreType.DMA((N_ROUNDS,)),
        ],
        compiler_params=pltpu.CompilerParams(vmem_limit_bytes=60 * MIB),
        name="extract",
    )(meta, cache)


def place_kernel(offset, count, has_base, index_ref, *rest):
    blocks = rest[:count]
    out_ref, sem = rest[-3 if has_base == 2 else -2], rest[-1]
    run_copies([
        pltpu.make_async_copy(blocks[i], out_ref.at[index_ref[offset + i]], sem.at[i])
        for i in range(count)
    ])


def place(index, offset, blocks, rows, base=None, ready=None, carry=None):
    count = len(blocks)
    out = [jax.ShapeDtypeStruct((rows,) + blocks[0].shape, blocks[0].dtype)]
    operands, aliases = [], {}
    if base is not None:
        aliases[1 + count] = 0
        operands.append(base)
    if ready is not None:
        operands.append(ready)
    if carry is not None:
        aliases[1 + count + len(operands)] = 1
        operands.append(carry)
        out.append(jax.ShapeDtypeStruct(carry.shape, carry.dtype))
    return pl.pallas_call(
        functools.partial(place_kernel, offset, count, len(out)),
        out_shape=out,
        in_specs=[SMEM] + [VMEM] * count + [ANY] * len(operands),
        out_specs=[ANY] * len(out),
        scratch_shapes=[pltpu.SemaphoreType.DMA((count,))],
        input_output_aliases=aliases,
        compiler_params=pltpu.CompilerParams(vmem_limit_bytes=16 * MIB),
        name="place",
    )(index, *blocks, *operands)


def attend_kernel(first, heads, scale, len_ref, rows_ref, *rest):
    n_out = heads // 2
    blocks, outs = rest[: -5 - n_out], rest[-5 - n_out : -5]
    q_ref, k_ref, v_ref, prob_ref, blend_ref = rest[-5:]
    count = q_ref.shape[0] // PAD

    def block(b, kind):
        return blocks[0][b, kind] if len(blocks) == 1 else blocks[b][kind]

    new = GROUP * HD
    picked = slice(first, first + count)
    for g in range(PAD):
        spread = pl.ds(g, count, stride=PAD)
        lane = min(g, heads - 1) * HD
        q_ref[spread, :] = rows_ref[picked, lane : lane + HD]
        k_ref[spread, :] = rows_ref[picked, new : new + HD]
        v_ref[spread, :] = rows_ref[picked, new + HD : new + 2 * HD]
    for b in range(count):
        rows = slice(b * PAD, (b + 1) * PAD)
        scores = lax.dot_general(
            q_ref[rows, :].astype(jnp.bfloat16),
            block(b, 0),
            (((1,), (1,)), ((), ())),
            preferred_element_type=jnp.float32,
        )
        live = lax.broadcasted_iota(jnp.int32, scores.shape, 1) < len_ref[b]
        prob_ref[rows, :] = jnp.where(live, scores * scale, -1e30)
    scores = prob_ref[...]
    own = jnp.sum(q_ref[...] * k_ref[...], axis=-1, keepdims=True) * scale
    top = jnp.maximum(jnp.max(scores, axis=-1, keepdims=True), own)
    weights = jnp.exp(scores - top)
    own_weight = jnp.exp(own - top)
    total = jnp.sum(weights, axis=-1, keepdims=True) + own_weight
    prob_ref[...] = weights / total
    own_prob = (own_weight / total).astype(jnp.bfloat16).astype(jnp.float32)
    fresh = own_prob * v_ref[...]
    for b in range(count):
        rows = slice(b * PAD, (b + 1) * PAD)
        blended = jnp.dot(
            prob_ref[rows, :].astype(jnp.bfloat16),
            block(b, 1),
            preferred_element_type=jnp.float32,
        )
        blend_ref[rows, :] = blended + fresh[rows, :]
    for g in range(heads):
        outs[g // 2][:, g % 2 * HD : (g % 2 + 1) * HD] = blend_ref[pl.ds(g, count, stride=PAD), :]


def attend(first, heads, lengths, table, blocks):
    span = blocks[0].shape[-2]
    count = lengths.shape[0]
    wide = pltpu.VMEM((count * PAD, HD), jnp.float32)
    return pl.pallas_call(
        functools.partial(attend_kernel, first, heads, 1.0 / math.sqrt(HD)),
        out_shape=[jax.ShapeDtypeStruct((count, 2 * HD), jnp.float32)] * (heads // 2),
        in_specs=[SMEM] + [VMEM] * (1 + len(blocks)),
        out_specs=[VMEM] * (heads // 2),
        scratch_shapes=[wide, wide, wide, pltpu.VMEM((count * PAD, span), jnp.float32), wide],
        compiler_params=pltpu.CompilerParams(vmem_limit_bytes=16 * MIB),
        name="attend",
    )(lengths, table, *blocks)


def owner(rank, far, near):
    return ((rank ^ near) & 9) | (far << 1)


def project_kernel(meta_ref, place_ref, kept_ref, traded_ref, res_ref, weight_ref, *outs):
    gathered = jnp.concatenate([kept_ref[...], traded_ref[...], res_ref[...]], axis=0)
    attn = jnp.dot(
        place_ref[...], gathered.astype(jnp.bfloat16), preferred_element_type=jnp.float32
    ).astype(jnp.bfloat16)
    rank = meta_ref[0]
    for near, out_ref in zip((0,) + NEAR, outs):
        for far in range(4):
            chunk = out_ref.shape[2]
            columns = pl.ds(pl.multiple_of(owner(rank, far, near) * chunk, chunk), chunk)
            out_ref[far] = jnp.dot(
                attn, weight_ref[:, columns], preferred_element_type=jnp.float32
            ).astype(out_ref.dtype)


def project(meta, order, kept, traded, res, weight, count):
    shape = (4, order.shape[0], weight.shape[1] // count)
    return pl.pallas_call(
        project_kernel,
        out_shape=[jax.ShapeDtypeStruct(shape, jnp.bfloat16)] * 4,
        in_specs=[SMEM] + [VMEM] * 5,
        out_specs=[VMEM] * 4,
        compiler_params=pltpu.CompilerParams(vmem_limit_bytes=24 * MIB),
        name="project",
    )(meta, order, kept, traded, res, weight)


def near_kernel(meta_ref, *refs):
    parts, outs = refs[:4], refs[4:]
    mine = meta_ref[0] // 2 % 4
    for step, out_ref in enumerate(outs):
        far = mine ^ step
        summed = parts[0][far].astype(jnp.float32)
        for part in parts[1:]:
            summed = summed + part[far].astype(jnp.float32)
        out_ref[...] = summed


def near_sum(meta, parts):
    return pl.pallas_call(
        near_kernel,
        out_shape=[jax.ShapeDtypeStruct(parts[0].shape[1:], jnp.float32)] * 4,
        in_specs=[SMEM] + [VMEM] * 4,
        out_specs=[VMEM] * 4,
        compiler_params=pltpu.CompilerParams(vmem_limit_bytes=16 * MIB),
        name="near_sum",
    )(meta, *parts)


def far_kernel(*refs):
    parts, residual_ref, out_ref = refs[:4], refs[4], refs[5]
    summed = (parts[0][...] + parts[1][...]) + (parts[2][...] + parts[3][...])
    out_ref[...] = (residual_ref[...].astype(jnp.float32) + summed).astype(out_ref.dtype)


def far_sum(parts, residual):
    return pl.pallas_call(
        far_kernel,
        out_shape=jax.ShapeDtypeStruct(residual.shape, residual.dtype),
        in_specs=[VMEM] * 5,
        out_specs=VMEM,
        compiler_params=pltpu.CompilerParams(vmem_limit_bytes=16 * MIB),
        name="far_sum",
    )(*parts, residual)


def stack_kernel(meta_ref, *refs):
    parts, out_ref = refs[:4], refs[4]
    for step, part in enumerate(parts):
        out_ref[meta_ref[0] // 2 % 4 ^ step] = part[...]


def stack(meta, parts):
    return pl.pallas_call(
        stack_kernel,
        out_shape=jax.ShapeDtypeStruct((4,) + parts[0].shape, parts[0].dtype),
        in_specs=[SMEM] + [VMEM] * 4,
        out_specs=VMEM,
        compiler_params=pltpu.CompilerParams(vmem_limit_bytes=16 * MIB),
        name="stack",
    )(meta, *parts)


def join_kernel(meta_ref, *refs):
    parts, out_ref = refs[:4], refs[4]
    rank = meta_ref[0]
    for near, part in zip((0,) + NEAR, parts):
        chunk = part.shape[2]
        for far in range(4):
            columns = pl.ds(pl.multiple_of(owner(rank, far, near) * chunk, chunk), chunk)
            out_ref[0, :, columns] = part[far]


def join(meta, parts, count):
    _, rows, chunk = parts[0].shape
    return pl.pallas_call(
        join_kernel,
        out_shape=jax.ShapeDtypeStruct((1, rows, count * chunk), parts[0].dtype),
        in_specs=[SMEM] + [VMEM] * 4,
        out_specs=VMEM,
        compiler_params=pltpu.CompilerParams(vmem_limit_bytes=16 * MIB),
        name="join",
    )(meta, *parts)


def hop(value, inst_count, tp_count, target):
    half = inst_count // 2
    pairs = [
        (i * tp_count + t, (i + half) % inst_count * tp_count + target(t))
        for i in range(inst_count)
        for t in range(tp_count)
    ]
    return lax.ppermute(value, ("inst", "tp"), pairs)


def after(value, others):
    return lax.optimization_barrier((value, *others))[0] if others else value


def swap(value, tp_count, bits=1):
    return lax.ppermute(value, "tp", [(t, t ^ bits) for t in range(tp_count)])


def on_device(source_cache, resident_cache, new_kv, queries, residual, lengths, out_weight):
    tp_count = lax.axis_size("tp")
    inst_count = lax.axis_size("inst")
    rank = lax.axis_index("tp")
    rows = queries.shape[1]
    adopt = tp_count
    chunk = out_weight.shape[1] // tp_count
    meta = rank.reshape(1).astype(jnp.int32)

    handed = hop(lengths[0], inst_count, tp_count, lambda t: t)
    other_q = swap(queries[0], tp_count)
    sent = list(extract(after(meta, [handed, other_q]), source_cache[0, 0]))

    def send(step, block):
        return hop(block, inst_count, tp_count, lambda t: round_target(t, step))

    arrived = []
    for step in range(N_ROUNDS):
        arrived.append(send(step, sent[step]))
    passed = [swap(arrived[k], tp_count) for k in range(EARLY)]

    index, order, select = tables(tp_count, rows)
    index = lax.dynamic_index_in_dim(jnp.asarray(index), rank, keepdims=False)
    order = lax.dynamic_index_in_dim(jnp.asarray(order, jnp.bfloat16), rank, keepdims=False)
    select = lax.dynamic_index_in_dim(jnp.asarray(select, jnp.bfloat16), rank, keepdims=False)
    mine = index[:N_ROUNDS]
    fresh = lax.dynamic_slice_in_dim(new_kv[0], rank // 2 * HD, HD, axis=2)
    table = jnp.concatenate([queries[0], other_q, fresh.reshape(rows, 2 * HD)], axis=1)
    table = jnp.dot(select, table, preferred_element_type=jnp.float32)
    hit = mine[:, None] == jnp.arange(rows, dtype=jnp.int32)[None, :]
    adopt_len = jnp.sum(jnp.where(hit, handed[None, :], 0), axis=1)
    (res,) = attend(N_ROUNDS, 2, lengths[0, adopt:], table, [resident_cache[0, 0]])
    own_residual = lax.dynamic_slice_in_dim(residual[0], rank * chunk, chunk, axis=1)

    table = after(table, [*passed, res, own_residual])
    kept, traded = attend(0, GROUP, adopt_len, table, arrived)

    adopted, done = None, 0
    def beside(ready, count):
        nonlocal adopted, done
        blocks = (arrived + passed)[done : done + count]
        carry = arrived[len(passed)]
        adopted, carry = place(index, done, blocks, adopt, adopted, ready, carry)
        done += count
        passed.append(swap(carry, tp_count))

    traded = swap(traded, tp_count)
    beside(kept, 2)
    parts = project(meta, order, kept, traded, res, out_weight, tp_count)
    first = parts[0]
    parts = [first] + [swap(part, tp_count, bits) for part, bits in zip(parts[1:], NEAR)]
    beside(first, 3)
    parts = near_sum(meta, [after(parts[0], passed[:-1])] + parts[1:])
    first = parts[0]
    parts = [first] + [swap(part, tp_count, bits) for part, bits in zip(parts[1:], FAR)]
    beside(first, 3)
    mixed = far_sum([after(parts[0], passed[:-1])] + parts[1:], own_residual)
    parts = [mixed] + [swap(mixed, tp_count, bits) for bits in FAR]
    beside(mixed, 3)
    mixed = stack(meta, [after(mixed, passed[:-1])] + parts[1:])
    parts = [mixed] + [swap(mixed, tp_count, bits) for bits in NEAR]
    beside(mixed, 3)
    mixed = join(meta, parts, tp_count)
    (adopted,) = place(index, done, (arrived + passed)[done:], adopt, adopted)
    return (mixed, adopted[None, None])


def solution(mesh):
    in_specs = (
        P("inst", "tp", None, None, None),
        P("inst", "tp", None, None, None, None),
        P("inst", None, None, None),
        P("inst", None, "tp"),
        P("inst", None, None),
        P("inst", None),
        P("tp", None),
    )
    out_specs = (P("inst", None, None), P("inst", "tp", None, None, None, None))
    return jax.shard_map(
        on_device, mesh=mesh, in_specs=in_specs, out_specs=out_specs, check_vma=False
    )
```

time: 159 us -> 133 us (0.84)
  waiting for transfers between devices: 70.1 us -> 42.5 us
  local copies, waits for them, and re-layouts: 8.07 us -> 4.51 us
  Pallas kernels: 11.6 us -> 15.1 us
    ppermute x10 -> x22, starting transfers between devices: 12.9 us -> 33.3 us  [swap(): return lax.ppermute(value, 'tp', [(t, t ^ bits) for t in range(tp_count)])]
    ppermute x10 -> x22, waiting for transfers between devices: 43.8 us -> 25.5 us  [swap(): return lax.ppermute(value, 'tp', [(t, t ^ bits) for t in range(tp_count)])]
    all_to_all x2 -> x0, waiting for transfers between devices: 13.7 us -> none  [the longest x1 13.7 us: on_device(): parts = lax.all_to_all(parts, 'tp', 0, 0)]
    all_to_all x2 -> x0, starting transfers between devices: 13.5 us -> none  [the longest x1 8.62 us: on_device(): parts = lax.all_to_all(parts, 'tp', 0, 0)]
    ppermute x9, starting transfers between devices: 40.9 us -> 35 us  [hop(): return lax.ppermute(value, ('inst', 'tp'), pairs)]
    ppermute x9, waiting for transfers between devices: 12.6 us -> 17 us  [hop(): return lax.ppermute(value, ('inst', 'tp'), pairs)]
    pallas_call x5 -> x11, Pallas kernels: 8.39 us -> 11.9 us  [the longest x6 8.51 us: place(): pl.pallas_call(functools.partial(place_kernel, offset, count, len(out)),...]
    unnamed x35 -> x10, local copies, waits for them, and re-layouts: 5.16 us -> 1.68 us
  transfers between devices with their start and end apart: 21 -> 31, of which waited for: 13 -> 12; matrix products, arithmetic and copies ran while one was open for 2% -> 3% of each run, Pallas kernels for 4% -> 7%
where the time goes in v2:
time: 133 us; the launch traced here: 132 us
  starting transfers between devices  68.3 us (51%)
  waiting for transfers between devices  42.5 us (32%)
  Pallas kernels  15.1 us (11%)
  local copies, waits for them, and re-layouts  4.51 us (3%)
    ppermute x9, starting transfers between devices, hop(): return lax.ppermute(value, ('inst', 'tp'), pairs)  35 us
    ppermute x22, starting transfers between devices, swap(): return lax.ppermute(value, 'tp', [(t, t ^ bits) for t in range(tp_count)])  33.3 us
    ppermute x22, waiting for transfers between devices, swap(): return lax.ppermute(value, 'tp', [(t, t ^ bits) for t in range(tp_count)])  25.5 us
    ppermute x9, waiting for transfers between devices, hop(): return lax.ppermute(value, ('inst', 'tp'), pairs)  17 us
    pallas_call x6, Pallas kernels, place(): pl.pallas_call(functools.partial(place_kernel, offset, count, len(out)),...  8.51 us
  transfers between devices with their start and end apart: 31, of which 12 were waited for; matrix products, arithmetic and copies ran while one was open for 3% of the time, Pallas kernels for 7%

profile of v2, /device:TPU:8, one launch (start us, length us, event | category | flops | bytes accessed | tf_op | source)
XLA Modules:
  0.0 132.4 jit_solution(16981529969476828820)
XLA Ops:
  0.6 2.0 %collective-permute-start.1 = (bf16[24,256]{1,0:T(8,128)(2,1)}, bf16[24,256]{1,0:T(8,128)(2,1)S(1)}, u32[]{:S(2)}, u32[]{:S(2)}) collective-permute-start(bf16[24,256]{1,0:T(8,128)(2,1)} %bitcast.29), channel_id=1, source_target_pairs={{0,1},{1,0},{2,3},{3,2},{4,5},{5,4},{6,7},{7,6},{8,9},{9,8},{10,11... | collective-permute-start | bytes 36872 | tf_op jit(solution)/shard_map/ppermute | solution.py:323
  2.6 2.3 %collective-permute-start = (s32[24]{0:T(128)}, s32[24]{0:T(128)S(1)}, u32[]{:S(2)}, u32[]{:S(2)}) collective-permute-start(s32[24]{0:T(128)} %bitcast.31), channel_id=1, source_target_pairs={{0,128},{1,129},{2,130},{3,131},{4,132},{5,133},{6,134},{7,135},{8... | collective-permute-start | bytes 296 | tf_op jit(solution)/shard_map/ppermute | solution.py:315
  4.9 2.9 %collective-permute-done = s32[24]{0:T(128)S(1)} collective-permute-done((s32[24]{0:T(128)}, s32[24]{0:T(128)S(1)}, u32[]{:S(2)}, u32[]{:S(2)}) %collective-permute-start) | collective-permute-done | bytes 128 | tf_op jit(solution)/shard_map/ppermute | solution.py:315
  7.8 2.4 %extract.1 = (bf16[2,512,128]{2,1,0:T(8,128)(2,1)}, bf16[2,512,128]{2,1,0:T(8,128)(2,1)}, bf16[2,512,128]{2,1,0:T(8,128)(2,1)}, bf16[2,512,128]{2,1,0:T(8,128)(2...) custom-call(s32[1]{0:T(128)} %bitcast.meta_ref, ...), custom_call_target="tpu_custom_call" | custom-call | tf_op jit(solution)/shard_map/extract/pallas_call | solution.py:87
  10.2 2.4 %collective-permute-start.2 = (bf16[2,512,128]{2,1,0:T(8,128)(2,1)}, bf16[2,512,128]{2,1,0:T(8,128)(2,1)S(1)}, u32[]{:S(2)}, u32[]{:S(2)}) collective-permute-start(bf16[2,512,128]{2,1,0:T(8,128)(2,1)} %get-tuple-element.36), channel_id=1, source_target_pairs={{0,128},{1,129},{2,130},{3,131},{4,132},{5,133},{6,134},{7,135},{8... | collective-permute-start | bytes 786440 | tf_op jit(solution)/shard_map/ppermute | solution.py:315
  12.6 6.5 %collective-permute-start.4 = (bf16[2,512,128]{2,1,0:T(8,128)(2,1)}, bf16[2,512,128]{2,1,0:T(8,128)(2,1)S(1)}, u32[]{:S(2)}, u32[]{:S(2)}) collective-permute-start(bf16[2,512,128]{2,1,0:T(8,128)(2,1)} %get-tuple-element.37), channel_id=1, source_target_pairs={{0,133},{1,132},{2,135},{3,134},{4,129},{5,128},{6,131},{7,130},{8... | collective-permute-start | bytes 786440 | tf_op jit(solution)/shard_map/ppermute | solution.py:315
  19.9 4.8 %collective-permute-start.6 = (bf16[2,512,128]{2,1,0:T(8,128)(2,1)}, bf16[2,512,128]{2,1,0:T(8,128)(2,1)S(1)}, u32[]{:S(2)}, u32[]{:S(2)}) collective-permute-start(bf16[2,512,128]{2,1,0:T(8,128)(2,1)} %get-tuple-element.38), channel_id=1, source_target_pairs={{0,136},{1,137},{2,138},{3,139},{4,140},{5,141},{6,142},{7,143},{8... | collective-permute-start | bytes 786440 | tf_op jit(solution)/shard_map/ppermute | solution.py:315
  24.6 1.0 collective-permute-start.3
  25.7 7.1 %collective-permute-done.4.rest_1_ = bf16[2,512,128]{2,1,0:T(8,128)(2,1)S(1)} collective-permute-done((bf16[2,512,128]{2,1,0:T(8,128)(2,1)}, bf16[2,512,128]{2,1,0:T(8,128)(2,1)S(1)}, u32[]{:S(2)}, u32[]{:S(2)}) %collective-permute-start.4) | collective-permute-done | bytes 262176 | tf_op jit(solution)/shard_map/ppermute | solution.py:315
  33.7 5.3 %collective-permute-start.9 = (bf16[2,512,128]{2,1,0:T(8,128)(2,1)}, bf16[2,512,128]{2,1,0:T(8,128)(2,1)S(1)}, u32[]{:S(2)}, u32[]{:S(2)}) collective-permute-start(bf16[2,512,128]{2,1,0:T(8,128)(2,1)} %get-tuple-element.41), channel_id=1, source_target_pairs={{0,130},{1,135},{2,132},{3,129},{4,134},{5,131},{6,128},{7,133},{8... | collective-permute-start | bytes 786440 | tf_op jit(solution)/shard_map/ppermute | solution.py:315
  39.0 8.0 %collective-permute-start.10 = (bf16[2,512,128]{2,1,0:T(8,128)(2,1)}, bf16[2,512,128]{2,1,0:T(8,128)(2,1)S(1)}, u32[]{:S(2)}, u32[]{:S(2)}) collective-permute-start(bf16[2,512,128]{2,1,0:T(8,128)(2,1)} %get-tuple-element.42), channel_id=1, source_target_pairs={{0,143},{1,138},{2,137},{3,140},{4,139},{5,142},{6,141},{7,136},{8... | collective-permute-start | bytes 786440 | tf_op jit(solution)/shard_map/ppermute | solution.py:315
  47.0 3.0 %collective-permute-start.11 = (bf16[2,512,128]{2,1,0:T(8,128)(2,1)}, bf16[2,512,128]{2,1,0:T(8,128)(2,1)S(1)}, u32[]{:S(2)}, u32[]{:S(2)}) collective-permute-start(bf16[2,512,128]{2,1,0:T(8,128)(2,1)} %get-tuple-element.43), channel_id=1, source_target_pairs={{0,138},{1,143},{2,140},{3,137},{4,142},{5,139},{6,136},{7,141},{8... | collective-permute-start | bytes 786440 | tf_op jit(solution)/shard_map/ppermute | solution.py:315
  50.0 2.7 %collective-permute-start.12 = (bf16[2,512,128]{2,1,0:T(8,128)(2,1)}, bf16[2,512,128]{2,1,0:T(8,128)(2,1)S(1)}, u32[]{:S(2)}, u32[]{:S(2)}) collective-permute-start(bf16[2,512,128]{2,1,0:T(8,128)(2,1)} %get-tuple-element.44), channel_id=1, source_target_pairs={{0,135},{1,130},{2,129},{3,132},{4,131},{5,134},{6,133},{7,128},{8... | collective-permute-start | bytes 786440 | tf_op jit(solution)/shard_map/ppermute | solution.py:315
  52.7 1.0 collective-permute-start.7
  54.6 0.9 fusion.rows_ref
  55.5 1.6 %copy-done.2 = bf16[1,1,8,2,512,128]{5,4,3,2,1,0:T(8,128)(2,1)S(1)} copy-done((bf16[1,1,8,2,512,128]{5,4,3,2,1,0:T(8,128)(2,1)S(1)}, bf16[1,1,8,2,512,128]{5,4,3,2,1,0:T(8,128)(2,1)}, u32[]{:S(2)}) %copy-start.2) | copy-done | bytes 2097176
  57.0 1.2 attend.2.res_ref
  58.3 3.6 %collective-permute-done.7.rest_2_ = bf16[2,512,128]{2,1,0:T(8,128)(2,1)S(1)} collective-permute-done((bf16[2,512,128]{2,1,0:T(8,128)(2,1)S(1)}, bf16[2,512,128]{2,1,0:T(8,128)(2,1)S(1)}, u32[]{:S(2)}, u32[]{:S(2)}) %collective-permute-start.7) | collective-permute-done | bytes 262176 | tf_op jit(solution)/shard_map/ppermute | solution.py:323
  61.9 4.3 %collective-permute-done.11.rest_6_.rest_1_.rest_5_ = bf16[2,512,128]{2,1,0:T(8,128)(2,1)S(1)} collective-permute-done((bf16[2,512,128]{2,1,0:T(8,128)(2,1)}, bf16[2,512,128]{2,1,0:T(8,128)(2,1)S(1)}, u32[]{:S(2)}, u32[]{:S(2)}) %collective-permute-start.11) | collective-permute-done | bytes 262176 | tf_op jit(solution)/shard_map/ppermute | solution.py:315
  66.2 2.7 %collective-permute-done.12.rest_7_.rest_2_.rest_5_ = bf16[2,512,128]{2,1,0:T(8,128)(2,1)S(1)} collective-permute-done((bf16[2,512,128]{2,1,0:T(8,128)(2,1)}, bf16[2,512,128]{2,1,0:T(8,128)(2,1)S(1)}, u32[]{:S(2)}, u32[]{:S(2)}) %collective-permute-start.12) | collective-permute-done | bytes 262176 | tf_op jit(solution)/shard_map/ppermute | solution.py:315
  68.9 1.2 attend.3
  70.1 1.4 %place.6 = (bf16[16,2,512,128]{3,2,1,0:T(8,128)(2,1)}, bf16[2,512,128]{2,1,0:T(8,128)(2,1)S(1)}) custom-call(s32[16]{0:T(128)S(1)} %get-tuple-element.68.index_ref, bf16[2,512,128]{2,1,0:T(8,128)(2,1)S(1)} %collective-permute-done.2.rest_0_, bf16[2,512,128]{2,1,0:T(8,128)(2,1)S(1)} %collective-permute-done.4.rest_1_, ...), custom_call_target="tpu_custom_call", output_to_operand_aliasing={{1}: (4, {})} | custom-call | tf_op jit(solution)/shard_map/place/pallas_call | solution.py:124
  71.5 1.4 %collective-permute-start.14 = (bf16[2,512,128]{2,1,0:T(8,128)(2,1)S(1)}, bf16[2,512,128]{2,1,0:T(8,128)(2,1)S(1)}, u32[]{:S(2)}, u32[]{:S(2)}) collective-permute-start(bf16[2,512,128]{2,1,0:T(8,128)(2,1)S(1)} %get-tuple-element.48), channel_id=1, source_target_pairs={{0,1},{1,0},{2,3},{3,2},{4,5},{5,4},{6,7},{7,6},{8,9},{9,8},{10,11... | collective-permute-start | bytes 786440 | tf_op jit(solution)/shard_map/ppermute | solution.py:323
  74.3 4.2 %collective-permute-done.13.traded_ref = f32[8,256]{1,0:T(8,128)S(1)} collective-permute-done((f32[8,256]{1,0:T(8,128)S(1)}, f32[8,256]{1,0:T(8,128)S(1)}, u32[]{:S(2)}, u32[]{:S(2)}) %collective-permute-start.13) | collective-permute-done | bytes 8224 | tf_op jit(solution)/shard_map/ppermute | solution.py:323
  78.5 0.9 project.1
  79.4 0.9 collective-permute-start.15
  80.3 2.8 %collective-permute-start.16 = (bf16[4,24,512]{2,1,0:T(8,128)(2,1)S(1)}, bf16[4,24,512]{2,1,0:T(8,128)(2,1)S(1)}, u32[]{:S(2)}, u32[]{:S(2)}) collective-permute-start(bf16[4,24,512]{2,1,0:T(8,128)(2,1)S(1)} %get-tuple-element.51), channel_id=1, source_target_pairs={{0,8},{1,9},{2,10},{3,11},{4,12},{5,13},{6,14},{7,15},{8,0},{9,1},... | collective-permute-start | bytes 294920 | tf_op jit(solution)/shard_map/ppermute | solution.py:323
  83.0 1.4 %collective-permute-start.17 = (bf16[4,24,512]{2,1,0:T(8,128)(2,1)S(1)}, bf16[4,24,512]{2,1,0:T(8,128)(2,1)S(1)}, u32[]{:S(2)}, u32[]{:S(2)}) collective-permute-start(bf16[4,24,512]{2,1,0:T(8,128)(2,1)S(1)} %get-tuple-element.52), channel_id=1, source_target_pairs={{0,9},{1,8},{2,11},{3,10},{4,13},{5,12},{6,15},{7,14},{8,1},{9,0},... | collective-permute-start | bytes 294920 | tf_op jit(solution)/shard_map/ppermute | solution.py:323
  84.5 1.4 %place.7 = (bf16[16,2,512,128]{3,2,1,0:T(8,128)(2,1)}, bf16[2,512,128]{2,1,0:T(8,128)(2,1)S(1)}) custom-call(s32[16]{0:T(128)S(1)} %get-tuple-element.68.index_ref, bf16[2,512,128]{2,1,0:T(8,128)(2,1)S(1)} %collective-permute-done.6.rest_2_.rest_0_, ...), custom_call_target="tpu_custom_call", output_to_operand_aliasing={{0}: (4, {}), {1}: (6, {})} | custom-call | tf_op jit(solution)/shard_map/place/pallas_call | solution.py:124
  85.9 0.9 collective-permute-start.18
  87.3 3.4 %collective-permute-done.17.refs_3_ = bf16[4,24,512]{2,1,0:T(8,128)(2,1)S(1)} collective-permute-done((bf16[4,24,512]{2,1,0:T(8,128)(2,1)S(1)}, bf16[4,24,512]{2,1,0:T(8,128)(2,1)S(1)}, u32[]{:S(2)}, u32[]{:S(2)}) %collective-permute-start.17) | collective-permute-done | bytes 98336 | tf_op jit(solution)/shard_map/ppermute | solution.py:323
  90.8 1.4 %place.8 = (bf16[16,2,512,128]{3,2,1,0:T(8,128)(2,1)}, bf16[2,512,128]{2,1,0:T(8,128)(2,1)S(1)}) custom-call(s32[16]{0:T(128)S(1)} %get-tuple-element.68.index_ref, bf16[2,512,128]{2,1,0:T(8,128)(2,1)S(1)} %collective-permute-done.10.rest_5_.rest_0_, ...), custom_call_target="tpu_custom_call", output_to_operand_aliasing={{0}: (4, {}), {1}: (6, {})} | custom-call | tf_op jit(solution)/shard_map/place/pallas_call | solution.py:124
  93.0 1.2 collective-permute-start.19
  94.2 3.6 %collective-permute-start.20 = (f32[24,512]{1,0:T(8,128)S(1)}, f32[24,512]{1,0:T(8,128)S(1)}, u32[]{:S(2)}, u32[]{:S(2)}) collective-permute-start(f32[24,512]{1,0:T(8,128)S(1)} %get-tuple-element.58), channel_id=1, source_target_pairs={{0,4},{1,5},{2,6},{3,7},{4,0},{5,1},{6,2},{7,3},{8,12},{9,13},{10,... | collective-permute-start | bytes 147464 | tf_op jit(solution)/shard_map/ppermute | solution.py:323
  97.8 1.7 %collective-permute-start.21 = (f32[24,512]{1,0:T(8,128)S(1)}, f32[24,512]{1,0:T(8,128)S(1)}, u32[]{:S(2)}, u32[]{:S(2)}) collective-permute-start(f32[24,512]{1,0:T(8,128)S(1)} %get-tuple-element.59), channel_id=1, source_target_pairs={{0,6},{1,7},{2,4},{3,5},{4,2},{5,3},{6,0},{7,1},{8,14},{9,15},{10,... | collective-permute-start | bytes 147464 | tf_op jit(solution)/shard_map/ppermute | solution.py:323
  99.5 6.6 %collective-permute-done.20.refs_2_ = f32[24,512]{1,0:T(8,128)S(1)} collective-permute-done((f32[24,512]{1,0:T(8,128)S(1)}, f32[24,512]{1,0:T(8,128)S(1)}, u32[]{:S(2)}, u32[]{:S(2)}) %collective-permute-start.20) | collective-permute-done | bytes 49184 | tf_op jit(solution)/shard_map/ppermute | solution.py:323
  106.2 0.9 collective-permute-start.23
  107.1 2.0 %collective-permute-start.24 = (bf16[24,512]{1,0:T(8,128)(2,1)S(1)}, bf16[24,512]{1,0:T(8,128)(2,1)S(1)}, u32[]{:S(2)}, u32[]{:S(2)}) collective-permute-start(bf16[24,512]{1,0:T(8,128)(2,1)S(1)} %far_sum.1.refs_0_.rest_4_), channel_id=1, source_target_pairs={{0,4},{1,5},{2,6},{3,7},{4,0},{5,1},{6,2},{7,3},{8,12},{9,13},{10,... | collective-permute-start | bytes 73736 | tf_op jit(solution)/shard_map/ppermute | solution.py:323
  109.0 3.7 %collective-permute-start.25 = (bf16[24,512]{1,0:T(8,128)(2,1)S(1)}, bf16[24,512]{1,0:T(8,128)(2,1)S(1)}, u32[]{:S(2)}, u32[]{:S(2)}) collective-permute-start(bf16[24,512]{1,0:T(8,128)(2,1)S(1)} %far_sum.1.refs_0_.rest_4_), channel_id=1, source_target_pairs={{0,6},{1,7},{2,4},{3,5},{4,2},{5,3},{6,0},{7,1},{8,14},{9,15},{10,... | collective-permute-start | bytes 73736 | tf_op jit(solution)/shard_map/ppermute | solution.py:323
  112.7 1.4 %place.9 = (bf16[16,2,512,128]{3,2,1,0:T(8,128)(2,1)}, bf16[2,512,128]{2,1,0:T(8,128)(2,1)S(1)}) custom-call(s32[16]{0:T(128)S(1)} %get-tuple-element.68.index_ref, bf16[2,512,128]{2,1,0:T(8,128)(2,1)S(1)} %collective-permute-done.3.rest_0_, bf16[2,512,128]{2,1,0:T(8,128)(2,1)S(1)} %collective-permute-done.5.rest_1_, ...), custom_call_target="tpu_custom_call", output_to_operand_aliasing={{0}: (4, {}), {1}: (6, {})} | custom-call | tf_op jit(solution)/shard_map/place/pallas_call | solution.py:124
  114.5 0.9 collective-permute-done.24.refs_2_
  115.4 1.4 %place.10 = (bf16[16,2,512,128]{3,2,1,0:T(8,128)(2,1)}, bf16[2,512,128]{2,1,0:T(8,128)(2,1)S(1)}) custom-call(s32[16]{0:T(128)S(1)} %get-tuple-element.68.index_ref, bf16[2,512,128]{2,1,0:T(8,128)(2,1)S(1)} %collective-permute-done.14.rest_0_, ...), custom_call_target="tpu_custom_call", output_to_operand_aliasing={{0}: (4, {}), {1}: (6, {})} | custom-call | tf_op jit(solution)/shard_map/place/pallas_call | solution.py:124
  116.9 1.9 %collective-permute-start.30 = (bf16[2,512,128]{2,1,0:T(8,128)(2,1)S(1)}, bf16[2,512,128]{2,1,0:T(8,128)(2,1)S(1)}, u32[]{:S(2)}, u32[]{:S(2)}) collective-permute-start(bf16[2,512,128]{2,1,0:T(8,128)(2,1)S(1)} %get-tuple-element.66), channel_id=1, source_target_pairs={{0,1},{1,0},{2,3},{3,2},{4,5},{5,4},{6,7},{7,6},{8,9},{9,8},{10,11... | collective-permute-start | bytes 786440 | tf_op jit(solution)/shard_map/ppermute | solution.py:323
  119.0 2.5 %collective-permute-start.27 = (bf16[4,24,512]{2,1,0:T(8,128)(2,1)S(1)}, bf16[4,24,512]{2,1,0:T(8,128)(2,1)S(1)}, u32[]{:S(2)}, u32[]{:S(2)}) collective-permute-start(bf16[4,24,512]{2,1,0:T(8,128)(2,1)S(1)} %stack.1.refs_0_.rest_4_), channel_id=1, source_target_pairs={{0,8},{1,9},{2,10},{3,11},{4,12},{5,13},{6,14},{7,15},{8,0},{9,1},... | collective-permute-start | bytes 294920 | tf_op jit(solution)/shard_map/ppermute | solution.py:323
  121.5 2.3 %collective-permute-start.28 = (bf16[4,24,512]{2,1,0:T(8,128)(2,1)S(1)}, bf16[4,24,512]{2,1,0:T(8,128)(2,1)S(1)}, u32[]{:S(2)}, u32[]{:S(2)}) collective-permute-start(bf16[4,24,512]{2,1,0:T(8,128)(2,1)S(1)} %stack.1.refs_0_.rest_4_), channel_id=1, source_target_pairs={{0,9},{1,8},{2,11},{3,10},{4,13},{5,12},{6,15},{7,14},{8,1},{9,0},... | collective-permute-start | bytes 294920 | tf_op jit(solution)/shard_map/ppermute | solution.py:323
  123.8 3.8 %collective-permute-done.26.refs_1_ = bf16[4,24,512]{2,1,0:T(8,128)(2,1)S(1)} collective-permute-done((bf16[4,24,512]{2,1,0:T(8,128)(2,1)S(1)}, bf16[4,24,512]{2,1,0:T(8,128)(2,1)S(1)}, u32[]{:S(2)}, u32[]{:S(2)}) %collective-permute-start.26) | collective-permute-done | bytes 98336 | tf_op jit(solution)/shard_map/ppermute | solution.py:323
  127.6 2.5 %collective-permute-done.28.refs_3_ = bf16[4,24,512]{2,1,0:T(8,128)(2,1)S(1)} collective-permute-done((bf16[4,24,512]{2,1,0:T(8,128)(2,1)S(1)}, bf16[4,24,512]{2,1,0:T(8,128)(2,1)S(1)}, u32[]{:S(2)}, u32[]{:S(2)}) %collective-permute-start.28) | collective-permute-done | bytes 98336 | tf_op jit(solution)/shard_map/ppermute | solution.py:323
  130.8 1.4 %place.11 = bf16[16,2,512,128]{3,2,1,0:T(8,128)(2,1)} custom-call(s32[16]{0:T(128)S(1)} %get-tuple-element.68.index_ref, bf16[2,512,128]{2,1,0:T(8,128)(2,1)S(1)} %collective-permute-done.29.rest_0_, bf16[2,512,128]{2,1,0:T(8,128)(2,1)S(1)} %collective-permute-done.30.rest_1_, ...), custom_call_target="tpu_custom_call", output_to_operand_aliasing={{}: (3, {})} | custom-call | tf_op jit(solution)/shard_map/place/pallas_call | solution.py:124
  (46 shorter events, 6.7 us)
Async XLA Ops:
  0.6 18.5 %copy-start = (bf16[1,24,8192]{2,1,0:T(8,128)(2,1)S(1)}, bf16[1,24,8192]{2,1,0:T(8,128)(2,1)}, u32[]{:S(2)}) copy-start(bf16[1,24,8192]{2,1,0:T(8,128)(2,1)} %param.14) | copy-start | bytes 1179652
  0.6 7.2 %collective-permute-start.1 = (bf16[24,256]{1,0:T(8,128)(2,1)}, bf16[24,256]{1,0:T(8,128)(2,1)S(1)}, u32[]{:S(2)}, u32[]{:S(2)}) collective-permute-start(bf16[24,256]{1,0:T(8,128)(2,1)} %bitcast.29), channel_id=1, source_target_pairs={{0,1},{1,0},{2,3},{3,2},{4,5},{5,4},{6,7},{7,6},{8,9},{9,8},{10,11... | collective-permute-start | bytes 36872 | tf_op jit(solution)/shard_map/ppermute | solution.py:323
  2.6 5.2 %collective-permute-start = (s32[24]{0:T(128)}, s32[24]{0:T(128)S(1)}, u32[]{:S(2)}, u32[]{:S(2)}) collective-permute-start(s32[24]{0:T(128)} %bitcast.31), channel_id=1, source_target_pairs={{0,128},{1,129},{2,130},{3,131},{4,132},{5,133},{6,134},{7,135},{8... | collective-permute-start | bytes 296 | tf_op jit(solution)/shard_map/ppermute | solution.py:315
  10.2 14.4 %collective-permute-start.2 = (bf16[2,512,128]{2,1,0:T(8,128)(2,1)}, bf16[2,512,128]{2,1,0:T(8,128)(2,1)S(1)}, u32[]{:S(2)}, u32[]{:S(2)}) collective-permute-start(bf16[2,512,128]{2,1,0:T(8,128)(2,1)} %get-tuple-element.36), channel_id=1, source_target_pairs={{0,128},{1,129},{2,130},{3,131},{4,132},{5,133},{6,134},{7,135},{8... | collective-permute-start | bytes 786440 | tf_op jit(solution)/shard_map/ppermute | solution.py:315
  12.6 20.2 %collective-permute-start.4 = (bf16[2,512,128]{2,1,0:T(8,128)(2,1)}, bf16[2,512,128]{2,1,0:T(8,128)(2,1)S(1)}, u32[]{:S(2)}, u32[]{:S(2)}) collective-permute-start(bf16[2,512,128]{2,1,0:T(8,128)(2,1)} %get-tuple-element.37), channel_id=1, source_target_pairs={{0,133},{1,132},{2,135},{3,134},{4,129},{5,128},{6,131},{7,130},{8... | collective-permute-start | bytes 786440 | tf_op jit(solution)/shard_map/ppermute | solution.py:315
  19.9 19.1 %collective-permute-start.6 = (bf16[2,512,128]{2,1,0:T(8,128)(2,1)}, bf16[2,512,128]{2,1,0:T(8,128)(2,1)S(1)}, u32[]{:S(2)}, u32[]{:S(2)}) collective-permute-start(bf16[2,512,128]{2,1,0:T(8,128)(2,1)} %get-tuple-element.38), channel_id=1, source_target_pairs={{0,136},{1,137},{2,138},{3,139},{4,140},{5,141},{6,142},{7,143},{8... | collective-permute-start | bytes 786440 | tf_op jit(solution)/shard_map/ppermute | solution.py:315
  24.6 22.3 %collective-permute-start.8 = (bf16[2,512,128]{2,1,0:T(8,128)(2,1)}, bf16[2,512,128]{2,1,0:T(8,128)(2,1)S(1)}, u32[]{:S(2)}, u32[]{:S(2)}) collective-permute-start(bf16[2,512,128]{2,1,0:T(8,128)(2,1)} %get-tuple-element.40), channel_id=1, source_target_pairs={{0,141},{1,140},{2,143},{3,142},{4,137},{5,136},{6,139},{7,138},{8... | collective-permute-start | bytes 786440 | tf_op jit(solution)/shard_map/ppermute | solution.py:315
  24.6 25.4 %collective-permute-start.3 = (bf16[2,512,128]{2,1,0:T(8,128)(2,1)S(1)}, bf16[2,512,128]{2,1,0:T(8,128)(2,1)S(1)}, u32[]{:S(2)}, u32[]{:S(2)}) collective-permute-start(bf16[2,512,128]{2,1,0:T(8,128)(2,1)S(1)} %collective-permute-done.2.rest_0_), channel_id=1, source_target_pairs={{0,1},{1,0},{2,3},{3,2},{4,5},{5,4},{6,7},{7,6},{8,9},{9,8},{10,11... | collective-permute-start | bytes 786440 | tf_op jit(solution)/shard_map/ppermute | solution.py:323
  32.8 19.9 %collective-permute-start.5 = (bf16[2,512,128]{2,1,0:T(8,128)(2,1)S(1)}, bf16[2,512,128]{2,1,0:T(8,128)(2,1)S(1)}, u32[]{:S(2)}, u32[]{:S(2)}) collective-permute-start(bf16[2,512,128]{2,1,0:T(8,128)(2,1)S(1)} %collective-permute-done.4.rest_1_), channel_id=1, source_target_pairs={{0,1},{1,0},{2,3},{3,2},{4,5},{5,4},{6,7},{7,6},{8,9},{9,8},{10,11... | collective-permute-start | bytes 786440 | tf_op jit(solution)/shard_map/ppermute | solution.py:323
  33.7 44.8 %copy-start.1 = (bf16[256,8192]{1,0:T(8,128)(2,1)S(1)}, bf16[256,8192]{1,0:T(8,128)(2,1)}, u32[]{:S(2)}) copy-start(bf16[256,8192]{1,0:T(8,128)(2,1)} %weight_ref.1) | copy-start | bytes 12582916
  33.7 28.2 %collective-permute-start.9 = (bf16[2,512,128]{2,1,0:T(8,128)(2,1)}, bf16[2,512,128]{2,1,0:T(8,128)(2,1)S(1)}, u32[]{:S(2)}, u32[]{:S(2)}) collective-permute-start(bf16[2,512,128]{2,1,0:T(8,128)(2,1)} %get-tuple-element.41), channel_id=1, source_target_pairs={{0,130},{1,135},{2,132},{3,129},{4,134},{5,131},{6,128},{7,133},{8... | collective-permute-start | bytes 786440 | tf_op jit(solution)/shard_map/ppermute | solution.py:315
  39.0 22.9 %collective-permute-start.10 = (bf16[2,512,128]{2,1,0:T(8,128)(2,1)}, bf16[2,512,128]{2,1,0:T(8,128)(2,1)S(1)}, u32[]{:S(2)}, u32[]{:S(2)}) collective-permute-start(bf16[2,512,128]{2,1,0:T(8,128)(2,1)} %get-tuple-element.42), channel_id=1, source_target_pairs={{0,143},{1,138},{2,137},{3,140},{4,139},{5,142},{6,141},{7,136},{8... | collective-permute-start | bytes 786440 | tf_op jit(solution)/shard_map/ppermute | solution.py:315
  47.0 19.3 %collective-permute-start.11 = (bf16[2,512,128]{2,1,0:T(8,128)(2,1)}, bf16[2,512,128]{2,1,0:T(8,128)(2,1)S(1)}, u32[]{:S(2)}, u32[]{:S(2)}) collective-permute-start(bf16[2,512,128]{2,1,0:T(8,128)(2,1)} %get-tuple-element.43), channel_id=1, source_target_pairs={{0,138},{1,143},{2,140},{3,137},{4,142},{5,139},{6,136},{7,141},{8... | collective-permute-start | bytes 786440 | tf_op jit(solution)/shard_map/ppermute | solution.py:315
  50.0 18.9 %collective-permute-start.12 = (bf16[2,512,128]{2,1,0:T(8,128)(2,1)}, bf16[2,512,128]{2,1,0:T(8,128)(2,1)S(1)}, u32[]{:S(2)}, u32[]{:S(2)}) collective-permute-start(bf16[2,512,128]{2,1,0:T(8,128)(2,1)} %get-tuple-element.44), channel_id=1, source_target_pairs={{0,135},{1,130},{2,129},{3,132},{4,131},{5,134},{6,133},{7,128},{8... | collective-permute-start | bytes 786440 | tf_op jit(solution)/shard_map/ppermute | solution.py:315
  52.7 9.2 %collective-permute-start.7 = (bf16[2,512,128]{2,1,0:T(8,128)(2,1)S(1)}, bf16[2,512,128]{2,1,0:T(8,128)(2,1)S(1)}, u32[]{:S(2)}, u32[]{:S(2)}) collective-permute-start(bf16[2,512,128]{2,1,0:T(8,128)(2,1)S(1)} %collective-permute-done.6.rest_2_.rest_0_), channel_id=1, source_target_pairs={{0,1},{1,0},{2,3},{3,2},{4,5},{5,4},{6,7},{7,6},{8,9},{9,8},{10,11... | collective-permute-start | bytes 786440 | tf_op jit(solution)/shard_map/ppermute | solution.py:323
  55.4 1.6 %copy-start.2 = (bf16[1,1,8,2,512,128]{5,4,3,2,1,0:T(8,128)(2,1)S(1)}, bf16[1,1,8,2,512,128]{5,4,3,2,1,0:T(8,128)(2,1)}, u32[]{:S(2)}) copy-start(bf16[1,1,8,2,512,128]{5,4,3,2,1,0:T(8,128)(2,1)} %param.11) | copy-start | bytes 6291460
  71.5 15.4 %collective-permute-start.14 = (bf16[2,512,128]{2,1,0:T(8,128)(2,1)S(1)}, bf16[2,512,128]{2,1,0:T(8,128)(2,1)S(1)}, u32[]{:S(2)}, u32[]{:S(2)}) collective-permute-start(bf16[2,512,128]{2,1,0:T(8,128)(2,1)S(1)} %get-tuple-element.48), channel_id=1, source_target_pairs={{0,1},{1,0},{2,3},{3,2},{4,5},{5,4},{6,7},{7,6},{8,9},{9,8},{10,11... | collective-permute-start | bytes 786440 | tf_op jit(solution)/shard_map/ppermute | solution.py:323
  72.8 5.7 %collective-permute-start.13 = (f32[8,256]{1,0:T(8,128)S(1)}, f32[8,256]{1,0:T(8,128)S(1)}, u32[]{:S(2)}, u32[]{:S(2)}) collective-permute-start(f32[8,256]{1,0:T(8,128)S(1)} %get-tuple-element.46), channel_id=1, source_target_pairs={{0,1},{1,0},{2,3},{3,2},{4,5},{5,4},{6,7},{7,6},{8,9},{9,8},{10,11... | collective-permute-start | bytes 24584 | tf_op jit(solution)/shard_map/ppermute | solution.py:323
  79.4 7.5 %collective-permute-start.15 = (bf16[4,24,512]{2,1,0:T(8,128)(2,1)S(1)}, bf16[4,24,512]{2,1,0:T(8,128)(2,1)S(1)}, u32[]{:S(2)}, u32[]{:S(2)}) collective-permute-start(bf16[4,24,512]{2,1,0:T(8,128)(2,1)S(1)} %get-tuple-element.50), channel_id=1, source_target_pairs={{0,1},{1,0},{2,3},{3,2},{4,5},{5,4},{6,7},{7,6},{8,9},{9,8},{10,11... | collective-permute-start | bytes 294920 | tf_op jit(solution)/shard_map/ppermute | solution.py:323
  80.3 7.1 %collective-permute-start.16 = (bf16[4,24,512]{2,1,0:T(8,128)(2,1)S(1)}, bf16[4,24,512]{2,1,0:T(8,128)(2,1)S(1)}, u32[]{:S(2)}, u32[]{:S(2)}) collective-permute-start(bf16[4,24,512]{2,1,0:T(8,128)(2,1)S(1)} %get-tuple-element.51), channel_id=1, source_target_pairs={{0,8},{1,9},{2,10},{3,11},{4,12},{5,13},{6,14},{7,15},{8,0},{9,1},... | collective-permute-start | bytes 294920 | tf_op jit(solution)/shard_map/ppermute | solution.py:323
  83.0 7.7 %collective-permute-start.17 = (bf16[4,24,512]{2,1,0:T(8,128)(2,1)S(1)}, bf16[4,24,512]{2,1,0:T(8,128)(2,1)S(1)}, u32[]{:S(2)}, u32[]{:S(2)}) collective-permute-start(bf16[4,24,512]{2,1,0:T(8,128)(2,1)S(1)} %get-tuple-element.52), channel_id=1, source_target_pairs={{0,9},{1,8},{2,11},{3,10},{4,13},{5,12},{6,15},{7,14},{8,1},{9,0},... | collective-permute-start | bytes 294920 | tf_op jit(solution)/shard_map/ppermute | solution.py:323
  85.9 13.6 %collective-permute-start.18 = (bf16[2,512,128]{2,1,0:T(8,128)(2,1)S(1)}, bf16[2,512,128]{2,1,0:T(8,128)(2,1)S(1)}, u32[]{:S(2)}, u32[]{:S(2)}) collective-permute-start(bf16[2,512,128]{2,1,0:T(8,128)(2,1)S(1)} %get-tuple-element.55), channel_id=1, source_target_pairs={{0,1},{1,0},{2,3},{3,2},{4,5},{5,4},{6,7},{7,6},{8,9},{9,8},{10,11... | collective-permute-start | bytes 786440 | tf_op jit(solution)/shard_map/ppermute | solution.py:323
  92.2 22.3 %collective-permute-start.22 = (bf16[2,512,128]{2,1,0:T(8,128)(2,1)S(1)}, bf16[2,512,128]{2,1,0:T(8,128)(2,1)S(1)}, u32[]{:S(2)}, u32[]{:S(2)}) collective-permute-start(bf16[2,512,128]{2,1,0:T(8,128)(2,1)S(1)} %get-tuple-element.61), channel_id=1, source_target_pairs={{0,1},{1,0},{2,3},{3,2},{4,5},{5,4},{6,7},{7,6},{8,9},{9,8},{10,11... | collective-permute-start | bytes 786440 | tf_op jit(solution)/shard_map/ppermute | solution.py:323
  93.0 6.5 %collective-permute-start.19 = (f32[24,512]{1,0:T(8,128)S(1)}, f32[24,512]{1,0:T(8,128)S(1)}, u32[]{:S(2)}, u32[]{:S(2)}) collective-permute-start(f32[24,512]{1,0:T(8,128)S(1)} %get-tuple-element.57), channel_id=1, source_target_pairs={{0,2},{1,3},{2,0},{3,1},{4,6},{5,7},{6,4},{7,5},{8,10},{9,11},{10,... | collective-permute-start | bytes 147464 | tf_op jit(solution)/shard_map/ppermute | solution.py:323
  94.2 11.9 %collective-permute-start.20 = (f32[24,512]{1,0:T(8,128)S(1)}, f32[24,512]{1,0:T(8,128)S(1)}, u32[]{:S(2)}, u32[]{:S(2)}) collective-permute-start(f32[24,512]{1,0:T(8,128)S(1)} %get-tuple-element.58), channel_id=1, source_target_pairs={{0,4},{1,5},{2,6},{3,7},{4,0},{5,1},{6,2},{7,3},{8,12},{9,13},{10,... | collective-permute-start | bytes 147464 | tf_op jit(solution)/shard_map/ppermute | solution.py:323
  97.8 8.3 %collective-permute-start.21 = (f32[24,512]{1,0:T(8,128)S(1)}, f32[24,512]{1,0:T(8,128)S(1)}, u32[]{:S(2)}, u32[]{:S(2)}) collective-permute-start(f32[24,512]{1,0:T(8,128)S(1)} %get-tuple-element.59), channel_id=1, source_target_pairs={{0,6},{1,7},{2,4},{3,5},{4,2},{5,3},{6,0},{7,1},{8,14},{9,15},{10,... | collective-permute-start | bytes 147464 | tf_op jit(solution)/shard_map/ppermute | solution.py:323
  106.2 8.4 %collective-permute-start.23 = (bf16[24,512]{1,0:T(8,128)(2,1)S(1)}, bf16[24,512]{1,0:T(8,128)(2,1)S(1)}, u32[]{:S(2)}, u32[]{:S(2)}) collective-permute-start(bf16[24,512]{1,0:T(8,128)(2,1)S(1)} %far_sum.1.refs_0_.rest_4_), channel_id=1, source_target_pairs={{0,2},{1,3},{2,0},{3,1},{4,6},{5,7},{6,4},{7,5},{8,10},{9,11},{10,... | collective-permute-start | bytes 73736 | tf_op jit(solution)/shard_map/ppermute | solution.py:323
  107.1 8.3 %collective-permute-start.24 = (bf16[24,512]{1,0:T(8,128)(2,1)S(1)}, bf16[24,512]{1,0:T(8,128)(2,1)S(1)}, u32[]{:S(2)}, u32[]{:S(2)}) collective-permute-start(bf16[24,512]{1,0:T(8,128)(2,1)S(1)} %far_sum.1.refs_0_.rest_4_), channel_id=1, source_target_pairs={{0,4},{1,5},{2,6},{3,7},{4,0},{5,1},{6,2},{7,3},{8,12},{9,13},{10,... | collective-permute-start | bytes 73736 | tf_op jit(solution)/shard_map/ppermute | solution.py:323
  109.0 6.4 %collective-permute-start.25 = (bf16[24,512]{1,0:T(8,128)(2,1)S(1)}, bf16[24,512]{1,0:T(8,128)(2,1)S(1)}, u32[]{:S(2)}, u32[]{:S(2)}) collective-permute-start(bf16[24,512]{1,0:T(8,128)(2,1)S(1)} %far_sum.1.refs_0_.rest_4_), channel_id=1, source_target_pairs={{0,6},{1,7},{2,4},{3,5},{4,2},{5,3},{6,0},{7,1},{8,14},{9,15},{10,... | collective-permute-start | bytes 73736 | tf_op jit(solution)/shard_map/ppermute | solution.py:323
  114.2 16.6 %collective-permute-start.29 = (bf16[2,512,128]{2,1,0:T(8,128)(2,1)S(1)}, bf16[2,512,128]{2,1,0:T(8,128)(2,1)S(1)}, u32[]{:S(2)}, u32[]{:S(2)}) collective-permute-start(bf16[2,512,128]{2,1,0:T(8,128)(2,1)S(1)} %get-tuple-element.64), channel_id=1, source_target_pairs={{0,1},{1,0},{2,3},{3,2},{4,5},{5,4},{6,7},{7,6},{8,9},{9,8},{10,11... | collective-permute-start | bytes 786440 | tf_op jit(solution)/shard_map/ppermute | solution.py:323
  116.9 14.0 %collective-permute-start.30 = (bf16[2,512,128]{2,1,0:T(8,128)(2,1)S(1)}, bf16[2,512,128]{2,1,0:T(8,128)(2,1)S(1)}, u32[]{:S(2)}, u32[]{:S(2)}) collective-permute-start(bf16[2,512,128]{2,1,0:T(8,128)(2,1)S(1)} %get-tuple-element.66), channel_id=1, source_target_pairs={{0,1},{1,0},{2,3},{3,2},{4,5},{5,4},{6,7},{7,6},{8,9},{9,8},{10,11... | collective-permute-start | bytes 786440 | tf_op jit(solution)/shard_map/ppermute | solution.py:323
  118.8 8.8 %collective-permute-start.26 = (bf16[4,24,512]{2,1,0:T(8,128)(2,1)S(1)}, bf16[4,24,512]{2,1,0:T(8,128)(2,1)S(1)}, u32[]{:S(2)}, u32[]{:S(2)}) collective-permute-start(bf16[4,24,512]{2,1,0:T(8,128)(2,1)S(1)} %stack.1.refs_0_.rest_4_), channel_id=1, source_target_pairs={{0,1},{1,0},{2,3},{3,2},{4,5},{5,4},{6,7},{7,6},{8,9},{9,8},{10,11... | collective-permute-start | bytes 294920 | tf_op jit(solution)/shard_map/ppermute | solution.py:323
  119.0 8.6 %collective-permute-start.27 = (bf16[4,24,512]{2,1,0:T(8,128)(2,1)S(1)}, bf16[4,24,512]{2,1,0:T(8,128)(2,1)S(1)}, u32[]{:S(2)}, u32[]{:S(2)}) collective-permute-start(bf16[4,24,512]{2,1,0:T(8,128)(2,1)S(1)} %stack.1.refs_0_.rest_4_), channel_id=1, source_target_pairs={{0,8},{1,9},{2,10},{3,11},{4,12},{5,13},{6,14},{7,15},{8,0},{9,1},... | collective-permute-start | bytes 294920 | tf_op jit(solution)/shard_map/ppermute | solution.py:323
  121.5 8.6 %collective-permute-start.28 = (bf16[4,24,512]{2,1,0:T(8,128)(2,1)S(1)}, bf16[4,24,512]{2,1,0:T(8,128)(2,1)S(1)}, u32[]{:S(2)}, u32[]{:S(2)}) collective-permute-start(bf16[4,24,512]{2,1,0:T(8,128)(2,1)S(1)} %stack.1.refs_0_.rest_4_), channel_id=1, source_target_pairs={{0,9},{1,8},{2,11},{3,10},{4,13},{5,12},{6,15},{7,14},{8,1},{9,0},... | collective-permute-start | bytes 294920 | tf_op jit(solution)/shard_map/ppermute | solution.py:323

commit v3 on v2

--- a/solution.py
+++ b/solution.py
@@ -20,9 +20,12 @@
 FAR = (2, 4, 6)
 ROUNDS = ((0, 0), (-3, 0), (0, 1), (-3, 1), (2, 0), (-1, 1), (2, 1), (-1, 0))
 N_ROUNDS = len(ROUNDS)
-EARLY = 3
-FIRST = 5
-SMALL = 4
+PLACED = 13
+EARLY = 5
+NEXT = 2
+LAST = 1
+FIRST = 0
+SMALL = -1
 
 ANY = pl.BlockSpec(memory_space=pl.ANY)
 VMEM = pl.BlockSpec(memory_space=pltpu.VMEM)
@@ -99,16 +102,15 @@
     )(meta, cache)
 
 
-def place_kernel(offset, count, has_base, index_ref, *rest):
-    blocks = rest[:count]
-    out_ref, sem = rest[-3 if has_base == 2 else -2], rest[-1]
+def place_kernel(offset, count, n_out, index_ref, *rest):
+    blocks, out_ref, sem = rest[:count], rest[-1 - n_out], rest[-1]
     run_copies([
         pltpu.make_async_copy(blocks[i], out_ref.at[index_ref[offset + i]], sem.at[i])
         for i in range(count)
     ])
 
 
-def place(index, offset, blocks, rows, base=None, ready=None, carry=None):
+def place(index, offset, blocks, rows, base=None, ready=None, carry=()):
     count = len(blocks)
     out = [jax.ShapeDtypeStruct((rows,) + blocks[0].shape, blocks[0].dtype)]
     operands, aliases = [], {}
@@ -117,10 +119,10 @@
         operands.append(base)
     if ready is not None:
         operands.append(ready)
-    if carry is not None:
-        aliases[1 + count + len(operands)] = 1
-        operands.append(carry)
-        out.append(jax.ShapeDtypeStruct(carry.shape, carry.dtype))
+    for array in carry:
+        aliases[1 + count + len(operands)] = len(out)
+        operands.append(array)
+        out.append(jax.ShapeDtypeStruct(array.shape, array.dtype))
     return pl.pallas_call(
         functools.partial(place_kernel, offset, count, len(out)),
         out_shape=out,
@@ -227,60 +229,46 @@
     )(meta, order, kept, traded, res, weight)
 
 
-def near_kernel(meta_ref, *refs):
-    parts, outs = refs[:4], refs[4:]
-    mine = meta_ref[0] // 2 % 4
-    for step, out_ref in enumerate(outs):
-        far = mine ^ step
+def near_kernel(*refs):
+    parts, out_ref = refs[:4], refs[4]
+    for far in range(4):
         summed = parts[0][far].astype(jnp.float32)
         for part in parts[1:]:
             summed = summed + part[far].astype(jnp.float32)
-        out_ref[...] = summed
-
-
-def near_sum(meta, parts):
+        out_ref[far] = summed.astype(out_ref.dtype)
+
+
+def near_sum(parts):
     return pl.pallas_call(
         near_kernel,
-        out_shape=[jax.ShapeDtypeStruct(parts[0].shape[1:], jnp.float32)] * 4,
-        in_specs=[SMEM] + [VMEM] * 4,
-        out_specs=[VMEM] * 4,
+        out_shape=jax.ShapeDtypeStruct(parts[0].shape, parts[0].dtype),
+        in_specs=[VMEM] * 4,
+        out_specs=VMEM,
         compiler_params=pltpu.CompilerParams(vmem_limit_bytes=16 * MIB),
         name="near_sum",
-    )(meta, *parts)
-
-
-def far_kernel(*refs):
+    )(*parts)
+
+
+def far_kernel(meta_ref, *refs):
     parts, residual_ref, out_ref = refs[:4], refs[4], refs[5]
-    summed = (parts[0][...] + parts[1][...]) + (parts[2][...] + parts[3][...])
-    out_ref[...] = (residual_ref[...].astype(jnp.float32) + summed).astype(out_ref.dtype)
-
-
-def far_sum(parts, residual):
+    chunk = out_ref.shape[2]
+    for far in range(4):
+        one, two, three, four = [part[far].astype(jnp.float32) for part in parts]
+        summed = (one + two) + (three + four)
+        columns = pl.ds(pl.multiple_of(owner(meta_ref[0], far, 0) * chunk, chunk), chunk)
+        own = residual_ref[:, columns].astype(jnp.float32)
+        out_ref[far] = (own + summed).astype(out_ref.dtype)
+
+
+def far_sum(meta, parts, residual):
     return pl.pallas_call(
         far_kernel,
-        out_shape=jax.ShapeDtypeStruct(residual.shape, residual.dtype),
-        in_specs=[VMEM] * 5,
+        out_shape=jax.ShapeDtypeStruct(parts[0].shape, residual.dtype),
+        in_specs=[SMEM] + [VMEM] * 5,
         out_specs=VMEM,
         compiler_params=pltpu.CompilerParams(vmem_limit_bytes=16 * MIB),
         name="far_sum",
-    )(*parts, residual)
-
-
-def stack_kernel(meta_ref, *refs):
-    parts, out_ref = refs[:4], refs[4]
-    for step, part in enumerate(parts):
-        out_ref[meta_ref[0] // 2 % 4 ^ step] = part[...]
-
-
-def stack(meta, parts):
-    return pl.pallas_call(
-        stack_kernel,
-        out_shape=jax.ShapeDtypeStruct((4,) + parts[0].shape, parts[0].dtype),
-        in_specs=[SMEM] + [VMEM] * 4,
-        out_specs=VMEM,
-        compiler_params=pltpu.CompilerParams(vmem_limit_bytes=16 * MIB),
-        name="stack",
-    )(meta, *parts)
+    )(meta, *parts, residual)
 
 
 def join_kernel(meta_ref, *refs):
@@ -332,17 +320,14 @@
     chunk = out_weight.shape[1] // tp_count
     meta = rank.reshape(1).astype(jnp.int32)
 
+
+    def send(step, block):
+        return hop(block, inst_count, tp_count, lambda t: round_target(t, step))
+
     handed = hop(lengths[0], inst_count, tp_count, lambda t: t)
     other_q = swap(queries[0], tp_count)
     sent = list(extract(after(meta, [handed, other_q]), source_cache[0, 0]))
-
-    def send(step, block):
-        return hop(block, inst_count, tp_count, lambda t: round_target(t, step))
-
-    arrived = []
-    for step in range(N_ROUNDS):
-        arrived.append(send(step, sent[step]))
-    passed = [swap(arrived[k], tp_count) for k in range(EARLY)]
+    arrived = [send(step, sent[step]) for step in range(N_ROUNDS)]
 
     index, order, select = tables(tp_count, rows)
     index = lax.dynamic_index_in_dim(jnp.asarray(index), rank, keepdims=False)
@@ -355,38 +340,29 @@
     hit = mine[:, None] == jnp.arange(rows, dtype=jnp.int32)[None, :]
     adopt_len = jnp.sum(jnp.where(hit, handed[None, :], 0), axis=1)
     (res,) = attend(N_ROUNDS, 2, lengths[0, adopt:], table, [resident_cache[0, 0]])
-    own_residual = lax.dynamic_slice_in_dim(residual[0], rank * chunk, chunk, axis=1)
-
-    table = after(table, [*passed, res, own_residual])
+
+    passed = [swap(block, tp_count) for block in arrived[:EARLY]]
+    table = after(table, [*passed, res])
     kept, traded = attend(0, GROUP, adopt_len, table, arrived)
 
-    adopted, done = None, 0
-    def beside(ready, count):
-        nonlocal adopted, done
-        blocks = (arrived + passed)[done : done + count]
-        carry = arrived[len(passed)]
-        adopted, carry = place(index, done, blocks, adopt, adopted, ready, carry)
-        done += count
-        passed.append(swap(carry, tp_count))
+    def pass_on(ready, count):
+        for _ in range(count):
+            block = after(arrived[len(passed)], [ready])
+            passed.append(swap(block, tp_count))
 
     traded = swap(traded, tp_count)
-    beside(kept, 2)
     parts = project(meta, order, kept, traded, res, out_weight, tp_count)
-    first = parts[0]
-    parts = [first] + [swap(part, tp_count, bits) for part, bits in zip(parts[1:], NEAR)]
-    beside(first, 3)
-    parts = near_sum(meta, [after(parts[0], passed[:-1])] + parts[1:])
-    first = parts[0]
-    parts = [first] + [swap(part, tp_count, bits) for part, bits in zip(parts[1:], FAR)]
-    beside(first, 3)
-    mixed = far_sum([after(parts[0], passed[:-1])] + parts[1:], own_residual)
-    parts = [mixed] + [swap(mixed, tp_count, bits) for bits in FAR]
-    beside(mixed, 3)
-    mixed = stack(meta, [after(mixed, passed[:-1])] + parts[1:])
+    pass_on(parts[0], 1)
+    parts = [parts[0]] + [swap(part, tp_count, bits) for part, bits in zip(parts[1:], NEAR)]
+    part = near_sum([after(parts[0], passed[:-1])] + parts[1:])
+    pass_on(part, 1)
+    parts = [part] + [swap(part, tp_count, bits) for bits in FAR]
+    mixed = far_sum(meta, [after(part, passed[:-1])] + parts[1:], residual[0])
+    pass_on(mixed, 1)
     parts = [mixed] + [swap(mixed, tp_count, bits) for bits in NEAR]
-    beside(mixed, 3)
+    (adopted,) = place(index, 0, (arrived + passed)[:PLACED], adopt, None, mixed)
     mixed = join(meta, parts, tp_count)
-    (adopted,) = place(index, done, (arrived + passed)[done:], adopt, adopted)
+    (adopted,) = place(index, PLACED, (arrived + passed)[PLACED:], adopt, adopted)
     return (mixed, adopted[None, None])
 
 

time: 133 us -> 125 us (0.940)
  starting transfers between devices: 68.3 us -> 59.2 us
  waiting for transfers between devices: 42.5 us -> 49.1 us
  Pallas kernels: 15.1 us -> 10.5 us
    ppermute x22 -> x19, waiting for transfers between devices: 25.5 us -> 33.7 us  [swap(): return lax.ppermute(value, 'tp', [(t, t ^ bits) for t in range(tp_count)])]
    ppermute x22 -> x19, starting transfers between devices: 33.3 us -> 27.5 us  [swap(): return lax.ppermute(value, 'tp', [(t, t ^ bits) for t in range(tp_count)])]
    pallas_call x6 -> x2, Pallas kernels: 8.51 us -> 3.83 us  [place(): pl.pallas_call(functools.partial(place_kernel, offset, count, len(out)),...]
    ppermute x9, starting transfers between devices: 35 us -> 31.8 us  [hop(): return lax.ppermute(value, ('inst', 'tp'), pairs)]
    ppermute x9, waiting for transfers between devices: 17 us -> 15.3 us  [hop(): return lax.ppermute(value, ('inst', 'tp'), pairs)]
  transfers between devices with their start and end apart: 31 -> 28, of which waited for: 12 -> 12; matrix products, arithmetic and copies ran while one was open for 3% -> 3% of each run, Pallas kernels for 7% -> 4%
where the time goes in v3:
time: 125 us; the launch traced here: 124 us
  starting transfers between devices  59.2 us (47%)
  waiting for transfers between devices  49.1 us (39%)
  Pallas kernels  10.5 us (8%)
  local copies, waits for them, and re-layouts  3.73 us (3%)
    ppermute x19, waiting for transfers between devices, swap(): return lax.ppermute(value, 'tp', [(t, t ^ bits) for t in range(tp_count)])  33.7 us
    ppermute x9, starting transfers between devices, hop(): return lax.ppermute(value, ('inst', 'tp'), pairs)  31.8 us
    ppermute x19, starting transfers between devices, swap(): return lax.ppermute(value, 'tp', [(t, t ^ bits) for t in range(tp_count)])  27.5 us
    ppermute x9, waiting for transfers between devices, hop(): return lax.ppermute(value, ('inst', 'tp'), pairs)  15.3 us
    pallas_call x2, Pallas kernels, place(): pl.pallas_call(functools.partial(place_kernel, offset, count, len(out)),...  3.83 us
  transfers between devices with their start and end apart: 28, of which 12 were waited for; matrix products, arithmetic and copies ran while one was open for 3% of the time, Pallas kernels for 4%

profile of v3, /device:TPU:8, one launch (start us, length us, event | category | flops | bytes accessed | tf_op | source)
XLA Modules:
  0.0 124.4 jit_solution(4644121647100084631)
XLA Ops:
  0.6 2.0 %collective-permute-start.1 = (bf16[24,256]{1,0:T(8,128)(2,1)}, bf16[24,256]{1,0:T(8,128)(2,1)S(1)}, u32[]{:S(2)}, u32[]{:S(2)}) collective-permute-start(bf16[24,256]{1,0:T(8,128)(2,1)} %bitcast.29), channel_id=1, source_target_pairs={{0,1},{1,0},{2,3},{3,2},{4,5},{5,4},{6,7},{7,6},{8,9},{9,8},{10,11... | collective-permute-start | bytes 36872 | tf_op jit(solution)/shard_map/ppermute | solution.py:311
  2.6 2.3 %collective-permute-start = (s32[24]{0:T(128)}, s32[24]{0:T(128)S(1)}, u32[]{:S(2)}, u32[]{:S(2)}) collective-permute-start(s32[24]{0:T(128)} %bitcast.31), channel_id=1, source_target_pairs={{0,128},{1,129},{2,130},{3,131},{4,132},{5,133},{6,134},{7,135},{8... | collective-permute-start | bytes 296 | tf_op jit(solution)/shard_map/ppermute | solution.py:303
  4.9 2.9 %collective-permute-done = s32[24]{0:T(128)S(1)} collective-permute-done((s32[24]{0:T(128)}, s32[24]{0:T(128)S(1)}, u32[]{:S(2)}, u32[]{:S(2)}) %collective-permute-start) | collective-permute-done | bytes 128 | tf_op jit(solution)/shard_map/ppermute | solution.py:303
  7.8 2.4 %extract.1 = (bf16[2,512,128]{2,1,0:T(8,128)(2,1)}, bf16[2,512,128]{2,1,0:T(8,128)(2,1)}, bf16[2,512,128]{2,1,0:T(8,128)(2,1)}, bf16[2,512,128]{2,1,0:T(8,128)(2...) custom-call(s32[1]{0:T(128)} %bitcast.meta_ref, ...), custom_call_target="tpu_custom_call" | custom-call | tf_op jit(solution)/shard_map/extract/pallas_call | solution.py:90
  10.2 5.1 %collective-permute-start.10 = (bf16[2,512,128]{2,1,0:T(8,128)(2,1)}, bf16[2,512,128]{2,1,0:T(8,128)(2,1)S(1)}, u32[]{:S(2)}, u32[]{:S(2)}) collective-permute-start(bf16[2,512,128]{2,1,0:T(8,128)(2,1)} %get-tuple-element.28), channel_id=1, source_target_pairs={{0,130},{1,135},{2,132},{3,129},{4,134},{5,131},{6,128},{7,133},{8... | collective-permute-start | bytes 786440 | tf_op jit(solution)/shard_map/ppermute | solution.py:303
  15.3 1.2 collective-permute-start.2
  16.6 3.9 %collective-permute-start.4 = (bf16[2,512,128]{2,1,0:T(8,128)(2,1)}, bf16[2,512,128]{2,1,0:T(8,128)(2,1)S(1)}, u32[]{:S(2)}, u32[]{:S(2)}) collective-permute-start(bf16[2,512,128]{2,1,0:T(8,128)(2,1)} %get-tuple-element.25), channel_id=1, source_target_pairs={{0,133},{1,132},{2,135},{3,134},{4,129},{5,128},{6,131},{7,130},{8... | collective-permute-start | bytes 786440 | tf_op jit(solution)/shard_map/ppermute | solution.py:303
  20.5 0.7 slice_bitcast_fusion.len_ref
  21.2 3.7 %collective-permute-start.6 = (bf16[2,512,128]{2,1,0:T(8,128)(2,1)}, bf16[2,512,128]{2,1,0:T(8,128)(2,1)S(1)}, u32[]{:S(2)}, u32[]{:S(2)}) collective-permute-start(bf16[2,512,128]{2,1,0:T(8,128)(2,1)} %get-tuple-element.26), channel_id=1, source_target_pairs={{0,136},{1,137},{2,138},{3,139},{4,140},{5,141},{6,142},{7,143},{8... | collective-permute-start | bytes 786440 | tf_op jit(solution)/shard_map/ppermute | solution.py:303
  24.9 4.5 %collective-permute-start.8 = (bf16[2,512,128]{2,1,0:T(8,128)(2,1)}, bf16[2,512,128]{2,1,0:T(8,128)(2,1)S(1)}, u32[]{:S(2)}, u32[]{:S(2)}) collective-permute-start(bf16[2,512,128]{2,1,0:T(8,128)(2,1)} %get-tuple-element.27), channel_id=1, source_target_pairs={{0,141},{1,140},{2,143},{3,142},{4,137},{5,136},{6,139},{7,138},{8... | collective-permute-start | bytes 786440 | tf_op jit(solution)/shard_map/ppermute | solution.py:303
  29.4 3.1 %collective-permute-start.11 = (bf16[2,512,128]{2,1,0:T(8,128)(2,1)S(1)}, bf16[2,512,128]{2,1,0:T(8,128)(2,1)S(1)}, u32[]{:S(2)}, u32[]{:S(2)}) collective-permute-start(bf16[2,512,128]{2,1,0:T(8,128)(2,1)S(1)} %collective-permute-done.10.rest_4_), channel_id=1, source_target_pairs={{0,1},{1,0},{2,3},{3,2},{4,5},{5,4},{6,7},{7,6},{8,9},{9,8},{10,11... | collective-permute-start | bytes 786440 | tf_op jit(solution)/shard_map/ppermute | solution.py:311
  32.6 12.4 %collective-permute-done.2.rest_0_ = bf16[2,512,128]{2,1,0:T(8,128)(2,1)S(1)} collective-permute-done((bf16[2,512,128]{2,1,0:T(8,128)(2,1)}, bf16[2,512,128]{2,1,0:T(8,128)(2,1)S(1)}, u32[]{:S(2)}, u32[]{:S(2)}) %collective-permute-start.2) | collective-permute-done | bytes 262176 | tf_op jit(solution)/shard_map/ppermute | solution.py:303
  45.0 2.0 %collective-permute-start.5 = (bf16[2,512,128]{2,1,0:T(8,128)(2,1)S(1)}, bf16[2,512,128]{2,1,0:T(8,128)(2,1)S(1)}, u32[]{:S(2)}, u32[]{:S(2)}) collective-permute-start(bf16[2,512,128]{2,1,0:T(8,128)(2,1)S(1)} %collective-permute-done.4.rest_1_), channel_id=1, source_target_pairs={{0,1},{1,0},{2,3},{3,2},{4,5},{5,4},{6,7},{7,6},{8,9},{9,8},{10,11... | collective-permute-start | bytes 786440 | tf_op jit(solution)/shard_map/ppermute | solution.py:311
  47.0 0.7 fusion.10
  47.7 7.2 %collective-permute-start.12 = (bf16[2,512,128]{2,1,0:T(8,128)(2,1)}, bf16[2,512,128]{2,1,0:T(8,128)(2,1)S(1)}, u32[]{:S(2)}, u32[]{:S(2)}) collective-permute-start(bf16[2,512,128]{2,1,0:T(8,128)(2,1)} %get-tuple-element.30), channel_id=1, source_target_pairs={{0,143},{1,138},{2,137},{3,140},{4,139},{5,142},{6,141},{7,136},{8... | collective-permute-start | bytes 786440 | tf_op jit(solution)/shard_map/ppermute | solution.py:303
  54.9 3.8 %collective-permute-start.14 = (bf16[2,512,128]{2,1,0:T(8,128)(2,1)}, bf16[2,512,128]{2,1,0:T(8,128)(2,1)S(1)}, u32[]{:S(2)}, u32[]{:S(2)}) collective-permute-start(bf16[2,512,128]{2,1,0:T(8,128)(2,1)} %get-tuple-element.32), channel_id=1, source_target_pairs={{0,135},{1,130},{2,129},{3,132},{4,131},{5,134},{6,133},{7,128},{8... | collective-permute-start | bytes 786440 | tf_op jit(solution)/shard_map/ppermute | solution.py:303
  58.8 0.5 collective-permute-start.7
  59.3 0.5 collective-permute-done.5.rest_9_
  59.8 1.0 collective-permute-start.9
  61.0 0.9 fusion.rows_ref
  61.9 1.6 %copy-done.2 = bf16[1,1,8,2,512,128]{5,4,3,2,1,0:T(8,128)(2,1)S(1)} copy-done((bf16[1,1,8,2,512,128]{5,4,3,2,1,0:T(8,128)(2,1)S(1)}, bf16[1,1,8,2,512,128]{5,4,3,2,1,0:T(8,128)(2,1)}, u32[]{:S(2)}) %copy-start.2) | copy-done | bytes 2097176
  63.5 1.2 attend.2.res_ref
  64.7 6.4 %collective-permute-done.7.rest_10_ = bf16[2,512,128]{2,1,0:T(8,128)(2,1)S(1)} collective-permute-done((bf16[2,512,128]{2,1,0:T(8,128)(2,1)S(1)}, bf16[2,512,128]{2,1,0:T(8,128)(2,1)S(1)}, u32[]{:S(2)}, u32[]{:S(2)}) %collective-permute-start.7) | collective-permute-done | bytes 262176 | tf_op jit(solution)/shard_map/ppermute | solution.py:311
  71.1 4.7 %collective-permute-done.9.rest_11_ = bf16[2,512,128]{2,1,0:T(8,128)(2,1)S(1)} collective-permute-done((bf16[2,512,128]{2,1,0:T(8,128)(2,1)S(1)}, bf16[2,512,128]{2,1,0:T(8,128)(2,1)S(1)}, u32[]{:S(2)}, u32[]{:S(2)}) %collective-permute-start.9) | collective-permute-done | bytes 262176 | tf_op jit(solution)/shard_map/ppermute | solution.py:311
  75.8 1.2 attend.3
  77.0 0.4 collective-permute-start.15
  77.3 0.7 dynamic-slice_bitcast_fusion.place_ref
  78.0 2.7 %collective-permute-done.15.traded_ref = f32[8,256]{1,0:T(8,128)S(1)} collective-permute-done((f32[8,256]{1,0:T(8,128)S(1)}, f32[8,256]{1,0:T(8,128)S(1)}, u32[]{:S(2)}, u32[]{:S(2)}) %collective-permute-start.15) | collective-permute-done | bytes 8224 | tf_op jit(solution)/shard_map/ppermute | solution.py:311
  80.7 0.9 project.1
  81.6 0.4 collective-permute-start.19
  82.0 1.7 %collective-permute-start.16 = (bf16[4,24,512]{2,1,0:T(8,128)(2,1)S(1)}, bf16[4,24,512]{2,1,0:T(8,128)(2,1)S(1)}, u32[]{:S(2)}, u32[]{:S(2)}) collective-permute-start(bf16[4,24,512]{2,1,0:T(8,128)(2,1)S(1)} %get-tuple-element.37), channel_id=1, source_target_pairs={{0,1},{1,0},{2,3},{3,2},{4,5},{5,4},{6,7},{7,6},{8,9},{9,8},{10,11... | collective-permute-start | bytes 294920 | tf_op jit(solution)/shard_map/ppermute | solution.py:311
  83.7 3.0 %collective-permute-start.17 = (bf16[4,24,512]{2,1,0:T(8,128)(2,1)S(1)}, bf16[4,24,512]{2,1,0:T(8,128)(2,1)S(1)}, u32[]{:S(2)}, u32[]{:S(2)}) collective-permute-start(bf16[4,24,512]{2,1,0:T(8,128)(2,1)S(1)} %get-tuple-element.38), channel_id=1, source_target_pairs={{0,8},{1,9},{2,10},{3,11},{4,12},{5,13},{6,14},{7,15},{8,0},{9,1},... | collective-permute-start | bytes 294920 | tf_op jit(solution)/shard_map/ppermute | solution.py:311
  87.0 4.1 %collective-permute-done.16.refs_1_ = bf16[4,24,512]{2,1,0:T(8,128)(2,1)S(1)} collective-permute-done((bf16[4,24,512]{2,1,0:T(8,128)(2,1)S(1)}, bf16[4,24,512]{2,1,0:T(8,128)(2,1)S(1)}, u32[]{:S(2)}, u32[]{:S(2)}) %collective-permute-start.16) | collective-permute-done | bytes 98336 | tf_op jit(solution)/shard_map/ppermute | solution.py:311
  91.1 3.5 %collective-permute-done.18.refs_3_ = bf16[4,24,512]{2,1,0:T(8,128)(2,1)S(1)} collective-permute-done((bf16[4,24,512]{2,1,0:T(8,128)(2,1)S(1)}, bf16[4,24,512]{2,1,0:T(8,128)(2,1)S(1)}, u32[]{:S(2)}, u32[]{:S(2)}) %collective-permute-start.18) | collective-permute-done | bytes 98336 | tf_op jit(solution)/shard_map/ppermute | solution.py:311
  94.7 0.8 collective-permute-start.20
  95.4 5.4 %collective-permute-start.21 = (bf16[4,24,512]{2,1,0:T(8,128)(2,1)S(1)}, bf16[4,24,512]{2,1,0:T(8,128)(2,1)S(1)}, u32[]{:S(2)}, u32[]{:S(2)}) collective-permute-start(bf16[4,24,512]{2,1,0:T(8,128)(2,1)S(1)} %near_sum.1.refs_0_), channel_id=1, source_target_pairs={{0,4},{1,5},{2,6},{3,7},{4,0},{5,1},{6,2},{7,3},{8,12},{9,13},{10,... | collective-permute-start | bytes 294920 | tf_op jit(solution)/shard_map/ppermute | solution.py:311
  100.9 0.4 collective-permute-start.22
  101.2 1.4 %collective-permute-start.26 = (bf16[2,512,128]{2,1,0:T(8,128)(2,1)S(1)}, bf16[2,512,128]{2,1,0:T(8,128)(2,1)S(1)}, u32[]{:S(2)}, u32[]{:S(2)}) collective-permute-start(bf16[2,512,128]{2,1,0:T(8,128)(2,1)S(1)} %collective-permute-done.13.rest_6_), channel_id=1, source_target_pairs={{0,1},{1,0},{2,3},{3,2},{4,5},{5,4},{6,7},{7,6},{8,9},{9,8},{10,11... | collective-permute-start | bytes 786440 | tf_op jit(solution)/shard_map/ppermute | solution.py:311
  102.6 0.9 collective-permute-done.20.refs_1_
  103.5 7.1 %collective-permute-done.21.refs_2_ = bf16[4,24,512]{2,1,0:T(8,128)(2,1)S(1)} collective-permute-done((bf16[4,24,512]{2,1,0:T(8,128)(2,1)S(1)}, bf16[4,24,512]{2,1,0:T(8,128)(2,1)S(1)}, u32[]{:S(2)}, u32[]{:S(2)}) %collective-permute-start.21) | collective-permute-done | bytes 98336 | tf_op jit(solution)/shard_map/ppermute | solution.py:311
  110.8 2.0 %collective-permute-start.23 = (bf16[4,24,512]{2,1,0:T(8,128)(2,1)S(1)}, bf16[4,24,512]{2,1,0:T(8,128)(2,1)S(1)}, u32[]{:S(2)}, u32[]{:S(2)}) collective-permute-start(bf16[4,24,512]{2,1,0:T(8,128)(2,1)S(1)} %far_sum.1.refs_0_.rest_13_), channel_id=1, source_target_pairs={{0,1},{1,0},{2,3},{3,2},{4,5},{5,4},{6,7},{7,6},{8,9},{9,8},{10,11... | collective-permute-start | bytes 294920 | tf_op jit(solution)/shard_map/ppermute | solution.py:311
  112.8 0.5 collective-permute-start.24
  113.3 2.6 %collective-permute-start.25 = (bf16[4,24,512]{2,1,0:T(8,128)(2,1)S(1)}, bf16[4,24,512]{2,1,0:T(8,128)(2,1)S(1)}, u32[]{:S(2)}, u32[]{:S(2)}) collective-permute-start(bf16[4,24,512]{2,1,0:T(8,128)(2,1)S(1)} %far_sum.1.refs_0_.rest_13_), channel_id=1, source_target_pairs={{0,9},{1,8},{2,11},{3,10},{4,13},{5,12},{6,15},{7,14},{8,1},{9,0},... | collective-permute-start | bytes 294920 | tf_op jit(solution)/shard_map/ppermute | solution.py:311
  115.8 2.4 %place.2.rest_3_ = bf16[16,2,512,128]{3,2,1,0:T(8,128)(2,1)} custom-call(s32[16]{0:T(128)S(1)} %get-tuple-element.44.index_ref, bf16[2,512,128]{2,1,0:T(8,128)(2,1)S(1)} %collective-permute-done.2.rest_0_, bf16[2,512,128]{2,1,0:T(8,128)(2,1)S(1)} %collective-permute-done.4.rest_1_, bf16[2,512,128]{2,1,0:T(8,128)(2,1)S(1)} %collective-permute-done.6.rest_2_, ...), custom_call_target="tpu_custom_call" | custom-call | tf_op jit(solution)/shard_map/place/pallas_call | solution.py:126
  118.2 2.7 %collective-permute-done.23.refs_1_ = bf16[4,24,512]{2,1,0:T(8,128)(2,1)S(1)} collective-permute-done((bf16[4,24,512]{2,1,0:T(8,128)(2,1)S(1)}, bf16[4,24,512]{2,1,0:T(8,128)(2,1)S(1)}, u32[]{:S(2)}, u32[]{:S(2)}) %collective-permute-start.23) | collective-permute-done | bytes 98336 | tf_op jit(solution)/shard_map/ppermute | solution.py:311
  121.0 1.1 collective-permute-done.25.refs_3_
  122.0 0.8 join.1
  122.8 1.4 %place.3 = bf16[16,2,512,128]{3,2,1,0:T(8,128)(2,1)} custom-call(s32[16]{0:T(128)S(1)} %get-tuple-element.44.index_ref, bf16[2,512,128]{2,1,0:T(8,128)(2,1)S(1)} %collective-permute-done.19.rest_0_, bf16[2,512,128]{2,1,0:T(8,128)(2,1)S(1)} %collective-permute-done.26.rest_1_, ...), custom_call_target="tpu_custom_call", output_to_operand_aliasing={{}: (4, {})} | custom-call | tf_op jit(solution)/shard_map/place/pallas_call | solution.py:126
  (33 shorter events, 0.7 us)
Async XLA Ops:
  0.6 60.2 %copy-start = (bf16[1,24,2,1024]{3,2,1,0:T(2,128)(2,1)S(1)}, bf16[1,24,2,1024]{3,2,1,0:T(2,128)(2,1)}, u32[]{:S(2)}) copy-start(bf16[1,24,2,1024]{3,2,1,0:T(2,128)(2,1)} %param.12) | copy-start | bytes 294916
  0.6 7.2 %collective-permute-start.1 = (bf16[24,256]{1,0:T(8,128)(2,1)}, bf16[24,256]{1,0:T(8,128)(2,1)S(1)}, u32[]{:S(2)}, u32[]{:S(2)}) collective-permute-start(bf16[24,256]{1,0:T(8,128)(2,1)} %bitcast.29), channel_id=1, source_target_pairs={{0,1},{1,0},{2,3},{3,2},{4,5},{5,4},{6,7},{7,6},{8,9},{9,8},{10,11... | collective-permute-start | bytes 36872 | tf_op jit(solution)/shard_map/ppermute | solution.py:311
  2.6 5.2 %collective-permute-start = (s32[24]{0:T(128)}, s32[24]{0:T(128)S(1)}, u32[]{:S(2)}, u32[]{:S(2)}) collective-permute-start(s32[24]{0:T(128)} %bitcast.31), channel_id=1, source_target_pairs={{0,128},{1,129},{2,130},{3,131},{4,132},{5,133},{6,134},{7,135},{8... | collective-permute-start | bytes 296 | tf_op jit(solution)/shard_map/ppermute | solution.py:303
  10.2 19.2 %collective-permute-start.10 = (bf16[2,512,128]{2,1,0:T(8,128)(2,1)}, bf16[2,512,128]{2,1,0:T(8,128)(2,1)S(1)}, u32[]{:S(2)}, u32[]{:S(2)}) collective-permute-start(bf16[2,512,128]{2,1,0:T(8,128)(2,1)} %get-tuple-element.28), channel_id=1, source_target_pairs={{0,130},{1,135},{2,132},{3,129},{4,134},{5,131},{6,128},{7,133},{8... | collective-permute-start | bytes 786440 | tf_op jit(solution)/shard_map/ppermute | solution.py:303
  15.3 29.7 %collective-permute-start.2 = (bf16[2,512,128]{2,1,0:T(8,128)(2,1)}, bf16[2,512,128]{2,1,0:T(8,128)(2,1)S(1)}, u32[]{:S(2)}, u32[]{:S(2)}) collective-permute-start(bf16[2,512,128]{2,1,0:T(8,128)(2,1)} %get-tuple-element.24), channel_id=1, source_target_pairs={{0,128},{1,129},{2,130},{3,131},{4,132},{5,133},{6,134},{7,135},{8... | collective-permute-start | bytes 786440 | tf_op jit(solution)/shard_map/ppermute | solution.py:303
  16.6 28.5 %collective-permute-start.4 = (bf16[2,512,128]{2,1,0:T(8,128)(2,1)}, bf16[2,512,128]{2,1,0:T(8,128)(2,1)S(1)}, u32[]{:S(2)}, u32[]{:S(2)}) collective-permute-start(bf16[2,512,128]{2,1,0:T(8,128)(2,1)} %get-tuple-element.25), channel_id=1, source_target_pairs={{0,133},{1,132},{2,135},{3,134},{4,129},{5,128},{6,131},{7,130},{8... | collective-permute-start | bytes 786440 | tf_op jit(solution)/shard_map/ppermute | solution.py:303
  21.2 26.5 %collective-permute-start.6 = (bf16[2,512,128]{2,1,0:T(8,128)(2,1)}, bf16[2,512,128]{2,1,0:T(8,128)(2,1)S(1)}, u32[]{:S(2)}, u32[]{:S(2)}) collective-permute-start(bf16[2,512,128]{2,1,0:T(8,128)(2,1)} %get-tuple-element.26), channel_id=1, source_target_pairs={{0,136},{1,137},{2,138},{3,139},{4,140},{5,141},{6,142},{7,143},{8... | collective-permute-start | bytes 786440 | tf_op jit(solution)/shard_map/ppermute | solution.py:303
  24.9 30.0 %collective-permute-start.8 = (bf16[2,512,128]{2,1,0:T(8,128)(2,1)}, bf16[2,512,128]{2,1,0:T(8,128)(2,1)S(1)}, u32[]{:S(2)}, u32[]{:S(2)}) collective-permute-start(bf16[2,512,128]{2,1,0:T(8,128)(2,1)} %get-tuple-element.27), channel_id=1, source_target_pairs={{0,141},{1,140},{2,143},{3,142},{4,137},{5,136},{6,139},{7,138},{8... | collective-permute-start | bytes 786440 | tf_op jit(solution)/shard_map/ppermute | solution.py:303
  29.4 25.5 %collective-permute-start.11 = (bf16[2,512,128]{2,1,0:T(8,128)(2,1)S(1)}, bf16[2,512,128]{2,1,0:T(8,128)(2,1)S(1)}, u32[]{:S(2)}, u32[]{:S(2)}) collective-permute-start(bf16[2,512,128]{2,1,0:T(8,128)(2,1)S(1)} %collective-permute-done.10.rest_4_), channel_id=1, source_target_pairs={{0,1},{1,0},{2,3},{3,2},{4,5},{5,4},{6,7},{7,6},{8,9},{9,8},{10,11... | collective-permute-start | bytes 786440 | tf_op jit(solution)/shard_map/ppermute | solution.py:311
  45.0 13.8 %collective-permute-start.3 = (bf16[2,512,128]{2,1,0:T(8,128)(2,1)S(1)}, bf16[2,512,128]{2,1,0:T(8,128)(2,1)S(1)}, u32[]{:S(2)}, u32[]{:S(2)}) collective-permute-start(bf16[2,512,128]{2,1,0:T(8,128)(2,1)S(1)} %collective-permute-done.2.rest_0_), channel_id=1, source_target_pairs={{0,1},{1,0},{2,3},{3,2},{4,5},{5,4},{6,7},{7,6},{8,9},{9,8},{10,11... | collective-permute-start | bytes 786440 | tf_op jit(solution)/shard_map/ppermute | solution.py:311
  45.0 14.8 %collective-permute-start.5 = (bf16[2,512,128]{2,1,0:T(8,128)(2,1)S(1)}, bf16[2,512,128]{2,1,0:T(8,128)(2,1)S(1)}, u32[]{:S(2)}, u32[]{:S(2)}) collective-permute-start(bf16[2,512,128]{2,1,0:T(8,128)(2,1)S(1)} %collective-permute-done.4.rest_1_), channel_id=1, source_target_pairs={{0,1},{1,0},{2,3},{3,2},{4,5},{5,4},{6,7},{7,6},{8,9},{9,8},{10,11... | collective-permute-start | bytes 786440 | tf_op jit(solution)/shard_map/ppermute | solution.py:311
  47.7 33.0 %copy-start.1 = (bf16[256,8192]{1,0:T(8,128)(2,1)S(1)}, bf16[256,8192]{1,0:T(8,128)(2,1)}, u32[]{:S(2)}) copy-start(bf16[256,8192]{1,0:T(8,128)(2,1)} %weight_ref.1) | copy-start | bytes 12582916
  47.7 28.0 %collective-permute-start.12 = (bf16[2,512,128]{2,1,0:T(8,128)(2,1)}, bf16[2,512,128]{2,1,0:T(8,128)(2,1)S(1)}, u32[]{:S(2)}, u32[]{:S(2)}) collective-permute-start(bf16[2,512,128]{2,1,0:T(8,128)(2,1)} %get-tuple-element.30), channel_id=1, source_target_pairs={{0,143},{1,138},{2,137},{3,140},{4,139},{5,142},{6,141},{7,136},{8... | collective-permute-start | bytes 786440 | tf_op jit(solution)/shard_map/ppermute | solution.py:303
  54.9 20.8 %collective-permute-start.13 = (bf16[2,512,128]{2,1,0:T(8,128)(2,1)}, bf16[2,512,128]{2,1,0:T(8,128)(2,1)S(1)}, u32[]{:S(2)}, u32[]{:S(2)}) collective-permute-start(bf16[2,512,128]{2,1,0:T(8,128)(2,1)} %get-tuple-element.31), channel_id=1, source_target_pairs={{0,138},{1,143},{2,140},{3,137},{4,142},{5,139},{6,136},{7,141},{8... | collective-permute-start | bytes 786440 | tf_op jit(solution)/shard_map/ppermute | solution.py:303
  54.9 20.8 %collective-permute-start.14 = (bf16[2,512,128]{2,1,0:T(8,128)(2,1)}, bf16[2,512,128]{2,1,0:T(8,128)(2,1)S(1)}, u32[]{:S(2)}, u32[]{:S(2)}) collective-permute-start(bf16[2,512,128]{2,1,0:T(8,128)(2,1)} %get-tuple-element.32), channel_id=1, source_target_pairs={{0,135},{1,130},{2,129},{3,132},{4,131},{5,134},{6,133},{7,128},{8... | collective-permute-start | bytes 786440 | tf_op jit(solution)/shard_map/ppermute | solution.py:303
  58.8 12.3 %collective-permute-start.7 = (bf16[2,512,128]{2,1,0:T(8,128)(2,1)S(1)}, bf16[2,512,128]{2,1,0:T(8,128)(2,1)S(1)}, u32[]{:S(2)}, u32[]{:S(2)}) collective-permute-start(bf16[2,512,128]{2,1,0:T(8,128)(2,1)S(1)} %collective-permute-done.6.rest_2_), channel_id=1, source_target_pairs={{0,1},{1,0},{2,3},{3,2},{4,5},{5,4},{6,7},{7,6},{8,9},{9,8},{10,11... | collective-permute-start | bytes 786440 | tf_op jit(solution)/shard_map/ppermute | solution.py:311
  59.8 16.0 %collective-permute-start.9 = (bf16[2,512,128]{2,1,0:T(8,128)(2,1)S(1)}, bf16[2,512,128]{2,1,0:T(8,128)(2,1)S(1)}, u32[]{:S(2)}, u32[]{:S(2)}) collective-permute-start(bf16[2,512,128]{2,1,0:T(8,128)(2,1)S(1)} %collective-permute-done.8.rest_3_), channel_id=1, source_target_pairs={{0,1},{1,0},{2,3},{3,2},{4,5},{5,4},{6,7},{7,6},{8,9},{9,8},{10,11... | collective-permute-start | bytes 786440 | tf_op jit(solution)/shard_map/ppermute | solution.py:311
  61.9 1.6 %copy-start.2 = (bf16[1,1,8,2,512,128]{5,4,3,2,1,0:T(8,128)(2,1)S(1)}, bf16[1,1,8,2,512,128]{5,4,3,2,1,0:T(8,128)(2,1)}, u32[]{:S(2)}) copy-start(bf16[1,1,8,2,512,128]{5,4,3,2,1,0:T(8,128)(2,1)} %param.11) | copy-start | bytes 6291460
  63.5 47.1 %copy-start.3 = (bf16[1,24,8192]{2,1,0:T(8,128)(2,1)S(1)}, bf16[1,24,8192]{2,1,0:T(8,128)(2,1)}, u32[]{:S(2)}) copy-start(bf16[1,24,8192]{2,1,0:T(8,128)(2,1)} %param.14) | copy-start | bytes 1179652
  77.0 3.7 %collective-permute-start.15 = (f32[8,256]{1,0:T(8,128)S(1)}, f32[8,256]{1,0:T(8,128)S(1)}, u32[]{:S(2)}, u32[]{:S(2)}) collective-permute-start(f32[8,256]{1,0:T(8,128)S(1)} %get-tuple-element.34), channel_id=1, source_target_pairs={{0,1},{1,0},{2,3},{3,2},{4,5},{5,4},{6,7},{7,6},{8,9},{9,8},{10,11... | collective-permute-start | bytes 24584 | tf_op jit(solution)/shard_map/ppermute | solution.py:311
  81.6 21.0 %collective-permute-start.19 = (bf16[2,512,128]{2,1,0:T(8,128)(2,1)S(1)}, bf16[2,512,128]{2,1,0:T(8,128)(2,1)S(1)}, u32[]{:S(2)}, u32[]{:S(2)}) collective-permute-start(bf16[2,512,128]{2,1,0:T(8,128)(2,1)S(1)} %collective-permute-done.12.rest_5_), channel_id=1, source_target_pairs={{0,1},{1,0},{2,3},{3,2},{4,5},{5,4},{6,7},{7,6},{8,9},{9,8},{10,11... | collective-permute-start | bytes 786440 | tf_op jit(solution)/shard_map/ppermute | solution.py:311
  82.0 9.1 %collective-permute-start.16 = (bf16[4,24,512]{2,1,0:T(8,128)(2,1)S(1)}, bf16[4,24,512]{2,1,0:T(8,128)(2,1)S(1)}, u32[]{:S(2)}, u32[]{:S(2)}) collective-permute-start(bf16[4,24,512]{2,1,0:T(8,128)(2,1)S(1)} %get-tuple-element.37), channel_id=1, source_target_pairs={{0,1},{1,0},{2,3},{3,2},{4,5},{5,4},{6,7},{7,6},{8,9},{9,8},{10,11... | collective-permute-start | bytes 294920 | tf_op jit(solution)/shard_map/ppermute | solution.py:311
  83.7 7.4 %collective-permute-start.17 = (bf16[4,24,512]{2,1,0:T(8,128)(2,1)S(1)}, bf16[4,24,512]{2,1,0:T(8,128)(2,1)S(1)}, u32[]{:S(2)}, u32[]{:S(2)}) collective-permute-start(bf16[4,24,512]{2,1,0:T(8,128)(2,1)S(1)} %get-tuple-element.38), channel_id=1, source_target_pairs={{0,8},{1,9},{2,10},{3,11},{4,12},{5,13},{6,14},{7,15},{8,0},{9,1},... | collective-permute-start | bytes 294920 | tf_op jit(solution)/shard_map/ppermute | solution.py:311
  86.7 7.9 %collective-permute-start.18 = (bf16[4,24,512]{2,1,0:T(8,128)(2,1)S(1)}, bf16[4,24,512]{2,1,0:T(8,128)(2,1)S(1)}, u32[]{:S(2)}, u32[]{:S(2)}) collective-permute-start(bf16[4,24,512]{2,1,0:T(8,128)(2,1)S(1)} %get-tuple-element.39), channel_id=1, source_target_pairs={{0,9},{1,8},{2,11},{3,10},{4,13},{5,12},{6,15},{7,14},{8,1},{9,0},... | collective-permute-start | bytes 294920 | tf_op jit(solution)/shard_map/ppermute | solution.py:311
  94.7 8.9 %collective-permute-start.20 = (bf16[4,24,512]{2,1,0:T(8,128)(2,1)S(1)}, bf16[4,24,512]{2,1,0:T(8,128)(2,1)S(1)}, u32[]{:S(2)}, u32[]{:S(2)}) collective-permute-start(bf16[4,24,512]{2,1,0:T(8,128)(2,1)S(1)} %near_sum.1.refs_0_), channel_id=1, source_target_pairs={{0,2},{1,3},{2,0},{3,1},{4,6},{5,7},{6,4},{7,5},{8,10},{9,11},{10,... | collective-permute-start | bytes 294920 | tf_op jit(solution)/shard_map/ppermute | solution.py:311
  95.4 15.2 %collective-permute-start.21 = (bf16[4,24,512]{2,1,0:T(8,128)(2,1)S(1)}, bf16[4,24,512]{2,1,0:T(8,128)(2,1)S(1)}, u32[]{:S(2)}, u32[]{:S(2)}) collective-permute-start(bf16[4,24,512]{2,1,0:T(8,128)(2,1)S(1)} %near_sum.1.refs_0_), channel_id=1, source_target_pairs={{0,4},{1,5},{2,6},{3,7},{4,0},{5,1},{6,2},{7,3},{8,12},{9,13},{10,... | collective-permute-start | bytes 294920 | tf_op jit(solution)/shard_map/ppermute | solution.py:311
  100.9 9.7 %collective-permute-start.22 = (bf16[4,24,512]{2,1,0:T(8,128)(2,1)S(1)}, bf16[4,24,512]{2,1,0:T(8,128)(2,1)S(1)}, u32[]{:S(2)}, u32[]{:S(2)}) collective-permute-start(bf16[4,24,512]{2,1,0:T(8,128)(2,1)S(1)} %near_sum.1.refs_0_), channel_id=1, source_target_pairs={{0,6},{1,7},{2,4},{3,5},{4,2},{5,3},{6,0},{7,1},{8,14},{9,15},{10,... | collective-permute-start | bytes 294920 | tf_op jit(solution)/shard_map/ppermute | solution.py:311
  101.2 21.6 %collective-permute-start.26 = (bf16[2,512,128]{2,1,0:T(8,128)(2,1)S(1)}, bf16[2,512,128]{2,1,0:T(8,128)(2,1)S(1)}, u32[]{:S(2)}, u32[]{:S(2)}) collective-permute-start(bf16[2,512,128]{2,1,0:T(8,128)(2,1)S(1)} %collective-permute-done.13.rest_6_), channel_id=1, source_target_pairs={{0,1},{1,0},{2,3},{3,2},{4,5},{5,4},{6,7},{7,6},{8,9},{9,8},{10,11... | collective-permute-start | bytes 786440 | tf_op jit(solution)/shard_map/ppermute | solution.py:311
  110.7 12.2 %collective-permute-start.27 = (bf16[2,512,128]{2,1,0:T(8,128)(2,1)S(1)}, bf16[2,512,128]{2,1,0:T(8,128)(2,1)S(1)}, u32[]{:S(2)}, u32[]{:S(2)}) collective-permute-start(bf16[2,512,128]{2,1,0:T(8,128)(2,1)S(1)} %collective-permute-done.14.rest_7_), channel_id=1, source_target_pairs={{0,1},{1,0},{2,3},{3,2},{4,5},{5,4},{6,7},{7,6},{8,9},{9,8},{10,11... | collective-permute-start | bytes 786440 | tf_op jit(solution)/shard_map/ppermute | solution.py:311
  110.8 10.2 %collective-permute-start.23 = (bf16[4,24,512]{2,1,0:T(8,128)(2,1)S(1)}, bf16[4,24,512]{2,1,0:T(8,128)(2,1)S(1)}, u32[]{:S(2)}, u32[]{:S(2)}) collective-permute-start(bf16[4,24,512]{2,1,0:T(8,128)(2,1)S(1)} %far_sum.1.refs_0_.rest_13_), channel_id=1, source_target_pairs={{0,1},{1,0},{2,3},{3,2},{4,5},{5,4},{6,7},{7,6},{8,9},{9,8},{10,11... | collective-permute-start | bytes 294920 | tf_op jit(solution)/shard_map/ppermute | solution.py:311
  112.8 8.2 %collective-permute-start.24 = (bf16[4,24,512]{2,1,0:T(8,128)(2,1)S(1)}, bf16[4,24,512]{2,1,0:T(8,128)(2,1)S(1)}, u32[]{:S(2)}, u32[]{:S(2)}) collective-permute-start(bf16[4,24,512]{2,1,0:T(8,128)(2,1)S(1)} %far_sum.1.refs_0_.rest_13_), channel_id=1, source_target_pairs={{0,8},{1,9},{2,10},{3,11},{4,12},{5,13},{6,14},{7,15},{8,0},{9,1},... | collective-permute-start | bytes 294920 | tf_op jit(solution)/shard_map/ppermute | solution.py:311
  113.3 8.7 %collective-permute-start.25 = (bf16[4,24,512]{2,1,0:T(8,128)(2,1)S(1)}, bf16[4,24,512]{2,1,0:T(8,128)(2,1)S(1)}, u32[]{:S(2)}, u32[]{:S(2)}) collective-permute-start(bf16[4,24,512]{2,1,0:T(8,128)(2,1)S(1)} %far_sum.1.refs_0_.rest_13_), channel_id=1, source_target_pairs={{0,9},{1,8},{2,11},{3,10},{4,13},{5,12},{6,15},{7,14},{8,1},{9,0},... | collective-permute-start | bytes 294920 | tf_op jit(solution)/shard_map/ppermute | solution.py:311

commit v4 on v3

--- a/solution.py
+++ b/solution.py
@@ -22,10 +22,6 @@
 N_ROUNDS = len(ROUNDS)
 PLACED = 13
 EARLY = 5
-NEXT = 2
-LAST = 1
-FIRST = 0
-SMALL = -1
 
 ANY = pl.BlockSpec(memory_space=pl.ANY)
 VMEM = pl.BlockSpec(memory_space=pltpu.VMEM)
@@ -63,13 +59,13 @@
         copy.wait()
 
 
-def extract_kernel(meta_ref, cache_ref, *rest):
-    outs, (held, in_sem, out_sem) = rest[:N_ROUNDS], rest[N_ROUNDS:]
+def extract_kernel(steps, meta_ref, cache_ref, *rest):
+    outs, (held, in_sem, out_sem) = rest[: len(steps)], rest[len(steps) :]
     rank = meta_ref[0]
     high, low = rank // NZ, rank % NZ
     sign = 1 - 2 * (low % 2)
     loads, stores = [], []
-    for step, (shift, flip) in enumerate(ROUNDS):
+    for step, (shift, flip) in enumerate([ROUNDS[step] for step in steps]):
         target = (high + flip) % 2 * NZ + (low + NZ + sign * shift) % NZ
         columns = pl.ds(pl.multiple_of(target // 2 * HD, HD), HD)
         loads.append(
@@ -85,17 +81,17 @@
         store.wait()
 
 
-def extract(meta, cache):
+def extract(steps, meta, cache):
     block = (2, cache.shape[1], HD)
     return pl.pallas_call(
-        extract_kernel,
-        out_shape=[jax.ShapeDtypeStruct(block, cache.dtype)] * N_ROUNDS,
+        functools.partial(extract_kernel, steps),
+        out_shape=[jax.ShapeDtypeStruct(block, cache.dtype)] * len(steps),
         in_specs=[SMEM, ANY],
-        out_specs=[ANY] * N_ROUNDS,
+        out_specs=[ANY] * len(steps),
         scratch_shapes=[
-            pltpu.VMEM((N_ROUNDS,) + block, cache.dtype),
-            pltpu.SemaphoreType.DMA((N_ROUNDS,)),
-            pltpu.SemaphoreType.DMA((N_ROUNDS,)),
+            pltpu.VMEM((len(steps),) + block, cache.dtype),
+            pltpu.SemaphoreType.DMA((len(steps),)),
+            pltpu.SemaphoreType.DMA((len(steps),)),
         ],
         compiler_params=pltpu.CompilerParams(vmem_limit_bytes=60 * MIB),
         name="extract",
@@ -326,7 +322,14 @@
 
     handed = hop(lengths[0], inst_count, tp_count, lambda t: t)
     other_q = swap(queries[0], tp_count)
-    sent = list(extract(after(meta, [handed, other_q]), source_cache[0, 0]))
+    first = (4, 0)
+    rest = tuple(step for step in range(N_ROUNDS) if step not in first)
+    sent = dict(zip(first, extract(first, meta, source_cache[0, 0])))
+    sent.update(zip(rest, extract(rest, meta, source_cache[0, 0])))
+    sent = [
+        sent[step] if step in first else after(sent[step], [handed, other_q])
+        for step in range(N_ROUNDS)
+    ]
     arrived = [send(step, sent[step]) for step in range(N_ROUNDS)]
 
     index, order, select = tables(tp_count, rows)

time: 125 us -> 121 us (0.968)
  waiting for transfers between devices: 49.1 us -> 39.8 us
  starting transfers between devices: 59.2 us -> 63.4 us
  local copies, waits for them, and re-layouts: 3.73 us -> 1.51 us
  Pallas kernels: 10.5 us -> 12.6 us
    ppermute x19, waiting for transfers between devices: 33.7 us -> 28.2 us  [swap(): return lax.ppermute(value, 'tp', [(t, t ^ bits) for t in range(tp_count)])]
    ppermute x19, starting transfers between devices: 27.5 us -> 31.5 us  [swap(): return lax.ppermute(value, 'tp', [(t, t ^ bits) for t in range(tp_count)])]
    ppermute x9, waiting for transfers between devices: 15.3 us -> 11.6 us  [hop(): return lax.ppermute(value, ('inst', 'tp'), pairs)]
    pallas_call x1 -> x2, Pallas kernels: 2.4 us -> 4 us  [extract(): pl.pallas_call(functools.partial(extract_kernel, steps), out_shape=[jax.S...]
    unnamed x9 -> x13, local copies, waits for them, and re-layouts: 1.61 us -> 0.04 us
  transfers between devices with their start and end apart: 28 -> 28, of which waited for: 12 -> 10; matrix products, arithmetic and copies ran while one was open for 3% -> 2% of each run, Pallas kernels for 4% -> 8%
where the time goes in v4:
time: 121 us; the launch traced here: 119 us
  starting transfers between devices  63.4 us (52%)
  waiting for transfers between devices  39.8 us (33%)
  Pallas kernels  12.6 us (10%)
  local copies, waits for them, and re-layouts  1.51 us (1%)
    ppermute x9, starting transfers between devices, hop(): return lax.ppermute(value, ('inst', 'tp'), pairs)  31.9 us
    ppermute x19, starting transfers between devices, swap(): return lax.ppermute(value, 'tp', [(t, t ^ bits) for t in range(tp_count)])  31.5 us
    ppermute x19, waiting for transfers between devices, swap(): return lax.ppermute(value, 'tp', [(t, t ^ bits) for t in range(tp_count)])  28.2 us
    ppermute x9, waiting for transfers between devices, hop(): return lax.ppermute(value, ('inst', 'tp'), pairs)  11.6 us
    pallas_call x2, Pallas kernels, place(): pl.pallas_call(functools.partial(place_kernel, offset, count, len(out)),...  4.41 us
    pallas_call x2, Pallas kernels, extract(): pl.pallas_call(functools.partial(extract_kernel, steps), out_shape=[jax.S...  4 us
    pallas_call x2, Pallas kernels, attend(): pl.pallas_call(functools.partial(attend_kernel, first, heads, 1.0 / math....  2.43 us
  transfers between devices with their start and end apart: 28, of which 10 were waited for; matrix products, arithmetic and copies ran while one was open for 2% of the time, Pallas kernels for 8%

profile of v4, /device:TPU:8, one launch (start us, length us, event | category | flops | bytes accessed | tf_op | source)
XLA Modules:
  0.0 119.3 jit_solution(7903643851306095497)
XLA Ops:
  0.7 2.0 %collective-permute-start.1 = (bf16[24,256]{1,0:T(8,128)(2,1)}, bf16[24,256]{1,0:T(8,128)(2,1)S(1)}, u32[]{:S(2)}, u32[]{:S(2)}) collective-permute-start(bf16[24,256]{1,0:T(8,128)(2,1)} %bitcast.30), channel_id=1, source_target_pairs={{0,1},{1,0},{2,3},{3,2},{4,5},{5,4},{6,7},{7,6},{8,9},{9,8},{10,11... | collective-permute-start | bytes 36872 | tf_op jit(solution)/shard_map/ppermute | solution.py:307
  2.7 2.3 %collective-permute-start = (s32[24]{0:T(128)}, s32[24]{0:T(128)S(1)}, u32[]{:S(2)}, u32[]{:S(2)}) collective-permute-start(s32[24]{0:T(128)} %bitcast.32), channel_id=1, source_target_pairs={{0,128},{1,129},{2,130},{3,131},{4,132},{5,133},{6,134},{7,135},{8... | collective-permute-start | bytes 296 | tf_op jit(solution)/shard_map/ppermute | solution.py:299
  5.0 1.8 %extract.2 = (bf16[2,512,128]{2,1,0:T(8,128)(2,1)}, bf16[2,512,128]{2,1,0:T(8,128)(2,1)}) custom-call(s32[1]{0:T(128)} %bitcast.meta_ref, bf16[2,512,1024]{2,1,0:T(8,128)(2,1)} %bitcast.26), custom_call_target="tpu_custom_call" | custom-call | tf_op jit(solution)/shard_map/extract/pallas_call | solution.py:86
  6.8 4.0 %collective-permute-start.10 = (bf16[2,512,128]{2,1,0:T(8,128)(2,1)}, bf16[2,512,128]{2,1,0:T(8,128)(2,1)S(1)}, u32[]{:S(2)}, u32[]{:S(2)}) collective-permute-start(bf16[2,512,128]{2,1,0:T(8,128)(2,1)} %get-tuple-element.35), channel_id=1, source_target_pairs={{0,130},{1,135},{2,132},{3,129},{4,134},{5,131},{6,128},{7,133},{8... | collective-permute-start | bytes 786440 | tf_op jit(solution)/shard_map/ppermute | solution.py:299
  10.8 2.3 %collective-permute-start.2 = (bf16[2,512,128]{2,1,0:T(8,128)(2,1)}, bf16[2,512,128]{2,1,0:T(8,128)(2,1)S(1)}, u32[]{:S(2)}, u32[]{:S(2)}) collective-permute-start(bf16[2,512,128]{2,1,0:T(8,128)(2,1)} %get-tuple-element.28), channel_id=1, source_target_pairs={{0,128},{1,129},{2,130},{3,131},{4,132},{5,133},{6,134},{7,135},{8... | collective-permute-start | bytes 786440 | tf_op jit(solution)/shard_map/ppermute | solution.py:299
  13.1 2.2 %extract.3 = (bf16[2,512,128]{2,1,0:T(8,128)(2,1)}, bf16[2,512,128]{2,1,0:T(8,128)(2,1)}, bf16[2,512,128]{2,1,0:T(8,128)(2,1)}, bf16[2,512,128]{2,1,0:T(8,128)(2...) custom-call(s32[1]{0:T(128)} %bitcast.meta_ref, bf16[2,512,1024]{2,1,0:T(8,128)(2,1)} %bitcast.27), custom_call_target="tpu_custom_call" | custom-call | tf_op jit(solution)/shard_map/extract/pallas_call | solution.py:86
  15.3 3.0 %collective-permute-start.4 = (bf16[2,512,128]{2,1,0:T(8,128)(2,1)}, bf16[2,512,128]{2,1,0:T(8,128)(2,1)S(1)}, u32[]{:S(2)}, u32[]{:S(2)}) collective-permute-start(bf16[2,512,128]{2,1,0:T(8,128)(2,1)} %get-tuple-element.30), channel_id=1, source_target_pairs={{0,133},{1,132},{2,135},{3,134},{4,129},{5,128},{6,131},{7,130},{8... | collective-permute-start | bytes 786440 | tf_op jit(solution)/shard_map/ppermute | solution.py:299
  18.3 0.1 slice_bitcast_fusion.len_ref
  18.4 4.8 %collective-permute-start.6 = (bf16[2,512,128]{2,1,0:T(8,128)(2,1)}, bf16[2,512,128]{2,1,0:T(8,128)(2,1)S(1)}, u32[]{:S(2)}, u32[]{:S(2)}) collective-permute-start(bf16[2,512,128]{2,1,0:T(8,128)(2,1)} %get-tuple-element.32), channel_id=1, source_target_pairs={{0,136},{1,137},{2,138},{3,139},{4,140},{5,141},{6,142},{7,143},{8... | collective-permute-start | bytes 786440 | tf_op jit(solution)/shard_map/ppermute | solution.py:299
  23.2 3.4 %collective-permute-start.8 = (bf16[2,512,128]{2,1,0:T(8,128)(2,1)}, bf16[2,512,128]{2,1,0:T(8,128)(2,1)S(1)}, u32[]{:S(2)}, u32[]{:S(2)}) collective-permute-start(bf16[2,512,128]{2,1,0:T(8,128)(2,1)} %get-tuple-element.34), channel_id=1, source_target_pairs={{0,141},{1,140},{2,143},{3,142},{4,137},{5,136},{6,139},{7,138},{8... | collective-permute-start | bytes 786440 | tf_op jit(solution)/shard_map/ppermute | solution.py:299
  26.6 3.1 %collective-permute-start.11 = (bf16[2,512,128]{2,1,0:T(8,128)(2,1)S(1)}, bf16[2,512,128]{2,1,0:T(8,128)(2,1)}, u32[]{:S(2)}, u32[]{:S(2)}) collective-permute-start(bf16[2,512,128]{2,1,0:T(8,128)(2,1)S(1)} %collective-permute-done.10.rest_4_), channel_id=1, source_target_pairs={{0,1},{1,0},{2,3},{3,2},{4,5},{5,4},{6,7},{7,6},{8,9},{9,8},{10,11... | collective-permute-start | bytes 786440 | tf_op jit(solution)/shard_map/ppermute | solution.py:307
  29.7 11.6 %collective-permute-done.2.rest_0_ = bf16[2,512,128]{2,1,0:T(8,128)(2,1)S(1)} collective-permute-done((bf16[2,512,128]{2,1,0:T(8,128)(2,1)}, bf16[2,512,128]{2,1,0:T(8,128)(2,1)S(1)}, u32[]{:S(2)}, u32[]{:S(2)}) %collective-permute-start.2) | collective-permute-done | bytes 262176 | tf_op jit(solution)/shard_map/ppermute | solution.py:299
  41.3 2.0 %collective-permute-start.5 = (bf16[2,512,128]{2,1,0:T(8,128)(2,1)S(1)}, bf16[2,512,128]{2,1,0:T(8,128)(2,1)}, u32[]{:S(2)}, u32[]{:S(2)}) collective-permute-start(bf16[2,512,128]{2,1,0:T(8,128)(2,1)S(1)} %collective-permute-done.4.rest_1_), channel_id=1, source_target_pairs={{0,1},{1,0},{2,3},{3,2},{4,5},{5,4},{6,7},{7,6},{8,9},{9,8},{10,11... | collective-permute-start | bytes 786440 | tf_op jit(solution)/shard_map/ppermute | solution.py:307
  43.3 0.7 fusion.10
  44.0 8.3 %collective-permute-start.12 = (bf16[2,512,128]{2,1,0:T(8,128)(2,1)}, bf16[2,512,128]{2,1,0:T(8,128)(2,1)S(1)}, u32[]{:S(2)}, u32[]{:S(2)}) collective-permute-start(bf16[2,512,128]{2,1,0:T(8,128)(2,1)} %get-tuple-element.38), channel_id=1, source_target_pairs={{0,143},{1,138},{2,137},{3,140},{4,139},{5,142},{6,141},{7,136},{8... | collective-permute-start | bytes 786440 | tf_op jit(solution)/shard_map/ppermute | solution.py:299
  52.3 3.8 %collective-permute-start.14 = (bf16[2,512,128]{2,1,0:T(8,128)(2,1)}, bf16[2,512,128]{2,1,0:T(8,128)(2,1)S(1)}, u32[]{:S(2)}, u32[]{:S(2)}) collective-permute-start(bf16[2,512,128]{2,1,0:T(8,128)(2,1)} %get-tuple-element.42), channel_id=1, source_target_pairs={{0,135},{1,130},{2,129},{3,132},{4,131},{5,134},{6,133},{7,128},{8... | collective-permute-start | bytes 786440 | tf_op jit(solution)/shard_map/ppermute | solution.py:299
  56.2 2.0 %collective-permute-start.9 = (bf16[2,512,128]{2,1,0:T(8,128)(2,1)S(1)}, bf16[2,512,128]{2,1,0:T(8,128)(2,1)S(1)}, u32[]{:S(2)}, u32[]{:S(2)}) collective-permute-start(bf16[2,512,128]{2,1,0:T(8,128)(2,1)S(1)} %collective-permute-done.8.rest_3_), channel_id=1, source_target_pairs={{0,1},{1,0},{2,3},{3,2},{4,5},{5,4},{6,7},{7,6},{8,9},{9,8},{10,11... | collective-permute-start | bytes 786440 | tf_op jit(solution)/shard_map/ppermute | solution.py:307
  58.2 0.2 select_reduce_fusion.len_ref
  58.4 0.8 fusion.rows_ref
  59.2 1.2 %attend.2.res_ref = f32[8,256]{1,0:T(8,128)S(1)} custom-call(s32[8]{0:T(128)S(1)} %slice_bitcast_fusion.len_ref, f32[16,768]{1,0:T(8,128)S(1)} %fusion.rows_ref, bf16[8,2,512,128]{3,2,1,0:T(8,128)(2,1)S(1)} %bitcast.23), custom_call_target="tpu_custom_call" | custom-call | tf_op jit(solution)/shard_map/attend/pallas_call | solution.py:186
  60.5 6.9 %collective-permute-done.7.rest_10_ = bf16[2,512,128]{2,1,0:T(8,128)(2,1)S(1)} collective-permute-done((bf16[2,512,128]{2,1,0:T(8,128)(2,1)S(1)}, bf16[2,512,128]{2,1,0:T(8,128)(2,1)S(1)}, u32[]{:S(2)}, u32[]{:S(2)}) %collective-permute-start.7) | collective-permute-done | bytes 262176 | tf_op jit(solution)/shard_map/ppermute | solution.py:307
  67.4 4.7 %collective-permute-done.9.rest_11_ = bf16[2,512,128]{2,1,0:T(8,128)(2,1)S(1)} collective-permute-done((bf16[2,512,128]{2,1,0:T(8,128)(2,1)S(1)}, bf16[2,512,128]{2,1,0:T(8,128)(2,1)S(1)}, u32[]{:S(2)}, u32[]{:S(2)}) %collective-permute-start.9) | collective-permute-done | bytes 262176 | tf_op jit(solution)/shard_map/ppermute | solution.py:307
  72.1 1.2 %attend.3 = (f32[8,256]{1,0:T(8,128)S(1)}, f32[8,256]{1,0:T(8,128)S(1)}) custom-call(s32[8]{0:T(128)S(1)} %select_reduce_fusion.len_ref, f32[16,768]{1,0:T(8,128)S(1)} %fusion.rows_ref, bf16[2,512,128]{2,1,0:T(8,128)(2,1)S(1)} %collective-permute-done.2.rest_0_, bf16[2,512,128]{2,1,0:T(8,128)(2,1)S(1)} %collective-permute-done.4.rest_1_, ...), custom_call_target="tpu_custom_call" | custom-call | tf_op jit(solution)/shard_map/attend/pallas_call | solution.py:186
  73.3 1.1 collective-permute-start.15
  74.3 0.7 dynamic-slice_bitcast_fusion.place_ref
  75.0 2.0 %collective-permute-done.15.traded_ref = f32[8,256]{1,0:T(8,128)S(1)} collective-permute-done((f32[8,256]{1,0:T(8,128)S(1)}, f32[8,256]{1,0:T(8,128)S(1)}, u32[]{:S(2)}, u32[]{:S(2)}) %collective-permute-start.15) | collective-permute-done | bytes 8224 | tf_op jit(solution)/shard_map/ppermute | solution.py:307
  77.0 0.9 project.1
  77.9 1.1 collective-permute-start.19
  79.0 1.0 collective-permute-start.16
  80.0 3.2 %collective-permute-start.17 = (bf16[4,24,512]{2,1,0:T(8,128)(2,1)S(1)}, bf16[4,24,512]{2,1,0:T(8,128)(2,1)S(1)}, u32[]{:S(2)}, u32[]{:S(2)}) collective-permute-start(bf16[4,24,512]{2,1,0:T(8,128)(2,1)S(1)} %get-tuple-element.48), channel_id=1, source_target_pairs={{0,8},{1,9},{2,10},{3,11},{4,12},{5,13},{6,14},{7,15},{8,0},{9,1},... | collective-permute-start | bytes 294920 | tf_op jit(solution)/shard_map/ppermute | solution.py:307
  83.2 0.7 collective-permute-start.18
  84.0 3.5 %collective-permute-done.16.refs_1_ = bf16[4,24,512]{2,1,0:T(8,128)(2,1)S(1)} collective-permute-done((bf16[4,24,512]{2,1,0:T(8,128)(2,1)S(1)}, bf16[4,24,512]{2,1,0:T(8,128)(2,1)S(1)}, u32[]{:S(2)}, u32[]{:S(2)}) %collective-permute-start.16) | collective-permute-done | bytes 98336 | tf_op jit(solution)/shard_map/ppermute | solution.py:307
  87.5 3.6 %collective-permute-done.18.refs_3_ = bf16[4,24,512]{2,1,0:T(8,128)(2,1)S(1)} collective-permute-done((bf16[4,24,512]{2,1,0:T(8,128)(2,1)S(1)}, bf16[4,24,512]{2,1,0:T(8,128)(2,1)S(1)}, u32[]{:S(2)}, u32[]{:S(2)}) %collective-permute-start.18) | collective-permute-done | bytes 98336 | tf_op jit(solution)/shard_map/ppermute | solution.py:307
  91.2 0.1 collective-permute-start.20
  91.3 4.5 %collective-permute-start.21 = (bf16[4,24,512]{2,1,0:T(8,128)(2,1)S(1)}, bf16[4,24,512]{2,1,0:T(8,128)(2,1)S(1)}, u32[]{:S(2)}, u32[]{:S(2)}) collective-permute-start(bf16[4,24,512]{2,1,0:T(8,128)(2,1)S(1)} %near_sum.1.refs_0_), channel_id=1, source_target_pairs={{0,4},{1,5},{2,6},{3,7},{4,0},{5,1},{6,2},{7,3},{8,12},{9,13},{10,... | collective-permute-start | bytes 294920 | tf_op jit(solution)/shard_map/ppermute | solution.py:307
  95.7 2.0 %collective-permute-start.22 = (bf16[4,24,512]{2,1,0:T(8,128)(2,1)S(1)}, bf16[4,24,512]{2,1,0:T(8,128)(2,1)S(1)}, u32[]{:S(2)}, u32[]{:S(2)}) collective-permute-start(bf16[4,24,512]{2,1,0:T(8,128)(2,1)S(1)} %near_sum.1.refs_0_), channel_id=1, source_target_pairs={{0,6},{1,7},{2,4},{3,5},{4,2},{5,3},{6,0},{7,1},{8,14},{9,15},{10,... | collective-permute-start | bytes 294920 | tf_op jit(solution)/shard_map/ppermute | solution.py:307
  97.7 2.6 %collective-permute-start.26 = (bf16[2,512,128]{2,1,0:T(8,128)(2,1)S(1)}, bf16[2,512,128]{2,1,0:T(8,128)(2,1)S(1)}, u32[]{:S(2)}, u32[]{:S(2)}) collective-permute-start(bf16[2,512,128]{2,1,0:T(8,128)(2,1)S(1)} %collective-permute-done.13.rest_6_), channel_id=1, source_target_pairs={{0,1},{1,0},{2,3},{3,2},{4,5},{5,4},{6,7},{7,6},{8,9},{9,8},{10,11... | collective-permute-start | bytes 786440 | tf_op jit(solution)/shard_map/ppermute | solution.py:307
  100.4 3.7 %collective-permute-done.21.refs_2_ = bf16[4,24,512]{2,1,0:T(8,128)(2,1)S(1)} collective-permute-done((bf16[4,24,512]{2,1,0:T(8,128)(2,1)S(1)}, bf16[4,24,512]{2,1,0:T(8,128)(2,1)S(1)}, u32[]{:S(2)}, u32[]{:S(2)}) %collective-permute-start.21) | collective-permute-done | bytes 98336 | tf_op jit(solution)/shard_map/ppermute | solution.py:307
  104.1 1.1 collective-permute-done.22.refs_3_
  105.3 1.0 collective-permute-start.27
  106.3 1.1 collective-permute-start.23
  107.4 0.3 collective-permute-start.24
  107.6 3.6 %collective-permute-start.25 = (bf16[4,24,512]{2,1,0:T(8,128)(2,1)S(1)}, bf16[4,24,512]{2,1,0:T(8,128)(2,1)S(1)}, u32[]{:S(2)}, u32[]{:S(2)}) collective-permute-start(bf16[4,24,512]{2,1,0:T(8,128)(2,1)S(1)} %far_sum.1.refs_0_.rest_13_), channel_id=1, source_target_pairs={{0,9},{1,8},{2,11},{3,10},{4,13},{5,12},{6,15},{7,14},{8,1},{9,0},... | collective-permute-start | bytes 294920 | tf_op jit(solution)/shard_map/ppermute | solution.py:307
  111.3 3.0 %place.2.rest_3_ = bf16[16,2,512,128]{3,2,1,0:T(8,128)(2,1)} custom-call(s32[16]{0:T(128)S(1)} %get-tuple-element.54.index_ref, bf16[2,512,128]{2,1,0:T(8,128)(2,1)S(1)} %collective-permute-done.2.rest_0_, bf16[2,512,128]{2,1,0:T(8,128)(2,1)S(1)} %collective-permute-done.4.rest_1_, bf16[2,512,128]{2,1,0:T(8,128)(2,1)S(1)} %collective-permute-done.6.rest_2_, ...), custom_call_target="tpu_custom_call" | custom-call | tf_op jit(solution)/shard_map/place/pallas_call | solution.py:122
  114.2 1.5 %collective-permute-done.23.refs_1_ = bf16[4,24,512]{2,1,0:T(8,128)(2,1)S(1)} collective-permute-done((bf16[4,24,512]{2,1,0:T(8,128)(2,1)S(1)}, bf16[4,24,512]{2,1,0:T(8,128)(2,1)S(1)}, u32[]{:S(2)}, u32[]{:S(2)}) %collective-permute-start.23) | collective-permute-done | bytes 98336 | tf_op jit(solution)/shard_map/ppermute | solution.py:307
  115.7 1.2 collective-permute-done.25.refs_3_
  116.9 0.8 join.1
  117.7 1.4 %place.3 = bf16[16,2,512,128]{3,2,1,0:T(8,128)(2,1)} custom-call(s32[16]{0:T(128)S(1)} %get-tuple-element.54.index_ref, bf16[2,512,128]{2,1,0:T(8,128)(2,1)S(1)} %collective-permute-done.19.rest_0_, bf16[2,512,128]{2,1,0:T(8,128)(2,1)S(1)} %collective-permute-done.26.rest_1_, ...), custom_call_target="tpu_custom_call", output_to_operand_aliasing={{}: (4, {})} | custom-call | tf_op jit(solution)/shard_map/place/pallas_call | solution.py:122
  (38 shorter events, 0.3 us)
Async XLA Ops:
  0.6 57.6 %copy-start = (bf16[1,24,2,1024]{3,2,1,0:T(2,128)(2,1)S(1)}, bf16[1,24,2,1024]{3,2,1,0:T(2,128)(2,1)}, u32[]{:S(2)}) copy-start(bf16[1,24,2,1024]{3,2,1,0:T(2,128)(2,1)} %param.12) | copy-start | bytes 294916
  0.6 57.8 %copy-start.4 = (bf16[1,24,256]{2,1,0:T(8,128)(2,1)S(1)}, bf16[1,24,256]{2,1,0:T(8,128)(2,1)}, u32[]{:S(2)}) copy-start(bf16[1,24,256]{2,1,0:T(8,128)(2,1)} %param.13) | copy-start | bytes 36868
  0.7 17.7 %copy-start.5 = (s32[1,24]{1,0:T(1,128)S(1)}, s32[1,24]{1,0:T(1,128)}, u32[]{:S(2)}) copy-start(s32[1,24]{1,0:T(1,128)} %param.15) | copy-start | bytes 292
  0.7 58.6 %copy-start.2 = (bf16[1,1,8,2,512,128]{5,4,3,2,1,0:T(8,128)(2,1)S(1)}, bf16[1,1,8,2,512,128]{5,4,3,2,1,0:T(8,128)(2,1)}, u32[]{:S(2)}) copy-start(bf16[1,1,8,2,512,128]{5,4,3,2,1,0:T(8,128)(2,1)} %param.11) | copy-start | bytes 6291460
  0.7 14.6 %collective-permute-start.1 = (bf16[24,256]{1,0:T(8,128)(2,1)}, bf16[24,256]{1,0:T(8,128)(2,1)S(1)}, u32[]{:S(2)}, u32[]{:S(2)}) collective-permute-start(bf16[24,256]{1,0:T(8,128)(2,1)} %bitcast.30), channel_id=1, source_target_pairs={{0,1},{1,0},{2,3},{3,2},{4,5},{5,4},{6,7},{7,6},{8,9},{9,8},{10,11... | collective-permute-start | bytes 36872 | tf_op jit(solution)/shard_map/ppermute | solution.py:307
  2.7 12.6 %collective-permute-start = (s32[24]{0:T(128)}, s32[24]{0:T(128)S(1)}, u32[]{:S(2)}, u32[]{:S(2)}) collective-permute-start(s32[24]{0:T(128)} %bitcast.32), channel_id=1, source_target_pairs={{0,128},{1,129},{2,130},{3,131},{4,132},{5,133},{6,134},{7,135},{8... | collective-permute-start | bytes 296 | tf_op jit(solution)/shard_map/ppermute | solution.py:299
  6.8 19.8 %collective-permute-start.10 = (bf16[2,512,128]{2,1,0:T(8,128)(2,1)}, bf16[2,512,128]{2,1,0:T(8,128)(2,1)S(1)}, u32[]{:S(2)}, u32[]{:S(2)}) collective-permute-start(bf16[2,512,128]{2,1,0:T(8,128)(2,1)} %get-tuple-element.35), channel_id=1, source_target_pairs={{0,130},{1,135},{2,132},{3,129},{4,134},{5,131},{6,128},{7,133},{8... | collective-permute-start | bytes 786440 | tf_op jit(solution)/shard_map/ppermute | solution.py:299
  10.8 30.5 %collective-permute-start.2 = (bf16[2,512,128]{2,1,0:T(8,128)(2,1)}, bf16[2,512,128]{2,1,0:T(8,128)(2,1)S(1)}, u32[]{:S(2)}, u32[]{:S(2)}) collective-permute-start(bf16[2,512,128]{2,1,0:T(8,128)(2,1)} %get-tuple-element.28), channel_id=1, source_target_pairs={{0,128},{1,129},{2,130},{3,131},{4,132},{5,133},{6,134},{7,135},{8... | collective-permute-start | bytes 786440 | tf_op jit(solution)/shard_map/ppermute | solution.py:299
  15.3 26.0 %collective-permute-start.4 = (bf16[2,512,128]{2,1,0:T(8,128)(2,1)}, bf16[2,512,128]{2,1,0:T(8,128)(2,1)S(1)}, u32[]{:S(2)}, u32[]{:S(2)}) collective-permute-start(bf16[2,512,128]{2,1,0:T(8,128)(2,1)} %get-tuple-element.30), channel_id=1, source_target_pairs={{0,133},{1,132},{2,135},{3,134},{4,129},{5,128},{6,131},{7,130},{8... | collective-permute-start | bytes 786440 | tf_op jit(solution)/shard_map/ppermute | solution.py:299
  18.4 25.7 %collective-permute-start.6 = (bf16[2,512,128]{2,1,0:T(8,128)(2,1)}, bf16[2,512,128]{2,1,0:T(8,128)(2,1)S(1)}, u32[]{:S(2)}, u32[]{:S(2)}) collective-permute-start(bf16[2,512,128]{2,1,0:T(8,128)(2,1)} %get-tuple-element.32), channel_id=1, source_target_pairs={{0,136},{1,137},{2,138},{3,139},{4,140},{5,141},{6,142},{7,143},{8... | collective-permute-start | bytes 786440 | tf_op jit(solution)/shard_map/ppermute | solution.py:299
  23.2 29.2 %collective-permute-start.8 = (bf16[2,512,128]{2,1,0:T(8,128)(2,1)}, bf16[2,512,128]{2,1,0:T(8,128)(2,1)S(1)}, u32[]{:S(2)}, u32[]{:S(2)}) collective-permute-start(bf16[2,512,128]{2,1,0:T(8,128)(2,1)} %get-tuple-element.34), channel_id=1, source_target_pairs={{0,141},{1,140},{2,143},{3,142},{4,137},{5,136},{6,139},{7,138},{8... | collective-permute-start | bytes 786440 | tf_op jit(solution)/shard_map/ppermute | solution.py:299
  26.6 25.7 %collective-permute-start.11 = (bf16[2,512,128]{2,1,0:T(8,128)(2,1)S(1)}, bf16[2,512,128]{2,1,0:T(8,128)(2,1)}, u32[]{:S(2)}, u32[]{:S(2)}) collective-permute-start(bf16[2,512,128]{2,1,0:T(8,128)(2,1)S(1)} %collective-permute-done.10.rest_4_), channel_id=1, source_target_pairs={{0,1},{1,0},{2,3},{3,2},{4,5},{5,4},{6,7},{7,6},{8,9},{9,8},{10,11... | collective-permute-start | bytes 786440 | tf_op jit(solution)/shard_map/ppermute | solution.py:307
  41.3 14.8 %collective-permute-start.3 = (bf16[2,512,128]{2,1,0:T(8,128)(2,1)S(1)}, bf16[2,512,128]{2,1,0:T(8,128)(2,1)}, u32[]{:S(2)}, u32[]{:S(2)}) collective-permute-start(bf16[2,512,128]{2,1,0:T(8,128)(2,1)S(1)} %collective-permute-done.2.rest_0_), channel_id=1, source_target_pairs={{0,1},{1,0},{2,3},{3,2},{4,5},{5,4},{6,7},{7,6},{8,9},{9,8},{10,11... | collective-permute-start | bytes 786440 | tf_op jit(solution)/shard_map/ppermute | solution.py:307
  41.3 14.9 %collective-permute-start.5 = (bf16[2,512,128]{2,1,0:T(8,128)(2,1)S(1)}, bf16[2,512,128]{2,1,0:T(8,128)(2,1)}, u32[]{:S(2)}, u32[]{:S(2)}) collective-permute-start(bf16[2,512,128]{2,1,0:T(8,128)(2,1)S(1)} %collective-permute-done.4.rest_1_), channel_id=1, source_target_pairs={{0,1},{1,0},{2,3},{3,2},{4,5},{5,4},{6,7},{7,6},{8,9},{9,8},{10,11... | collective-permute-start | bytes 786440 | tf_op jit(solution)/shard_map/ppermute | solution.py:307
  44.0 33.0 %copy-start.1 = (bf16[256,8192]{1,0:T(8,128)(2,1)S(1)}, bf16[256,8192]{1,0:T(8,128)(2,1)}, u32[]{:S(2)}) copy-start(bf16[256,8192]{1,0:T(8,128)(2,1)} %weight_ref.1) | copy-start | bytes 12582916
  44.0 28.0 %collective-permute-start.12 = (bf16[2,512,128]{2,1,0:T(8,128)(2,1)}, bf16[2,512,128]{2,1,0:T(8,128)(2,1)S(1)}, u32[]{:S(2)}, u32[]{:S(2)}) collective-permute-start(bf16[2,512,128]{2,1,0:T(8,128)(2,1)} %get-tuple-element.38), channel_id=1, source_target_pairs={{0,143},{1,138},{2,137},{3,140},{4,139},{5,142},{6,141},{7,136},{8... | collective-permute-start | bytes 786440 | tf_op jit(solution)/shard_map/ppermute | solution.py:299
  52.3 19.8 %collective-permute-start.13 = (bf16[2,512,128]{2,1,0:T(8,128)(2,1)}, bf16[2,512,128]{2,1,0:T(8,128)(2,1)S(1)}, u32[]{:S(2)}, u32[]{:S(2)}) collective-permute-start(bf16[2,512,128]{2,1,0:T(8,128)(2,1)} %get-tuple-element.40), channel_id=1, source_target_pairs={{0,138},{1,143},{2,140},{3,137},{4,142},{5,139},{6,136},{7,141},{8... | collective-permute-start | bytes 786440 | tf_op jit(solution)/shard_map/ppermute | solution.py:299
  52.3 19.7 %collective-permute-start.14 = (bf16[2,512,128]{2,1,0:T(8,128)(2,1)}, bf16[2,512,128]{2,1,0:T(8,128)(2,1)S(1)}, u32[]{:S(2)}, u32[]{:S(2)}) collective-permute-start(bf16[2,512,128]{2,1,0:T(8,128)(2,1)} %get-tuple-element.42), channel_id=1, source_target_pairs={{0,135},{1,130},{2,129},{3,132},{4,131},{5,134},{6,133},{7,128},{8... | collective-permute-start | bytes 786440 | tf_op jit(solution)/shard_map/ppermute | solution.py:299
  56.2 11.2 %collective-permute-start.7 = (bf16[2,512,128]{2,1,0:T(8,128)(2,1)S(1)}, bf16[2,512,128]{2,1,0:T(8,128)(2,1)S(1)}, u32[]{:S(2)}, u32[]{:S(2)}) collective-permute-start(bf16[2,512,128]{2,1,0:T(8,128)(2,1)S(1)} %collective-permute-done.6.rest_2_), channel_id=1, source_target_pairs={{0,1},{1,0},{2,3},{3,2},{4,5},{5,4},{6,7},{7,6},{8,9},{9,8},{10,11... | collective-permute-start | bytes 786440 | tf_op jit(solution)/shard_map/ppermute | solution.py:307
  56.2 15.9 %collective-permute-start.9 = (bf16[2,512,128]{2,1,0:T(8,128)(2,1)S(1)}, bf16[2,512,128]{2,1,0:T(8,128)(2,1)S(1)}, u32[]{:S(2)}, u32[]{:S(2)}) collective-permute-start(bf16[2,512,128]{2,1,0:T(8,128)(2,1)S(1)} %collective-permute-done.8.rest_3_), channel_id=1, source_target_pairs={{0,1},{1,0},{2,3},{3,2},{4,5},{5,4},{6,7},{7,6},{8,9},{9,8},{10,11... | collective-permute-start | bytes 786440 | tf_op jit(solution)/shard_map/ppermute | solution.py:307
  59.2 46.0 %copy-start.3 = (bf16[1,24,8192]{2,1,0:T(8,128)(2,1)S(1)}, bf16[1,24,8192]{2,1,0:T(8,128)(2,1)}, u32[]{:S(2)}) copy-start(bf16[1,24,8192]{2,1,0:T(8,128)(2,1)} %param.14) | copy-start | bytes 1179652
  73.3 3.7 %collective-permute-start.15 = (f32[8,256]{1,0:T(8,128)S(1)}, f32[8,256]{1,0:T(8,128)S(1)}, u32[]{:S(2)}, u32[]{:S(2)}) collective-permute-start(f32[8,256]{1,0:T(8,128)S(1)} %get-tuple-element.44), channel_id=1, source_target_pairs={{0,1},{1,0},{2,3},{3,2},{4,5},{5,4},{6,7},{7,6},{8,9},{9,8},{10,11... | collective-permute-start | bytes 24584 | tf_op jit(solution)/shard_map/ppermute | solution.py:307
  77.9 22.4 %collective-permute-start.19 = (bf16[2,512,128]{2,1,0:T(8,128)(2,1)S(1)}, bf16[2,512,128]{2,1,0:T(8,128)(2,1)S(1)}, u32[]{:S(2)}, u32[]{:S(2)}) collective-permute-start(bf16[2,512,128]{2,1,0:T(8,128)(2,1)S(1)} %collective-permute-done.12.rest_5_), channel_id=1, source_target_pairs={{0,1},{1,0},{2,3},{3,2},{4,5},{5,4},{6,7},{7,6},{8,9},{9,8},{10,11... | collective-permute-start | bytes 786440 | tf_op jit(solution)/shard_map/ppermute | solution.py:307
  79.0 8.5 %collective-permute-start.16 = (bf16[4,24,512]{2,1,0:T(8,128)(2,1)S(1)}, bf16[4,24,512]{2,1,0:T(8,128)(2,1)S(1)}, u32[]{:S(2)}, u32[]{:S(2)}) collective-permute-start(bf16[4,24,512]{2,1,0:T(8,128)(2,1)S(1)} %get-tuple-element.47), channel_id=1, source_target_pairs={{0,1},{1,0},{2,3},{3,2},{4,5},{5,4},{6,7},{7,6},{8,9},{9,8},{10,11... | collective-permute-start | bytes 294920 | tf_op jit(solution)/shard_map/ppermute | solution.py:307
  80.0 7.5 %collective-permute-start.17 = (bf16[4,24,512]{2,1,0:T(8,128)(2,1)S(1)}, bf16[4,24,512]{2,1,0:T(8,128)(2,1)S(1)}, u32[]{:S(2)}, u32[]{:S(2)}) collective-permute-start(bf16[4,24,512]{2,1,0:T(8,128)(2,1)S(1)} %get-tuple-element.48), channel_id=1, source_target_pairs={{0,8},{1,9},{2,10},{3,11},{4,12},{5,13},{6,14},{7,15},{8,0},{9,1},... | collective-permute-start | bytes 294920 | tf_op jit(solution)/shard_map/ppermute | solution.py:307
  83.2 7.9 %collective-permute-start.18 = (bf16[4,24,512]{2,1,0:T(8,128)(2,1)S(1)}, bf16[4,24,512]{2,1,0:T(8,128)(2,1)S(1)}, u32[]{:S(2)}, u32[]{:S(2)}) collective-permute-start(bf16[4,24,512]{2,1,0:T(8,128)(2,1)S(1)} %get-tuple-element.49), channel_id=1, source_target_pairs={{0,9},{1,8},{2,11},{3,10},{4,13},{5,12},{6,15},{7,14},{8,1},{9,0},... | collective-permute-start | bytes 294920 | tf_op jit(solution)/shard_map/ppermute | solution.py:307
  91.2 9.2 %collective-permute-start.20 = (bf16[4,24,512]{2,1,0:T(8,128)(2,1)S(1)}, bf16[4,24,512]{2,1,0:T(8,128)(2,1)S(1)}, u32[]{:S(2)}, u32[]{:S(2)}) collective-permute-start(bf16[4,24,512]{2,1,0:T(8,128)(2,1)S(1)} %near_sum.1.refs_0_), channel_id=1, source_target_pairs={{0,2},{1,3},{2,0},{3,1},{4,6},{5,7},{6,4},{7,5},{8,10},{9,11},{10,... | collective-permute-start | bytes 294920 | tf_op jit(solution)/shard_map/ppermute | solution.py:307
  91.3 12.8 %collective-permute-start.21 = (bf16[4,24,512]{2,1,0:T(8,128)(2,1)S(1)}, bf16[4,24,512]{2,1,0:T(8,128)(2,1)S(1)}, u32[]{:S(2)}, u32[]{:S(2)}) collective-permute-start(bf16[4,24,512]{2,1,0:T(8,128)(2,1)S(1)} %near_sum.1.refs_0_), channel_id=1, source_target_pairs={{0,4},{1,5},{2,6},{3,7},{4,0},{5,1},{6,2},{7,3},{8,12},{9,13},{10,... | collective-permute-start | bytes 294920 | tf_op jit(solution)/shard_map/ppermute | solution.py:307
  95.7 9.4 %collective-permute-start.22 = (bf16[4,24,512]{2,1,0:T(8,128)(2,1)S(1)}, bf16[4,24,512]{2,1,0:T(8,128)(2,1)S(1)}, u32[]{:S(2)}, u32[]{:S(2)}) collective-permute-start(bf16[4,24,512]{2,1,0:T(8,128)(2,1)S(1)} %near_sum.1.refs_0_), channel_id=1, source_target_pairs={{0,6},{1,7},{2,4},{3,5},{4,2},{5,3},{6,0},{7,1},{8,14},{9,15},{10,... | collective-permute-start | bytes 294920 | tf_op jit(solution)/shard_map/ppermute | solution.py:307
  97.7 20.0 %collective-permute-start.26 = (bf16[2,512,128]{2,1,0:T(8,128)(2,1)S(1)}, bf16[2,512,128]{2,1,0:T(8,128)(2,1)S(1)}, u32[]{:S(2)}, u32[]{:S(2)}) collective-permute-start(bf16[2,512,128]{2,1,0:T(8,128)(2,1)S(1)} %collective-permute-done.13.rest_6_), channel_id=1, source_target_pairs={{0,1},{1,0},{2,3},{3,2},{4,5},{5,4},{6,7},{7,6},{8,9},{9,8},{10,11... | collective-permute-start | bytes 786440 | tf_op jit(solution)/shard_map/ppermute | solution.py:307
  105.3 12.4 %collective-permute-start.27 = (bf16[2,512,128]{2,1,0:T(8,128)(2,1)S(1)}, bf16[2,512,128]{2,1,0:T(8,128)(2,1)S(1)}, u32[]{:S(2)}, u32[]{:S(2)}) collective-permute-start(bf16[2,512,128]{2,1,0:T(8,128)(2,1)S(1)} %collective-permute-done.14.rest_7_), channel_id=1, source_target_pairs={{0,1},{1,0},{2,3},{3,2},{4,5},{5,4},{6,7},{7,6},{8,9},{9,8},{10,11... | collective-permute-start | bytes 786440 | tf_op jit(solution)/shard_map/ppermute | solution.py:307
  106.3 9.5 %collective-permute-start.23 = (bf16[4,24,512]{2,1,0:T(8,128)(2,1)S(1)}, bf16[4,24,512]{2,1,0:T(8,128)(2,1)S(1)}, u32[]{:S(2)}, u32[]{:S(2)}) collective-permute-start(bf16[4,24,512]{2,1,0:T(8,128)(2,1)S(1)} %far_sum.1.refs_0_.rest_13_), channel_id=1, source_target_pairs={{0,1},{1,0},{2,3},{3,2},{4,5},{5,4},{6,7},{7,6},{8,9},{9,8},{10,11... | collective-permute-start | bytes 294920 | tf_op jit(solution)/shard_map/ppermute | solution.py:307
  107.4 8.4 %collective-permute-start.24 = (bf16[4,24,512]{2,1,0:T(8,128)(2,1)S(1)}, bf16[4,24,512]{2,1,0:T(8,128)(2,1)S(1)}, u32[]{:S(2)}, u32[]{:S(2)}) collective-permute-start(bf16[4,24,512]{2,1,0:T(8,128)(2,1)S(1)} %far_sum.1.refs_0_.rest_13_), channel_id=1, source_target_pairs={{0,8},{1,9},{2,10},{3,11},{4,12},{5,13},{6,14},{7,15},{8,0},{9,1},... | collective-permute-start | bytes 294920 | tf_op jit(solution)/shard_map/ppermute | solution.py:307
  107.6 9.3 %collective-permute-start.25 = (bf16[4,24,512]{2,1,0:T(8,128)(2,1)S(1)}, bf16[4,24,512]{2,1,0:T(8,128)(2,1)S(1)}, u32[]{:S(2)}, u32[]{:S(2)}) collective-permute-start(bf16[4,24,512]{2,1,0:T(8,128)(2,1)S(1)} %far_sum.1.refs_0_.rest_13_), channel_id=1, source_target_pairs={{0,9},{1,8},{2,11},{3,10},{4,13},{5,12},{6,15},{7,14},{8,1},{9,0},... | collective-permute-start | bytes 294920 | tf_op jit(solution)/shard_map/ppermute | solution.py:307

commit v5 on v4

--- a/solution.py
+++ b/solution.py
@@ -267,26 +267,41 @@
     )(meta, *parts, residual)
 
 
-def join_kernel(meta_ref, *refs):
-    parts, out_ref = refs[:4], refs[4]
+def finish_kernel(offset, count, meta_ref, index_ref, *rest):
+    parts, blocks = rest[:4], rest[4 : 4 + count]
+    mixed_ref, out_ref, sem = rest[-3:]
+    copies = [
+        pltpu.make_async_copy(blocks[i], out_ref.at[index_ref[offset + i]], sem.at[i])
+        for i in range(count)
+    ]
+    for copy in copies:
+        copy.start()
     rank = meta_ref[0]
     for near, part in zip((0,) + NEAR, parts):
         chunk = part.shape[2]
         for far in range(4):
             columns = pl.ds(pl.multiple_of(owner(rank, far, near) * chunk, chunk), chunk)
-            out_ref[0, :, columns] = part[far]
-
-
-def join(meta, parts, count):
+            mixed_ref[0, :, columns] = part[far]
+    for copy in copies:
+        copy.wait()
+
+
+def finish(meta, index, parts, tp_count, offset, blocks, base):
     _, rows, chunk = parts[0].shape
-    return pl.pallas_call(
-        join_kernel,
-        out_shape=jax.ShapeDtypeStruct((1, rows, count * chunk), parts[0].dtype),
-        in_specs=[SMEM] + [VMEM] * 4,
-        out_specs=VMEM,
+    count = len(blocks)
+    return pl.pallas_call(
+        functools.partial(finish_kernel, offset, count),
+        out_shape=[
+            jax.ShapeDtypeStruct((1, rows, tp_count * chunk), parts[0].dtype),
+            jax.ShapeDtypeStruct(base.shape, base.dtype),
+        ],
+        in_specs=[SMEM] * 2 + [VMEM] * (4 + count) + [ANY],
+        out_specs=[VMEM, ANY],
+        scratch_shapes=[pltpu.SemaphoreType.DMA((count,))],
+        input_output_aliases={6 + count: 1},
         compiler_params=pltpu.CompilerParams(vmem_limit_bytes=16 * MIB),
-        name="join",
-    )(meta, *parts)
+        name="finish",
+    )(meta, index, *parts, *blocks, base)
 
 
 def hop(value, inst_count, tp_count, target):
@@ -364,8 +379,8 @@
     pass_on(mixed, 1)
     parts = [mixed] + [swap(mixed, tp_count, bits) for bits in NEAR]
     (adopted,) = place(index, 0, (arrived + passed)[:PLACED], adopt, None, mixed)
-    mixed = join(meta, parts, tp_count)
-    (adopted,) = place(index, PLACED, (arrived + passed)[PLACED:], adopt, adopted)
+    late = (arrived + passed)[PLACED:]
+    mixed, adopted = finish(meta, index, parts, tp_count, PLACED, late, adopted)
     return (mixed, adopted[None, None])
 
 

time: 121 us -> 125 us (1.033)
  starting transfers between devices: 63.4 us -> 74.4 us
  waiting for transfers between devices: 39.8 us -> 31.9 us
    ppermute x19, starting transfers between devices: 31.5 us -> 45.4 us  [swap(): return lax.ppermute(value, 'tp', [(t, t ^ bits) for t in range(tp_count)])]
    ppermute x9, waiting for transfers between devices: 11.6 us -> 7.06 us  [hop(): return lax.ppermute(value, ('inst', 'tp'), pairs)]
    ppermute x19, waiting for transfers between devices: 28.2 us -> 24.8 us  [swap(): return lax.ppermute(value, 'tp', [(t, t ^ bits) for t in range(tp_count)])]
    ppermute x9, starting transfers between devices: 31.9 us -> 29 us  [hop(): return lax.ppermute(value, ('inst', 'tp'), pairs)]
    pallas_call x2 -> x1, Pallas kernels: 4.41 us -> 2.97 us  [place(): pl.pallas_call(functools.partial(place_kernel, offset, count, len(out)),...]
    pallas_call x1, Pallas kernels: 0.78 us -> 2.21 us  [finish(): pl.pallas_call(functools.partial(finish_kernel, offset, count), out_shape...]
  transfers between devices with their start and end apart: 28 -> 28, of which waited for: 10 -> 10; matrix products, arithmetic and copies ran while one was open for 2% -> 2% of each run, Pallas kernels for 8% -> 7%
where the time goes in v5:
time: 125 us; the launch traced here: 122 us
  starting transfers between devices  74.4 us (60%)
  waiting for transfers between devices  31.9 us (26%)
  Pallas kernels  12.6 us (10%)
  local copies, waits for them, and re-layouts  1.51 us (1%)
    ppermute x19, starting transfers between devices, swap(): return lax.ppermute(value, 'tp', [(t, t ^ bits) for t in range(tp_count)])  45.4 us
    ppermute x9, starting transfers between devices, hop(): return lax.ppermute(value, ('inst', 'tp'), pairs)  29 us
    ppermute x19, waiting for transfers between devices, swap(): return lax.ppermute(value, 'tp', [(t, t ^ bits) for t in range(tp_count)])  24.8 us
    ppermute x9, waiting for transfers between devices, hop(): return lax.ppermute(value, ('inst', 'tp'), pairs)  7.06 us
    pallas_call x2, Pallas kernels, extract(): pl.pallas_call(functools.partial(extract_kernel, steps), out_shape=[jax.S...  4.01 us
    pallas_call x1, Pallas kernels, place(): pl.pallas_call(functools.partial(place_kernel, offset, count, len(out)),...  2.97 us
  transfers between devices with their start and end apart: 28, of which 10 were waited for; matrix products, arithmetic and copies ran while one was open for 2% of the time, Pallas kernels for 7%

profile of v5, /device:TPU:8, one launch (start us, length us, event | category | flops | bytes accessed | tf_op | source)
XLA Modules:
  0.0 122.4 jit_solution(2394737032159698324)
XLA Ops:
  0.7 2.0 %collective-permute-start.1 = (bf16[24,256]{1,0:T(8,128)(2,1)}, bf16[24,256]{1,0:T(8,128)(2,1)S(1)}, u32[]{:S(2)}, u32[]{:S(2)}) collective-permute-start(bf16[24,256]{1,0:T(8,128)(2,1)} %bitcast.30), channel_id=1, source_target_pairs={{0,1},{1,0},{2,3},{3,2},{4,5},{5,4},{6,7},{7,6},{8,9},{9,8},{10,11... | collective-permute-start | bytes 36872 | tf_op jit(solution)/shard_map/ppermute | solution.py:322
  2.7 2.3 %collective-permute-start = (s32[24]{0:T(128)}, s32[24]{0:T(128)S(1)}, u32[]{:S(2)}, u32[]{:S(2)}) collective-permute-start(s32[24]{0:T(128)} %bitcast.32), channel_id=1, source_target_pairs={{0,128},{1,129},{2,130},{3,131},{4,132},{5,133},{6,134},{7,135},{8... | collective-permute-start | bytes 296 | tf_op jit(solution)/shard_map/ppermute | solution.py:314
  5.0 1.8 %extract.2 = (bf16[2,512,128]{2,1,0:T(8,128)(2,1)}, bf16[2,512,128]{2,1,0:T(8,128)(2,1)}) custom-call(s32[1]{0:T(128)} %bitcast.meta_ref, bf16[2,512,1024]{2,1,0:T(8,128)(2,1)} %bitcast.26), custom_call_target="tpu_custom_call" | custom-call | tf_op jit(solution)/shard_map/extract/pallas_call | solution.py:86
  6.8 1.3 %collective-permute-start.2 = (bf16[2,512,128]{2,1,0:T(8,128)(2,1)}, bf16[2,512,128]{2,1,0:T(8,128)(2,1)S(1)}, u32[]{:S(2)}, u32[]{:S(2)}) collective-permute-start(bf16[2,512,128]{2,1,0:T(8,128)(2,1)} %get-tuple-element.30), channel_id=1, source_target_pairs={{0,128},{1,129},{2,130},{3,131},{4,132},{5,133},{6,134},{7,135},{8... | collective-permute-start | bytes 786440 | tf_op jit(solution)/shard_map/ppermute | solution.py:314
  8.1 5.0 %collective-permute-start.10 = (bf16[2,512,128]{2,1,0:T(8,128)(2,1)}, bf16[2,512,128]{2,1,0:T(8,128)(2,1)S(1)}, u32[]{:S(2)}, u32[]{:S(2)}) collective-permute-start(bf16[2,512,128]{2,1,0:T(8,128)(2,1)} %get-tuple-element.37), channel_id=1, source_target_pairs={{0,130},{1,135},{2,132},{3,129},{4,134},{5,131},{6,128},{7,133},{8... | collective-permute-start | bytes 786440 | tf_op jit(solution)/shard_map/ppermute | solution.py:314
  13.1 2.2 %extract.3 = (bf16[2,512,128]{2,1,0:T(8,128)(2,1)}, bf16[2,512,128]{2,1,0:T(8,128)(2,1)}, bf16[2,512,128]{2,1,0:T(8,128)(2,1)}, bf16[2,512,128]{2,1,0:T(8,128)(2...) custom-call(s32[1]{0:T(128)} %bitcast.meta_ref, bf16[2,512,1024]{2,1,0:T(8,128)(2,1)} %bitcast.27), custom_call_target="tpu_custom_call" | custom-call | tf_op jit(solution)/shard_map/extract/pallas_call | solution.py:86
  15.4 5.4 %collective-permute-start.8 = (bf16[2,512,128]{2,1,0:T(8,128)(2,1)}, bf16[2,512,128]{2,1,0:T(8,128)(2,1)S(1)}, u32[]{:S(2)}, u32[]{:S(2)}) collective-permute-start(bf16[2,512,128]{2,1,0:T(8,128)(2,1)} %get-tuple-element.36), channel_id=1, source_target_pairs={{0,141},{1,140},{2,143},{3,142},{4,137},{5,136},{6,139},{7,138},{8... | collective-permute-start | bytes 786440 | tf_op jit(solution)/shard_map/ppermute | solution.py:314
  20.8 0.1 slice_bitcast_fusion.len_ref
  20.9 2.3 %collective-permute-start.6 = (bf16[2,512,128]{2,1,0:T(8,128)(2,1)}, bf16[2,512,128]{2,1,0:T(8,128)(2,1)S(1)}, u32[]{:S(2)}, u32[]{:S(2)}) collective-permute-start(bf16[2,512,128]{2,1,0:T(8,128)(2,1)} %get-tuple-element.34), channel_id=1, source_target_pairs={{0,136},{1,137},{2,138},{3,139},{4,140},{5,141},{6,142},{7,143},{8... | collective-permute-start | bytes 786440 | tf_op jit(solution)/shard_map/ppermute | solution.py:314
  23.1 3.5 %collective-permute-start.4 = (bf16[2,512,128]{2,1,0:T(8,128)(2,1)}, bf16[2,512,128]{2,1,0:T(8,128)(2,1)S(1)}, u32[]{:S(2)}, u32[]{:S(2)}) collective-permute-start(bf16[2,512,128]{2,1,0:T(8,128)(2,1)} %get-tuple-element.32), channel_id=1, source_target_pairs={{0,133},{1,132},{2,135},{3,134},{4,129},{5,128},{6,131},{7,130},{8... | collective-permute-start | bytes 786440 | tf_op jit(solution)/shard_map/ppermute | solution.py:314
  26.6 3.1 %collective-permute-start.3 = (bf16[2,512,128]{2,1,0:T(8,128)(2,1)S(1)}, bf16[2,512,128]{2,1,0:T(8,128)(2,1)}, u32[]{:S(2)}, u32[]{:S(2)}) collective-permute-start(bf16[2,512,128]{2,1,0:T(8,128)(2,1)S(1)} %collective-permute-done.2.rest_0_), channel_id=1, source_target_pairs={{0,1},{1,0},{2,3},{3,2},{4,5},{5,4},{6,7},{7,6},{8,9},{9,8},{10,11... | collective-permute-start | bytes 786440 | tf_op jit(solution)/shard_map/ppermute | solution.py:322
  29.8 0.1 collective-permute-start.11
  29.8 7.0 %collective-permute-done.8.rest_3_ = bf16[2,512,128]{2,1,0:T(8,128)(2,1)S(1)} collective-permute-done((bf16[2,512,128]{2,1,0:T(8,128)(2,1)}, bf16[2,512,128]{2,1,0:T(8,128)(2,1)S(1)}, u32[]{:S(2)}, u32[]{:S(2)}) %collective-permute-start.8) | collective-permute-done | bytes 262176 | tf_op jit(solution)/shard_map/ppermute | solution.py:314
  36.9 8.3 %collective-permute-start.9 = (bf16[2,512,128]{2,1,0:T(8,128)(2,1)S(1)}, bf16[2,512,128]{2,1,0:T(8,128)(2,1)}, u32[]{:S(2)}, u32[]{:S(2)}) collective-permute-start(bf16[2,512,128]{2,1,0:T(8,128)(2,1)S(1)} %collective-permute-done.8.rest_3_), channel_id=1, source_target_pairs={{0,1},{1,0},{2,3},{3,2},{4,5},{5,4},{6,7},{7,6},{8,9},{9,8},{10,11... | collective-permute-start | bytes 786440 | tf_op jit(solution)/shard_map/ppermute | solution.py:322
  45.2 0.7 constant_dynamic-slice_fusion.1
  45.9 3.0 %collective-permute-start.14 = (bf16[2,512,128]{2,1,0:T(8,128)(2,1)}, bf16[2,512,128]{2,1,0:T(8,128)(2,1)S(1)}, u32[]{:S(2)}, u32[]{:S(2)}) collective-permute-start(bf16[2,512,128]{2,1,0:T(8,128)(2,1)} %get-tuple-element.44), channel_id=1, source_target_pairs={{0,135},{1,130},{2,129},{3,132},{4,131},{5,134},{6,133},{7,128},{8... | collective-permute-start | bytes 786440 | tf_op jit(solution)/shard_map/ppermute | solution.py:314
  48.9 2.6 %collective-permute-start.13 = (bf16[2,512,128]{2,1,0:T(8,128)(2,1)}, bf16[2,512,128]{2,1,0:T(8,128)(2,1)S(1)}, u32[]{:S(2)}, u32[]{:S(2)}) collective-permute-start(bf16[2,512,128]{2,1,0:T(8,128)(2,1)} %get-tuple-element.42), channel_id=1, source_target_pairs={{0,138},{1,143},{2,140},{3,137},{4,142},{5,139},{6,136},{7,141},{8... | collective-permute-start | bytes 786440 | tf_op jit(solution)/shard_map/ppermute | solution.py:314
  51.5 3.6 %collective-permute-start.12 = (bf16[2,512,128]{2,1,0:T(8,128)(2,1)}, bf16[2,512,128]{2,1,0:T(8,128)(2,1)S(1)}, u32[]{:S(2)}, u32[]{:S(2)}) collective-permute-start(bf16[2,512,128]{2,1,0:T(8,128)(2,1)} %get-tuple-element.40), channel_id=1, source_target_pairs={{0,143},{1,138},{2,137},{3,140},{4,139},{5,142},{6,141},{7,136},{8... | collective-permute-start | bytes 786440 | tf_op jit(solution)/shard_map/ppermute | solution.py:314
  55.2 3.4 %collective-permute-start.7 = (bf16[2,512,128]{2,1,0:T(8,128)(2,1)S(1)}, bf16[2,512,128]{2,1,0:T(8,128)(2,1)S(1)}, u32[]{:S(2)}, u32[]{:S(2)}) collective-permute-start(bf16[2,512,128]{2,1,0:T(8,128)(2,1)S(1)} %collective-permute-done.6.rest_2_), channel_id=1, source_target_pairs={{0,1},{1,0},{2,3},{3,2},{4,5},{5,4},{6,7},{7,6},{8,9},{9,8},{10,11... | collective-permute-start | bytes 786440 | tf_op jit(solution)/shard_map/ppermute | solution.py:322
  58.6 0.1 collective-permute-start.5
  58.7 0.2 select_reduce_fusion.len_ref
  58.9 0.8 fusion.rows_ref
  59.8 1.2 attend.2.res_ref
  61.0 5.8 %collective-permute-done.7.rest_10_ = bf16[2,512,128]{2,1,0:T(8,128)(2,1)S(1)} collective-permute-done((bf16[2,512,128]{2,1,0:T(8,128)(2,1)S(1)}, bf16[2,512,128]{2,1,0:T(8,128)(2,1)S(1)}, u32[]{:S(2)}, u32[]{:S(2)}) %collective-permute-start.7) | collective-permute-done | bytes 262176 | tf_op jit(solution)/shard_map/ppermute | solution.py:322
  66.8 3.9 %collective-permute-done.5.rest_9_ = bf16[2,512,128]{2,1,0:T(8,128)(2,1)S(1)} collective-permute-done((bf16[2,512,128]{2,1,0:T(8,128)(2,1)S(1)}, bf16[2,512,128]{2,1,0:T(8,128)(2,1)S(1)}, u32[]{:S(2)}, u32[]{:S(2)}) %collective-permute-start.5) | collective-permute-done | bytes 262176 | tf_op jit(solution)/shard_map/ppermute | solution.py:322
  70.7 1.2 attend.3
  71.9 2.6 %collective-permute-start.15 = (f32[8,256]{1,0:T(8,128)S(1)}, f32[8,256]{1,0:T(8,128)S(1)}, u32[]{:S(2)}, u32[]{:S(2)}) collective-permute-start(f32[8,256]{1,0:T(8,128)S(1)} %get-tuple-element.46), channel_id=1, source_target_pairs={{0,1},{1,0},{2,3},{3,2},{4,5},{5,4},{6,7},{7,6},{8,9},{9,8},{10,11... | collective-permute-start | bytes 24584 | tf_op jit(solution)/shard_map/ppermute | solution.py:322
  74.5 0.7 dynamic-slice_bitcast_fusion.place_ref
  75.2 0.9 collective-permute-done.15.traded_ref
  76.1 0.9 project.1
  77.0 2.1 %collective-permute-start.19 = (bf16[2,512,128]{2,1,0:T(8,128)(2,1)S(1)}, bf16[2,512,128]{2,1,0:T(8,128)(2,1)S(1)}, u32[]{:S(2)}, u32[]{:S(2)}) collective-permute-start(bf16[2,512,128]{2,1,0:T(8,128)(2,1)S(1)} %collective-permute-done.12.rest_5_), channel_id=1, source_target_pairs={{0,1},{1,0},{2,3},{3,2},{4,5},{5,4},{6,7},{7,6},{8,9},{9,8},{10,11... | collective-permute-start | bytes 786440 | tf_op jit(solution)/shard_map/ppermute | solution.py:322
  79.1 0.1 collective-permute-start.16
  79.2 2.8 %collective-permute-start.17 = (bf16[4,24,512]{2,1,0:T(8,128)(2,1)S(1)}, bf16[4,24,512]{2,1,0:T(8,128)(2,1)S(1)}, u32[]{:S(2)}, u32[]{:S(2)}) collective-permute-start(bf16[4,24,512]{2,1,0:T(8,128)(2,1)S(1)} %get-tuple-element.50), channel_id=1, source_target_pairs={{0,8},{1,9},{2,10},{3,11},{4,12},{5,13},{6,14},{7,15},{8,0},{9,1},... | collective-permute-start | bytes 294920 | tf_op jit(solution)/shard_map/ppermute | solution.py:322
  82.0 2.1 %collective-permute-start.18 = (bf16[4,24,512]{2,1,0:T(8,128)(2,1)S(1)}, bf16[4,24,512]{2,1,0:T(8,128)(2,1)S(1)}, u32[]{:S(2)}, u32[]{:S(2)}) collective-permute-start(bf16[4,24,512]{2,1,0:T(8,128)(2,1)S(1)} %get-tuple-element.51), channel_id=1, source_target_pairs={{0,9},{1,8},{2,11},{3,10},{4,13},{5,12},{6,15},{7,14},{8,1},{9,0},... | collective-permute-start | bytes 294920 | tf_op jit(solution)/shard_map/ppermute | solution.py:322
  84.1 1.9 %collective-permute-done.16.refs_1_ = bf16[4,24,512]{2,1,0:T(8,128)(2,1)S(1)} collective-permute-done((bf16[4,24,512]{2,1,0:T(8,128)(2,1)S(1)}, bf16[4,24,512]{2,1,0:T(8,128)(2,1)S(1)}, u32[]{:S(2)}, u32[]{:S(2)}) %collective-permute-start.16) | collective-permute-done | bytes 98336 | tf_op jit(solution)/shard_map/ppermute | solution.py:322
  86.0 3.0 %collective-permute-done.18.refs_3_ = bf16[4,24,512]{2,1,0:T(8,128)(2,1)S(1)} collective-permute-done((bf16[4,24,512]{2,1,0:T(8,128)(2,1)S(1)}, bf16[4,24,512]{2,1,0:T(8,128)(2,1)S(1)}, u32[]{:S(2)}, u32[]{:S(2)}) %collective-permute-start.18) | collective-permute-done | bytes 98336 | tf_op jit(solution)/shard_map/ppermute | solution.py:322
  89.0 11.0 %collective-permute-start.22 = (bf16[4,24,512]{2,1,0:T(8,128)(2,1)S(1)}, bf16[4,24,512]{2,1,0:T(8,128)(2,1)S(1)}, u32[]{:S(2)}, u32[]{:S(2)}) collective-permute-start(bf16[4,24,512]{2,1,0:T(8,128)(2,1)S(1)} %near_sum.1.refs_0_), channel_id=1, source_target_pairs={{0,6},{1,7},{2,4},{3,5},{4,2},{5,3},{6,0},{7,1},{8,14},{9,15},{10,... | collective-permute-start | bytes 294920 | tf_op jit(solution)/shard_map/ppermute | solution.py:322
  100.0 2.5 %collective-permute-start.20 = (bf16[4,24,512]{2,1,0:T(8,128)(2,1)S(1)}, bf16[4,24,512]{2,1,0:T(8,128)(2,1)S(1)}, u32[]{:S(2)}, u32[]{:S(2)}) collective-permute-start(bf16[4,24,512]{2,1,0:T(8,128)(2,1)S(1)} %near_sum.1.refs_0_), channel_id=1, source_target_pairs={{0,2},{1,3},{2,0},{3,1},{4,6},{5,7},{6,4},{7,5},{8,10},{9,11},{10,... | collective-permute-start | bytes 294920 | tf_op jit(solution)/shard_map/ppermute | solution.py:322
  102.5 2.4 %collective-permute-done.22.refs_3_ = bf16[4,24,512]{2,1,0:T(8,128)(2,1)S(1)} collective-permute-done((bf16[4,24,512]{2,1,0:T(8,128)(2,1)S(1)}, bf16[4,24,512]{2,1,0:T(8,128)(2,1)S(1)}, u32[]{:S(2)}, u32[]{:S(2)}) %collective-permute-start.22) | collective-permute-done | bytes 98336 | tf_op jit(solution)/shard_map/ppermute | solution.py:322
  104.9 5.3 %collective-permute-done.21.refs_2_ = bf16[4,24,512]{2,1,0:T(8,128)(2,1)S(1)} collective-permute-done((bf16[4,24,512]{2,1,0:T(8,128)(2,1)S(1)}, bf16[4,24,512]{2,1,0:T(8,128)(2,1)S(1)}, u32[]{:S(2)}, u32[]{:S(2)}) %collective-permute-start.21) | collective-permute-done | bytes 98336 | tf_op jit(solution)/shard_map/ppermute | solution.py:322
  110.3 0.1 collective-permute-start.27
  110.4 0.2 collective-permute-start.25
  110.6 4.8 %collective-permute-start.24 = (bf16[4,24,512]{2,1,0:T(8,128)(2,1)S(1)}, bf16[4,24,512]{2,1,0:T(8,128)(2,1)S(1)}, u32[]{:S(2)}, u32[]{:S(2)}) collective-permute-start(bf16[4,24,512]{2,1,0:T(8,128)(2,1)S(1)} %far_sum.1.rest_13_.rest_0_), channel_id=1, source_target_pairs={{0,8},{1,9},{2,10},{3,11},{4,12},{5,13},{6,14},{7,15},{8,0},{9,1},... | collective-permute-start | bytes 294920 | tf_op jit(solution)/shard_map/ppermute | solution.py:322
  115.4 0.1 collective-permute-start.23
  115.5 3.0 %place.1.rest_7_ = bf16[16,2,512,128]{3,2,1,0:T(8,128)(2,1)} custom-call(s32[16]{0:T(128)S(1)} %get-tuple-element.59.index_ref, bf16[2,512,128]{2,1,0:T(8,128)(2,1)S(1)} %collective-permute-done.2.rest_0_, bf16[2,512,128]{2,1,0:T(8,128)(2,1)S(1)} %collective-permute-done.4.rest_1_, bf16[2,512,128]{2,1,0:T(8,128)(2,1)S(1)} %collective-permute-done.6.rest_2_, ...), custom_call_target="tpu_custom_call" | custom-call | tf_op jit(solution)/shard_map/place/pallas_call | solution.py:122
  118.5 0.1 collective-permute-done.24.rest_2_
  118.6 1.4 %collective-permute-done.23.rest_1_ = bf16[4,24,512]{2,1,0:T(8,128)(2,1)S(1)} collective-permute-done((bf16[4,24,512]{2,1,0:T(8,128)(2,1)S(1)}, bf16[4,24,512]{2,1,0:T(8,128)(2,1)S(1)}, u32[]{:S(2)}, u32[]{:S(2)}) %collective-permute-start.23) | collective-permute-done | bytes 98336 | tf_op jit(solution)/shard_map/ppermute | solution.py:322
  120.0 2.2 %finish.1 = (bf16[1,24,8192]{2,1,0:T(8,128)(2,1)}, bf16[16,2,512,128]{3,2,1,0:T(8,128)(2,1)}) custom-call(s32[1]{0:T(128)} %bitcast.meta_ref, s32[16]{0:T(128)S(1)} %get-tuple-element.59.index_ref, bf16[4,24,512]{2,1,0:T(8,128)(2,1)S(1)} %far_sum.1.rest_13_.rest_0_, ...), custom_call_target="tpu_custom_call", output_to_operand_aliasing={{1}: (9, {})} | custom-call | tf_op jit(solution)/shard_map/finish/pallas_call | solution.py:292
  (37 shorter events, 0.2 us)
Async XLA Ops:
  0.6 58.1 %copy-start = (bf16[1,24,2,1024]{3,2,1,0:T(2,128)(2,1)S(1)}, bf16[1,24,2,1024]{3,2,1,0:T(2,128)(2,1)}, u32[]{:S(2)}) copy-start(bf16[1,24,2,1024]{3,2,1,0:T(2,128)(2,1)} %param.12) | copy-start | bytes 294916
  0.6 58.3 %copy-start.4 = (bf16[1,24,256]{2,1,0:T(8,128)(2,1)S(1)}, bf16[1,24,256]{2,1,0:T(8,128)(2,1)}, u32[]{:S(2)}) copy-start(bf16[1,24,256]{2,1,0:T(8,128)(2,1)} %param.13) | copy-start | bytes 36868
  0.7 20.1 %copy-start.5 = (s32[1,24]{1,0:T(1,128)S(1)}, s32[1,24]{1,0:T(1,128)}, u32[]{:S(2)}) copy-start(s32[1,24]{1,0:T(1,128)} %param.15) | copy-start | bytes 292
  0.7 59.1 %copy-start.2 = (bf16[1,1,8,2,512,128]{5,4,3,2,1,0:T(8,128)(2,1)S(1)}, bf16[1,1,8,2,512,128]{5,4,3,2,1,0:T(8,128)(2,1)}, u32[]{:S(2)}) copy-start(bf16[1,1,8,2,512,128]{5,4,3,2,1,0:T(8,128)(2,1)} %param.11) | copy-start | bytes 6291460
  0.7 14.7 %collective-permute-start.1 = (bf16[24,256]{1,0:T(8,128)(2,1)}, bf16[24,256]{1,0:T(8,128)(2,1)S(1)}, u32[]{:S(2)}, u32[]{:S(2)}) collective-permute-start(bf16[24,256]{1,0:T(8,128)(2,1)} %bitcast.30), channel_id=1, source_target_pairs={{0,1},{1,0},{2,3},{3,2},{4,5},{5,4},{6,7},{7,6},{8,9},{9,8},{10,11... | collective-permute-start | bytes 36872 | tf_op jit(solution)/shard_map/ppermute | solution.py:322
  2.7 12.7 %collective-permute-start = (s32[24]{0:T(128)}, s32[24]{0:T(128)S(1)}, u32[]{:S(2)}, u32[]{:S(2)}) collective-permute-start(s32[24]{0:T(128)} %bitcast.32), channel_id=1, source_target_pairs={{0,128},{1,129},{2,130},{3,131},{4,132},{5,133},{6,134},{7,135},{8... | collective-permute-start | bytes 296 | tf_op jit(solution)/shard_map/ppermute | solution.py:314
  6.8 19.9 %collective-permute-start.2 = (bf16[2,512,128]{2,1,0:T(8,128)(2,1)}, bf16[2,512,128]{2,1,0:T(8,128)(2,1)S(1)}, u32[]{:S(2)}, u32[]{:S(2)}) collective-permute-start(bf16[2,512,128]{2,1,0:T(8,128)(2,1)} %get-tuple-element.30), channel_id=1, source_target_pairs={{0,128},{1,129},{2,130},{3,131},{4,132},{5,133},{6,134},{7,135},{8... | collective-permute-start | bytes 786440 | tf_op jit(solution)/shard_map/ppermute | solution.py:314
  8.1 21.7 %collective-permute-start.10 = (bf16[2,512,128]{2,1,0:T(8,128)(2,1)}, bf16[2,512,128]{2,1,0:T(8,128)(2,1)S(1)}, u32[]{:S(2)}, u32[]{:S(2)}) collective-permute-start(bf16[2,512,128]{2,1,0:T(8,128)(2,1)} %get-tuple-element.37), channel_id=1, source_target_pairs={{0,130},{1,135},{2,132},{3,129},{4,134},{5,131},{6,128},{7,133},{8... | collective-permute-start | bytes 786440 | tf_op jit(solution)/shard_map/ppermute | solution.py:314
  15.4 21.5 %collective-permute-start.8 = (bf16[2,512,128]{2,1,0:T(8,128)(2,1)}, bf16[2,512,128]{2,1,0:T(8,128)(2,1)S(1)}, u32[]{:S(2)}, u32[]{:S(2)}) collective-permute-start(bf16[2,512,128]{2,1,0:T(8,128)(2,1)} %get-tuple-element.36), channel_id=1, source_target_pairs={{0,141},{1,140},{2,143},{3,142},{4,137},{5,136},{6,139},{7,138},{8... | collective-permute-start | bytes 786440 | tf_op jit(solution)/shard_map/ppermute | solution.py:314
  20.9 25.1 %collective-permute-start.6 = (bf16[2,512,128]{2,1,0:T(8,128)(2,1)}, bf16[2,512,128]{2,1,0:T(8,128)(2,1)S(1)}, u32[]{:S(2)}, u32[]{:S(2)}) collective-permute-start(bf16[2,512,128]{2,1,0:T(8,128)(2,1)} %get-tuple-element.34), channel_id=1, source_target_pairs={{0,136},{1,137},{2,138},{3,139},{4,140},{5,141},{6,142},{7,143},{8... | collective-permute-start | bytes 786440 | tf_op jit(solution)/shard_map/ppermute | solution.py:314
  23.1 25.8 %collective-permute-start.4 = (bf16[2,512,128]{2,1,0:T(8,128)(2,1)}, bf16[2,512,128]{2,1,0:T(8,128)(2,1)S(1)}, u32[]{:S(2)}, u32[]{:S(2)}) collective-permute-start(bf16[2,512,128]{2,1,0:T(8,128)(2,1)} %get-tuple-element.32), channel_id=1, source_target_pairs={{0,133},{1,132},{2,135},{3,134},{4,129},{5,128},{6,131},{7,130},{8... | collective-permute-start | bytes 786440 | tf_op jit(solution)/shard_map/ppermute | solution.py:314
  26.6 24.9 %collective-permute-start.3 = (bf16[2,512,128]{2,1,0:T(8,128)(2,1)S(1)}, bf16[2,512,128]{2,1,0:T(8,128)(2,1)}, u32[]{:S(2)}, u32[]{:S(2)}) collective-permute-start(bf16[2,512,128]{2,1,0:T(8,128)(2,1)S(1)} %collective-permute-done.2.rest_0_), channel_id=1, source_target_pairs={{0,1},{1,0},{2,3},{3,2},{4,5},{5,4},{6,7},{7,6},{8,9},{9,8},{10,11... | collective-permute-start | bytes 786440 | tf_op jit(solution)/shard_map/ppermute | solution.py:322
  29.8 25.4 %collective-permute-start.11 = (bf16[2,512,128]{2,1,0:T(8,128)(2,1)S(1)}, bf16[2,512,128]{2,1,0:T(8,128)(2,1)}, u32[]{:S(2)}, u32[]{:S(2)}) collective-permute-start(bf16[2,512,128]{2,1,0:T(8,128)(2,1)S(1)} %collective-permute-done.10.rest_4_), channel_id=1, source_target_pairs={{0,1},{1,0},{2,3},{3,2},{4,5},{5,4},{6,7},{7,6},{8,9},{9,8},{10,11... | collective-permute-start | bytes 786440 | tf_op jit(solution)/shard_map/ppermute | solution.py:322
  36.9 21.7 %collective-permute-start.9 = (bf16[2,512,128]{2,1,0:T(8,128)(2,1)S(1)}, bf16[2,512,128]{2,1,0:T(8,128)(2,1)}, u32[]{:S(2)}, u32[]{:S(2)}) collective-permute-start(bf16[2,512,128]{2,1,0:T(8,128)(2,1)S(1)} %collective-permute-done.8.rest_3_), channel_id=1, source_target_pairs={{0,1},{1,0},{2,3},{3,2},{4,5},{5,4},{6,7},{7,6},{8,9},{9,8},{10,11... | collective-permute-start | bytes 786440 | tf_op jit(solution)/shard_map/ppermute | solution.py:322
  45.9 30.2 %copy-start.1 = (bf16[256,8192]{1,0:T(8,128)(2,1)S(1)}, bf16[256,8192]{1,0:T(8,128)(2,1)}, u32[]{:S(2)}) copy-start(bf16[256,8192]{1,0:T(8,128)(2,1)} %weight_ref.1) | copy-start | bytes 12582916
  45.9 24.8 %collective-permute-start.14 = (bf16[2,512,128]{2,1,0:T(8,128)(2,1)}, bf16[2,512,128]{2,1,0:T(8,128)(2,1)S(1)}, u32[]{:S(2)}, u32[]{:S(2)}) collective-permute-start(bf16[2,512,128]{2,1,0:T(8,128)(2,1)} %get-tuple-element.44), channel_id=1, source_target_pairs={{0,135},{1,130},{2,129},{3,132},{4,131},{5,134},{6,133},{7,128},{8... | collective-permute-start | bytes 786440 | tf_op jit(solution)/shard_map/ppermute | solution.py:314
  48.9 21.8 %collective-permute-start.13 = (bf16[2,512,128]{2,1,0:T(8,128)(2,1)}, bf16[2,512,128]{2,1,0:T(8,128)(2,1)S(1)}, u32[]{:S(2)}, u32[]{:S(2)}) collective-permute-start(bf16[2,512,128]{2,1,0:T(8,128)(2,1)} %get-tuple-element.42), channel_id=1, source_target_pairs={{0,138},{1,143},{2,140},{3,137},{4,142},{5,139},{6,136},{7,141},{8... | collective-permute-start | bytes 786440 | tf_op jit(solution)/shard_map/ppermute | solution.py:314
  51.5 19.2 %collective-permute-start.12 = (bf16[2,512,128]{2,1,0:T(8,128)(2,1)}, bf16[2,512,128]{2,1,0:T(8,128)(2,1)S(1)}, u32[]{:S(2)}, u32[]{:S(2)}) collective-permute-start(bf16[2,512,128]{2,1,0:T(8,128)(2,1)} %get-tuple-element.40), channel_id=1, source_target_pairs={{0,143},{1,138},{2,137},{3,140},{4,139},{5,142},{6,141},{7,136},{8... | collective-permute-start | bytes 786440 | tf_op jit(solution)/shard_map/ppermute | solution.py:314
  55.2 11.6 %collective-permute-start.7 = (bf16[2,512,128]{2,1,0:T(8,128)(2,1)S(1)}, bf16[2,512,128]{2,1,0:T(8,128)(2,1)S(1)}, u32[]{:S(2)}, u32[]{:S(2)}) collective-permute-start(bf16[2,512,128]{2,1,0:T(8,128)(2,1)S(1)} %collective-permute-done.6.rest_2_), channel_id=1, source_target_pairs={{0,1},{1,0},{2,3},{3,2},{4,5},{5,4},{6,7},{7,6},{8,9},{9,8},{10,11... | collective-permute-start | bytes 786440 | tf_op jit(solution)/shard_map/ppermute | solution.py:322
  58.6 12.1 %collective-permute-start.5 = (bf16[2,512,128]{2,1,0:T(8,128)(2,1)S(1)}, bf16[2,512,128]{2,1,0:T(8,128)(2,1)S(1)}, u32[]{:S(2)}, u32[]{:S(2)}) collective-permute-start(bf16[2,512,128]{2,1,0:T(8,128)(2,1)S(1)} %collective-permute-done.4.rest_1_), channel_id=1, source_target_pairs={{0,1},{1,0},{2,3},{3,2},{4,5},{5,4},{6,7},{7,6},{8,9},{9,8},{10,11... | collective-permute-start | bytes 786440 | tf_op jit(solution)/shard_map/ppermute | solution.py:322
  59.7 50.5 %copy-start.3 = (bf16[1,24,8192]{2,1,0:T(8,128)(2,1)S(1)}, bf16[1,24,8192]{2,1,0:T(8,128)(2,1)}, u32[]{:S(2)}) copy-start(bf16[1,24,8192]{2,1,0:T(8,128)(2,1)} %param.14) | copy-start | bytes 1179652
  71.9 4.2 %collective-permute-start.15 = (f32[8,256]{1,0:T(8,128)S(1)}, f32[8,256]{1,0:T(8,128)S(1)}, u32[]{:S(2)}, u32[]{:S(2)}) collective-permute-start(f32[8,256]{1,0:T(8,128)S(1)} %get-tuple-element.46), channel_id=1, source_target_pairs={{0,1},{1,0},{2,3},{3,2},{4,5},{5,4},{6,7},{7,6},{8,9},{9,8},{10,11... | collective-permute-start | bytes 24584 | tf_op jit(solution)/shard_map/ppermute | solution.py:322
  77.0 25.5 %collective-permute-start.19 = (bf16[2,512,128]{2,1,0:T(8,128)(2,1)S(1)}, bf16[2,512,128]{2,1,0:T(8,128)(2,1)S(1)}, u32[]{:S(2)}, u32[]{:S(2)}) collective-permute-start(bf16[2,512,128]{2,1,0:T(8,128)(2,1)S(1)} %collective-permute-done.12.rest_5_), channel_id=1, source_target_pairs={{0,1},{1,0},{2,3},{3,2},{4,5},{5,4},{6,7},{7,6},{8,9},{9,8},{10,11... | collective-permute-start | bytes 786440 | tf_op jit(solution)/shard_map/ppermute | solution.py:322
  79.1 6.9 %collective-permute-start.16 = (bf16[4,24,512]{2,1,0:T(8,128)(2,1)S(1)}, bf16[4,24,512]{2,1,0:T(8,128)(2,1)S(1)}, u32[]{:S(2)}, u32[]{:S(2)}) collective-permute-start(bf16[4,24,512]{2,1,0:T(8,128)(2,1)S(1)} %get-tuple-element.49), channel_id=1, source_target_pairs={{0,1},{1,0},{2,3},{3,2},{4,5},{5,4},{6,7},{7,6},{8,9},{9,8},{10,11... | collective-permute-start | bytes 294920 | tf_op jit(solution)/shard_map/ppermute | solution.py:322
  79.2 6.8 %collective-permute-start.17 = (bf16[4,24,512]{2,1,0:T(8,128)(2,1)S(1)}, bf16[4,24,512]{2,1,0:T(8,128)(2,1)S(1)}, u32[]{:S(2)}, u32[]{:S(2)}) collective-permute-start(bf16[4,24,512]{2,1,0:T(8,128)(2,1)S(1)} %get-tuple-element.50), channel_id=1, source_target_pairs={{0,8},{1,9},{2,10},{3,11},{4,12},{5,13},{6,14},{7,15},{8,0},{9,1},... | collective-permute-start | bytes 294920 | tf_op jit(solution)/shard_map/ppermute | solution.py:322
  82.0 7.0 %collective-permute-start.18 = (bf16[4,24,512]{2,1,0:T(8,128)(2,1)S(1)}, bf16[4,24,512]{2,1,0:T(8,128)(2,1)S(1)}, u32[]{:S(2)}, u32[]{:S(2)}) collective-permute-start(bf16[4,24,512]{2,1,0:T(8,128)(2,1)S(1)} %get-tuple-element.51), channel_id=1, source_target_pairs={{0,9},{1,8},{2,11},{3,10},{4,13},{5,12},{6,15},{7,14},{8,1},{9,0},... | collective-permute-start | bytes 294920 | tf_op jit(solution)/shard_map/ppermute | solution.py:322
  89.0 15.9 %collective-permute-start.22 = (bf16[4,24,512]{2,1,0:T(8,128)(2,1)S(1)}, bf16[4,24,512]{2,1,0:T(8,128)(2,1)S(1)}, u32[]{:S(2)}, u32[]{:S(2)}) collective-permute-start(bf16[4,24,512]{2,1,0:T(8,128)(2,1)S(1)} %near_sum.1.refs_0_), channel_id=1, source_target_pairs={{0,6},{1,7},{2,4},{3,5},{4,2},{5,3},{6,0},{7,1},{8,14},{9,15},{10,... | collective-permute-start | bytes 294920 | tf_op jit(solution)/shard_map/ppermute | solution.py:322
  100.0 10.2 %collective-permute-start.21 = (bf16[4,24,512]{2,1,0:T(8,128)(2,1)S(1)}, bf16[4,24,512]{2,1,0:T(8,128)(2,1)S(1)}, u32[]{:S(2)}, u32[]{:S(2)}) collective-permute-start(bf16[4,24,512]{2,1,0:T(8,128)(2,1)S(1)} %near_sum.1.refs_0_), channel_id=1, source_target_pairs={{0,4},{1,5},{2,6},{3,7},{4,0},{5,1},{6,2},{7,3},{8,12},{9,13},{10,... | collective-permute-start | bytes 294920 | tf_op jit(solution)/shard_map/ppermute | solution.py:322
  100.0 10.2 %collective-permute-start.20 = (bf16[4,24,512]{2,1,0:T(8,128)(2,1)S(1)}, bf16[4,24,512]{2,1,0:T(8,128)(2,1)S(1)}, u32[]{:S(2)}, u32[]{:S(2)}) collective-permute-start(bf16[4,24,512]{2,1,0:T(8,128)(2,1)S(1)} %near_sum.1.refs_0_), channel_id=1, source_target_pairs={{0,2},{1,3},{2,0},{3,1},{4,6},{5,7},{6,4},{7,5},{8,10},{9,11},{10,... | collective-permute-start | bytes 294920 | tf_op jit(solution)/shard_map/ppermute | solution.py:322
  102.5 16.0 %collective-permute-start.26 = (bf16[2,512,128]{2,1,0:T(8,128)(2,1)S(1)}, bf16[2,512,128]{2,1,0:T(8,128)(2,1)S(1)}, u32[]{:S(2)}, u32[]{:S(2)}) collective-permute-start(bf16[2,512,128]{2,1,0:T(8,128)(2,1)S(1)} %collective-permute-done.13.rest_6_), channel_id=1, source_target_pairs={{0,1},{1,0},{2,3},{3,2},{4,5},{5,4},{6,7},{7,6},{8,9},{9,8},{10,11... | collective-permute-start | bytes 786440 | tf_op jit(solution)/shard_map/ppermute | solution.py:322
  110.3 9.7 %collective-permute-start.27 = (bf16[2,512,128]{2,1,0:T(8,128)(2,1)S(1)}, bf16[2,512,128]{2,1,0:T(8,128)(2,1)S(1)}, u32[]{:S(2)}, u32[]{:S(2)}) collective-permute-start(bf16[2,512,128]{2,1,0:T(8,128)(2,1)S(1)} %collective-permute-done.14.rest_7_), channel_id=1, source_target_pairs={{0,1},{1,0},{2,3},{3,2},{4,5},{5,4},{6,7},{7,6},{8,9},{9,8},{10,11... | collective-permute-start | bytes 786440 | tf_op jit(solution)/shard_map/ppermute | solution.py:322
  110.4 8.1 %collective-permute-start.25 = (bf16[4,24,512]{2,1,0:T(8,128)(2,1)S(1)}, bf16[4,24,512]{2,1,0:T(8,128)(2,1)S(1)}, u32[]{:S(2)}, u32[]{:S(2)}) collective-permute-start(bf16[4,24,512]{2,1,0:T(8,128)(2,1)S(1)} %far_sum.1.rest_13_.rest_0_), channel_id=1, source_target_pairs={{0,9},{1,8},{2,11},{3,10},{4,13},{5,12},{6,15},{7,14},{8,1},{9,0},... | collective-permute-start | bytes 294920 | tf_op jit(solution)/shard_map/ppermute | solution.py:322
  110.6 8.0 %collective-permute-start.24 = (bf16[4,24,512]{2,1,0:T(8,128)(2,1)S(1)}, bf16[4,24,512]{2,1,0:T(8,128)(2,1)S(1)}, u32[]{:S(2)}, u32[]{:S(2)}) collective-permute-start(bf16[4,24,512]{2,1,0:T(8,128)(2,1)S(1)} %far_sum.1.rest_13_.rest_0_), channel_id=1, source_target_pairs={{0,8},{1,9},{2,10},{3,11},{4,12},{5,13},{6,14},{7,15},{8,0},{9,1},... | collective-permute-start | bytes 294920 | tf_op jit(solution)/shard_map/ppermute | solution.py:322
  115.4 4.6 %collective-permute-start.23 = (bf16[4,24,512]{2,1,0:T(8,128)(2,1)S(1)}, bf16[4,24,512]{2,1,0:T(8,128)(2,1)S(1)}, u32[]{:S(2)}, u32[]{:S(2)}) collective-permute-start(bf16[4,24,512]{2,1,0:T(8,128)(2,1)S(1)} %far_sum.1.rest_13_.rest_0_), channel_id=1, source_target_pairs={{0,1},{1,0},{2,3},{3,2},{4,5},{5,4},{6,7},{7,6},{8,9},{9,8},{10,11... | collective-permute-start | bytes 294920 | tf_op jit(solution)/shard_map/ppermute | solution.py:322
